TPU v7x, 32 devices: a whole 2x2x4 slice. The times are simulated.
32 devices in a mesh: dp: 4 (over y, x), fsdp: 8 (over z, core).
Axes of the slice: x: 2, y: 2, z: 4, core: 2. Of those that a mesh axis runs over, the one named last changes fastest.
Arguments:
- inputs: bfloat16 [16384, 512], P(('dp', 'fsdp')), may hold values from -6 to 6
- lengths: int32 [32, 3], P(('dp', 'fsdp')), may hold values from 0 to 512, as said below
- filters: bfloat16 [24, 512], replicated
- cotangent: bfloat16 [16384, 512], P(('dp', 'fsdp')), may hold values from -12 to 12
- mixer_weight: float32 [13824, 512], P(('dp', 'fsdp')), may hold values from -0.0546875 to 0.0546875
- gate_up_weight: float32 [4096, 512], P(('dp', 'fsdp')), may hold values from -0.25 to 0.25
- down_weight: float32 [2048, 512], P(('dp', 'fsdp')), may hold values from -0.125 to 0.125
- norm_gains: float32 [2, 512], P(None, ('dp', 'fsdp'))
- mixer_first: float32 [13824, 512], P(('dp', 'fsdp')), may hold values from -0.00021362305 to 0.00021362305
- gate_up_first: float32 [4096, 512], P(('dp', 'fsdp')), may hold values from -7.6293945e-05 to 7.6293945e-05
- down_first: float32 [2048, 512], P(('dp', 'fsdp')), may hold values from -0.00015258789 to 0.00015258789
- gains_first: float32 [2, 512], P(None, ('dp', 'fsdp')), may hold values from -0.00021362305 to 0.00021362305
- mixer_second: float32 [13824, 512], P(('dp', 'fsdp')), may hold values from 5.1835567e-09 to 2.053862e-08
- gate_up_second: float32 [4096, 512], P(('dp', 'fsdp')), may hold values from 8.313251e-10 to 3.3253005e-09
- down_second: float32 [2048, 512], P(('dp', 'fsdp')), may hold values from 3.3253005e-09 to 1.3301202e-08
- gains_second: float32 [2, 512], P(None, ('dp', 'fsdp')), may hold values from 5.1835567e-09 to 2.053862e-08
- mixer_average: float32 [13824, 512], P(('dp', 'fsdp')), may hold values from -0.0546875 to 0.0546875
Outputs:
- output: bfloat16 [16384, 512], P(('dp', 'fsdp'))
- input_grad: float32 [16384, 512], P(('dp', 'fsdp'))
- grad_norm: float32 [], replicated
- mixer_new: float32 [13824, 512], P(('dp', 'fsdp'))
- gate_up_new: float32 [4096, 512], P(('dp', 'fsdp'))
- down_new: float32 [2048, 512], P(('dp', 'fsdp'))
- gains_new: float32 [2, 512], P(None, ('dp', 'fsdp'))
- mixer_first_new: float32 [13824, 512], P(('dp', 'fsdp'))
- gate_up_first_new: float32 [4096, 512], P(('dp', 'fsdp'))
- down_first_new: float32 [2048, 512], P(('dp', 'fsdp'))
- gains_first_new: float32 [2, 512], P(None, ('dp', 'fsdp'))
- mixer_second_new: float32 [13824, 512], P(('dp', 'fsdp'))
- gate_up_second_new: float32 [4096, 512], P(('dp', 'fsdp'))
- down_second_new: float32 [2048, 512], P(('dp', 'fsdp'))
- gains_second_new: float32 [2, 512], P(None, ('dp', 'fsdp'))
- mixer_average_new: float32 [13824, 512], P(('dp', 'fsdp'))
Inputs may be any that keep to these rules, and one draw needn't show every extreme that they name: Each row is one device's documents: either 512, 0, 0, or two lengths from 128 to 192 and a third from 0 to 128. Some row is of the first kind.
All inputs are finite; a program needn't handle non-finite values.
Results may differ from a plain program's by a relative error of at most 0.01.
Values may be sent and summed in bfloat16 or wider, within the bound.
No kernel may reach another device: no remote copies, remote signals or barrier semaphores. Data moves between devices by JAX's collectives and lax.ppermute only.
A program may use at most 192 MiB of HBM per device.

v0:
```python
import jax
import jax.numpy as jnp
from jax import lax
from jax.sharding import PartitionSpec as P

FILTERS = 24
AR_ORDER = 3
FF = 2048
STEP = 10


NORM_EPS = 1e-05
CLIP_LIMIT = 1.0
BETA_ONE = 0.9
BETA_TWO = 0.95
ADAM_EPS = 1e-08
RATE_MATRIX = 0.03
RATE_GAIN = 0.5
DECAY_MATRIX = 0.1
AVERAGE_KEEP = 0.9
ROWS_CONTRACT = (((0,), (0,)), ((), ()))
LAST_CONTRACT = (((1,), (1,)), ((), ()))


def layout(lengths, slots):
    ends = jnp.cumsum(lengths, axis=-1)
    place = jnp.arange(slots, dtype=jnp.int32)
    return jnp.sum((place[:, None] >= ends[..., None, :]).astype(jnp.int32), axis=-1)


def filter_tiles(padded, offset, block):
    window = padded[:, offset * block : offset * block + 2 * block - 1]
    flipped = window[:, ::-1]
    extended = jnp.concatenate([flipped, jnp.zeros((flipped.shape[0], 1), flipped.dtype)], axis=1)
    tiled = jnp.tile(extended, (1, block))[:, : block * (2 * block - 1)]
    return tiled.reshape(flipped.shape[0], block, 2 * block - 1)[:, :, block - 1 :]


def pair_tiles(padded, segment, row_block, col_block, block):
    tiles = filter_tiles(padded, row_block - col_block, block)
    targets = segment[row_block * block : (row_block + 1) * block]
    sources = segment[col_block * block : (col_block + 1) * block]
    keep = (targets[:, None] == sources[None, :]) & (targets[:, None] < 3)
    return jnp.where(keep[None], tiles, jnp.zeros((), tiles.dtype))


def lag_keep(segment, lag):
    if lag == 0:
        return segment < 3
    earlier = jnp.concatenate([jnp.full((lag,), -1, jnp.int32), segment[:-lag]])
    return (earlier == segment) & (segment < 3)


def spectral_mix(projected, padded, segment, block):
    slots, width = (projected.shape[0], projected.shape[2])
    blocks = slots // block
    pieces = []
    for row_block in range(blocks):
        total = jnp.zeros((block, width), jnp.float32)
        for col_block in range(row_block + 1):

            def pair_sum(row_block=row_block, col_block=col_block):
                tiles = pair_tiles(padded, segment, row_block, col_block, block)
                values = projected[col_block * block : (col_block + 1) * block, :FILTERS]
                return jnp.einsum("kts,skd->td", tiles, values, preferred_element_type=jnp.float32)

            total = total + pair_sum()
        pieces.append(total)
    mixed = jnp.concatenate(pieces, axis=0)
    for lag in range(AR_ORDER):
        column = projected[:, FILTERS + lag].astype(jnp.float32)
        if lag > 0:
            column = jnp.concatenate([jnp.zeros((lag, width), jnp.float32), column[:-lag]], axis=0)
        mixed = mixed + jnp.where(lag_keep(segment, lag)[:, None], column, 0.0)
    return mixed


def spectral_back(grad_low, padded, segment, block):
    slots, width = grad_low.shape
    blocks = slots // block
    pieces = []
    for col_block in range(blocks):
        total = jnp.zeros((block, FILTERS, width), jnp.float32)
        for row_block in range(col_block, blocks):

            def pair_term(row_block=row_block, col_block=col_block):
                tiles = pair_tiles(padded, segment, row_block, col_block, block)
                incoming = grad_low[row_block * block : (row_block + 1) * block]
                return jnp.einsum(
                    "kts,td->skd", tiles, incoming, preferred_element_type=jnp.float32
                )

            total = total + pair_term()
        pieces.append(total)
    spectral = jnp.concatenate(pieces, axis=0)
    lagged = []
    widened = grad_low.astype(jnp.float32)
    for lag in range(AR_ORDER):
        masked = jnp.where(lag_keep(segment, lag)[:, None], widened, 0.0)
        if lag > 0:
            masked = jnp.concatenate([masked[lag:], jnp.zeros((lag, width), jnp.float32)], axis=0)
        lagged.append(masked)
    return jnp.concatenate([spectral, jnp.stack(lagged, axis=1)], axis=1)


def adam_step(weight, grad, first, second, rate, decay):
    first_new = BETA_ONE * first + (1.0 - BETA_ONE) * grad
    second_new = BETA_TWO * second + (1.0 - BETA_TWO) * grad * grad
    corr_one = 1.0 - BETA_ONE**STEP
    corr_two = 1.0 - BETA_TWO**STEP
    update = first_new / corr_one / (jnp.sqrt(second_new / corr_two) + ADAM_EPS)
    return (weight - rate * (update + decay * weight), first_new, second_new)


def body(
    inputs,
    lengths,
    filters,
    cotangent,
    mixer_weight,
    gate_up_weight,
    down_weight,
    norm_gains,
    mixer_first,
    gate_up_first,
    down_first,
    gains_first,
    mixer_second,
    gate_up_second,
    down_second,
    gains_second,
    mixer_average,
):
    slots, width = inputs.shape
    block = min(128, slots)
    segment = layout(lengths, slots)[0]
    live = segment < 3
    masters_low = (
        mixer_weight.astype(jnp.bfloat16),
        gate_up_weight.astype(jnp.bfloat16),
        down_weight.astype(jnp.bfloat16),
        norm_gains.astype(jnp.bfloat16),
    )
    mixer_full, gate_up_full, down_full, gains_full = (
        lax.all_gather(masters_low[0], ("dp", "fsdp"), axis=0, tiled=True),
        lax.all_gather(masters_low[1], ("dp", "fsdp"), axis=0, tiled=True),
        lax.all_gather(masters_low[2], ("dp", "fsdp"), axis=0, tiled=True),
        lax.all_gather(masters_low[3], ("dp", "fsdp"), axis=1, tiled=True),
    )
    gains_value = gains_full.astype(jnp.float32)
    padded = jnp.concatenate([jnp.zeros((FILTERS, block - 1), filters.dtype), filters], axis=1)
    source = inputs.astype(jnp.float32)
    scale_one = lax.rsqrt(jnp.mean(source * source, axis=-1, keepdims=True) + NORM_EPS)
    hat_one = source * scale_one
    normed = (hat_one * gains_value[0]).astype(jnp.bfloat16)
    projected = lax.dot_general(
        normed, mixer_full, LAST_CONTRACT, preferred_element_type=jnp.float32
    ).astype(jnp.bfloat16)
    projected = projected.reshape(slots, FILTERS + AR_ORDER, width)
    hidden = source + spectral_mix(projected, padded, segment, block)
    scale_two = lax.rsqrt(jnp.mean(hidden * hidden, axis=-1, keepdims=True) + NORM_EPS)
    hat_two = hidden * scale_two
    normed_two = (hat_two * gains_value[1]).astype(jnp.bfloat16)
    gate_up = lax.dot_general(
        normed_two, gate_up_full, LAST_CONTRACT, preferred_element_type=jnp.float32
    )
    gate = gate_up[:, :FF]
    upper = gate_up[:, FF:]
    sigma = jax.nn.sigmoid(gate)
    swish = gate * sigma
    act = (swish * upper).astype(jnp.bfloat16)
    branch = jnp.dot(act, down_full, preferred_element_type=jnp.float32)
    output = (hidden + branch).astype(jnp.bfloat16)
    mixer_full, gate_up_full, down_full, gains_full = (
        lax.all_gather(masters_low[0], ("dp", "fsdp"), axis=0, tiled=True),
        lax.all_gather(masters_low[1], ("dp", "fsdp"), axis=0, tiled=True),
        lax.all_gather(masters_low[2], ("dp", "fsdp"), axis=0, tiled=True),
        lax.all_gather(masters_low[3], ("dp", "fsdp"), axis=1, tiled=True),
    )
    gains_value = gains_full.astype(jnp.float32)
    back = jnp.where(live[:, None], cotangent, jnp.zeros((), jnp.bfloat16))
    grad_down = lax.dot_general(act, back, ROWS_CONTRACT, preferred_element_type=jnp.float32)
    grad_act = lax.dot_general(back, down_full, LAST_CONTRACT, preferred_element_type=jnp.float32)
    slope = sigma * (1.0 + gate * (1.0 - sigma))
    grad_gate_up = jnp.concatenate([grad_act * upper * slope, grad_act * swish], axis=1).astype(
        jnp.bfloat16
    )
    grad_gate_up_weight = lax.dot_general(
        grad_gate_up, normed_two, ROWS_CONTRACT, preferred_element_type=jnp.float32
    )
    grad_two = jnp.dot(grad_gate_up, gate_up_full, preferred_element_type=jnp.float32)
    weighted_two = grad_two * gains_value[1]
    gain_grad_two = jnp.sum(grad_two * hat_two, axis=0)
    grad_hidden = back.astype(jnp.float32) + scale_two * (
        weighted_two - hat_two * jnp.mean(weighted_two * hat_two, axis=-1, keepdims=True)
    )
    grad_low = grad_hidden.astype(jnp.bfloat16)
    grad_projected = (
        spectral_back(grad_low, padded, segment, block)
        .reshape(slots, (FILTERS + AR_ORDER) * width)
        .astype(jnp.bfloat16)
    )
    grad_mixer = lax.dot_general(
        grad_projected, normed, ROWS_CONTRACT, preferred_element_type=jnp.float32
    )
    grad_one = jnp.dot(grad_projected, mixer_full, preferred_element_type=jnp.float32)
    weighted_one = grad_one * gains_value[0]
    gain_grad_one = jnp.sum(grad_one * hat_one, axis=0)
    input_grad = grad_hidden + scale_one * (
        weighted_one - hat_one * jnp.mean(weighted_one * hat_one, axis=-1, keepdims=True)
    )
    grad_gains = jnp.stack([gain_grad_one, gain_grad_two], axis=0)
    shard_mixer, shard_gate_up, shard_down, shard_gains = (
        lax.psum_scatter(grad_mixer, ("dp", "fsdp"), scatter_dimension=0, tiled=True),
        lax.psum_scatter(grad_gate_up_weight, ("dp", "fsdp"), scatter_dimension=0, tiled=True),
        lax.psum_scatter(grad_down, ("dp", "fsdp"), scatter_dimension=0, tiled=True),
        lax.psum_scatter(grad_gains, ("dp", "fsdp"), scatter_dimension=1, tiled=True),
    )
    squares = (
        jnp.sum(shard_mixer * shard_mixer)
        + jnp.sum(shard_gate_up * shard_gate_up)
        + jnp.sum(shard_down * shard_down)
        + jnp.sum(shard_gains * shard_gains)
    )
    grad_norm = jnp.sqrt(lax.psum(squares, ("dp", "fsdp")))
    factor = CLIP_LIMIT / jnp.maximum(grad_norm, CLIP_LIMIT)
    mixer_new, mixer_first_new, mixer_second_new = adam_step(
        mixer_weight, shard_mixer * factor, mixer_first, mixer_second, RATE_MATRIX, DECAY_MATRIX
    )
    gate_up_new, gate_up_first_new, gate_up_second_new = adam_step(
        gate_up_weight,
        shard_gate_up * factor,
        gate_up_first,
        gate_up_second,
        RATE_MATRIX,
        DECAY_MATRIX,
    )
    down_new, down_first_new, down_second_new = adam_step(
        down_weight, shard_down * factor, down_first, down_second, RATE_MATRIX, DECAY_MATRIX
    )
    gains_new, gains_first_new, gains_second_new = adam_step(
        norm_gains, shard_gains * factor, gains_first, gains_second, RATE_GAIN, 0.0
    )
    mixer_average_new = AVERAGE_KEEP * mixer_average + (1.0 - AVERAGE_KEEP) * mixer_new
    return (
        output,
        input_grad,
        grad_norm,
        mixer_new,
        gate_up_new,
        down_new,
        gains_new,
        mixer_first_new,
        gate_up_first_new,
        down_first_new,
        gains_first_new,
        mixer_second_new,
        gate_up_second_new,
        down_second_new,
        gains_second_new,
        mixer_average_new,
    )


def solution(mesh):
    return jax.shard_map(
        body,
        mesh=mesh,
        in_specs=(
            P(("dp", "fsdp"), None),
            P(("dp", "fsdp"), None),
            P(),
            P(("dp", "fsdp"), None),
            P(("dp", "fsdp"), None),
            P(("dp", "fsdp"), None),
            P(("dp", "fsdp"), None),
            P(None, ("dp", "fsdp")),
            P(("dp", "fsdp"), None),
            P(("dp", "fsdp"), None),
            P(("dp", "fsdp"), None),
            P(None, ("dp", "fsdp")),
            P(("dp", "fsdp"), None),
            P(("dp", "fsdp"), None),
            P(("dp", "fsdp"), None),
            P(None, ("dp", "fsdp")),
            P(("dp", "fsdp"), None),
        ),
        out_specs=(
            P(("dp", "fsdp"), None),
            P(("dp", "fsdp"), None),
            P(),
            P(("dp", "fsdp"), None),
            P(("dp", "fsdp"), None),
            P(("dp", "fsdp"), None),
            P(None, ("dp", "fsdp")),
            P(("dp", "fsdp"), None),
            P(("dp", "fsdp"), None),
            P(("dp", "fsdp"), None),
            P(None, ("dp", "fsdp")),
            P(("dp", "fsdp"), None),
            P(("dp", "fsdp"), None),
            P(("dp", "fsdp"), None),
            P(None, ("dp", "fsdp")),
            P(("dp", "fsdp"), None),
        ),
        check_vma=False,
    )
```

profile of v0, /device:TPU:0, one launch (start us, length us, event | category | flops | bytes accessed | tf_op | source)
XLA Modules:
  0.0 1112.5 jit_solution(7490312065019038688)
XLA Ops:
  15.9 6.0 reshape.651
  23.3 6.0 reshape.653
  29.3 43.7 %all-gather = bf16[32,16,2]{1,2,0:T(2,128)(2,1)S(1)} all-gather(bf16[1,16,2]{1,2,0:T(2,128)(2,1)S(1)} %convert_bitcast_fusion.1), channel_id=1, replica_groups=mesh['dp'=4,'fsdp'=8] {'dp','fsdp'}, dimensions={0}, use_global_device_ids=true | all-gather | bytes 2112 | tf_op jit(solution)/shard_map/all_gather | solution.py:148
  74.8 6.0 reshape.654
  82.2 6.0 reshape.655
  88.5 4.9 broadcast_select_fusion.7
  95.8 3.9 broadcast_select_fusion.5
  117.8 21.6 %convolution_convert_fusion = bf16[512,13824]{1,0:T(8,128)(2,1)} fusion(bf16[13824,512]{1,0:T(8,128)(2,1)} %all-gather.5.cloned.1.call-done, bf16[512,512]{1,0:T(8,128)(2,1)S(1)} %copy-done.3, f32[512]{0:T(512)S(1)} %bitcast.229, f32[512]{0:T(512)S(1)} %add_rsqrt_fusion.1), kind=kOutput, calls=%fused_computation | convolution fusion | flops 7255883776 | bytes 28839936 | tf_op jit(solution)/shard_map/dot_general | solution.py:156
  139.3 18.7 %copy.120 = bf16[512,13824]{0,1:T(8,128)(2,1)} copy(bf16[512,13824]{1,0:T(8,128)(2,1)} %convolution_convert_fusion) | data formatting | bytes 28311552 | tf_op jit(solution)/shard_map/convert_element_type | solution.py:158
  176.6 4.1 fusion.31
  193.8 8.2 fusion.125
  202.0 38.3 %all-gather.9.cloned.1.call-done = bf16[2048,512]{1,0:T(8,128)(2,1)} async-done(((bf16[64,512]{1,0:T(8,128)(2,1)}), bf16[2048,512]{1,0:T(8,128)(2,1)}) %all-gather.9.cloned.1.call-update) | async-done | bytes 2097168 | tf_op jit(solution)/shard_map/all_gather | solution.py:147
  240.3 7.0 multiply_convert_fusion.1
  254.9 3.6 fusion.99
  258.5 3.6 fusion.103
  262.1 3.6 fusion.109
  270.4 3.6 fusion.111
  284.3 8.6 fusion.2
  292.8 10.8 fusion.1
  303.6 14.6 %pad_maximum_fusion = bf16[512,27,512]{2,0,1:T(8,128)(2,1)} fusion(bf16[512,1,512]{2,0,1:T(8,128)(2,1)} %pad_bitcast_fusion, bf16[512,1,512]{2,0,1:T(8,128)(2,1)} %pad_bitcast_fusion.1, bf16[512,1,512]{2,0,1:T(8,128)(2,1)} %get-tuple-element.33, bf16[128,24,512]{2,0,1:T(8,128)(2,1)} %convert_bitcast_fusion, bf16[128,24,512]{2,0,1:T(8,128)(2,1)} %fusion.3, ...), kind=kLoop, calls=%fused_computation.1 | loop fusion | flops 99090432 | bytes 28311552 | tf_op jit(solution)/shard_map/concatenate | solution.py:103
  318.2 18.7 %copy.139 = bf16[512,27,512]{0,2,1:T(8,128)(2,1)} copy(bf16[512,27,512]{2,0,1:T(8,128)(2,1)} %pad_maximum_fusion) | data formatting | bytes 28311552 | tf_op jit(solution)/shard_map/concatenate | solution.py:103
  336.9 15.7 %fusion.84 = (f32[512]{0:T(512)S(1)}, f32[512]{0:T(512)S(1)}, f32[512,512]{1,0:T(8,128)}) fusion(bf16[512,512]{1,0:T(8,128)(2,1)S(1)} %copy-done.4, f32[512]{0:T(512)S(1)} %add_rsqrt_fusion.1, f32[512]{0:T(512)S(1)} %bitcast.230, bf16[512,13824]{0,1:T(8,128)(2,1)} %bitcast.171, bf16[13824,512]{1,0:T(8,128)(2,1)} %all-gather.5.cloned.1.call-done), kind=kOutput, calls=%fused_computation.68 | convolution fusion | flops 7249591296 | bytes 29892608 | tf_op jit(solution)/shard_map/dot_general | solution.py:206
  353.5 5.0 fusion.123
  359.8 7.9 fusion.10
  367.8 18.4 %fusion.93 = f32[13824,512]{1,0:T(8,128)} fusion(bf16[512,13824]{0,1:T(8,128)(2,1)} %bitcast.172, bf16[512,512]{1,0:T(8,128)(2,1)S(1)} %copy-done.4, f32[512]{0:T(512)S(1)} %bitcast.231, f32[512]{0:T(512)S(1)} %add_rsqrt_fusion.1), kind=kOutput, calls=%fused_computation.109 | convolution fusion | flops 7248805888 | bytes 42995712 | tf_op jit(solution)/shard_map/dot_general | solution.py:203
  386.2 4.4 fusion.30
  390.6 95.3 %reduce-scatter.13.cloned.1.call-done = f32[16,2]{1,0:T(8,128)} async-done(((f32[512,2]{1,0:T(8,128)}), f32[16,2]{1,0:T(8,128)}) %reduce-scatter.13.cloned.1.call-update) | async-done | bytes 144
  487.3 140.3 %reduce-scatter.11.cloned.1.call-done = f32[64,512]{1,0:T(8,128)} async-done(((f32[2048,512]{1,0:T(8,128)}), f32[64,512]{1,0:T(8,128)}) %reduce-scatter.11.cloned.1.call-update) | async-done | bytes 131088 | tf_op jit(solution)/shard_map/reduce_scatter | solution.py:216
  629.1 149.0 %reduce-scatter.9.cloned.1.call-done = f32[128,512]{1,0:T(8,128)} async-done(((f32[4096,512]{1,0:T(8,128)}), f32[128,512]{1,0:T(8,128)}) %reduce-scatter.9.cloned.1.call-update) | async-done | bytes 262160 | tf_op jit(solution)/shard_map/reduce_scatter | solution.py:215
  779.7 268.0 %reduce-scatter.7.cloned.1.call-done = f32[432,512]{1,0:T(8,128)} async-done(((f32[13824,512]{1,0:T(8,128)}), f32[432,512]{1,0:T(8,128)}) %reduce-scatter.7.cloned.1.call-update) | async-done | bytes 884752 | tf_op jit(solution)/shard_map/reduce_scatter | solution.py:214
  1054.8 40.1 %psum.7 = f32[]{:T(128)} all-reduce(f32[]{:T(128)S(6)} %add.221), channel_id=1, replica_groups=mesh['dp'=4,'fsdp'=8] {'dp','fsdp'}, use_global_device_ids=true, to_apply=%region_16.17 | all-reduce | flops 1 | bytes 8 | tf_op jit(solution)/shard_map/psum | solution.py:225
  1100.3 4.1 multiply_add_fusion.1
  (181 shorter events, 103.8 us)
Async XLA Ops:
  7.2 110.6 %all-gather.5.cloned.1.call-start = ((), (), s32[]{:S(2)}) async-start(), calls=%async_computation.4 | async-start | bytes 14598144 | tf_op jit(solution)/shard_map/all_gather | solution.py:145
  9.2 184.5 %all-gather.7.cloned.1.call-start = ((), (), s32[]{:S(2)}) async-start(), calls=%async_computation.5 | async-start | bytes 4325376 | tf_op jit(solution)/shard_map/all_gather | solution.py:146
  10.9 229.3 %all-gather.9.cloned.1.call-start = ((), (), s32[]{:S(2)}) async-start(), calls=%async_computation.6 | async-start | bytes 2162688 | tf_op jit(solution)/shard_map/all_gather | solution.py:147
  12.6 473.3 %reduce-scatter.13.cloned.1.call-start = ((), (), s32[]{:S(2)}) async-start(), calls=%async_computation.10 | async-start | bytes 270336
  22.2 7.0 copy-start.28
  22.3 51.0 %copy-start.3 = (bf16[512,512]{1,0:T(8,128)(2,1)S(1)}, bf16[512,512]{1,0:T(8,128)(2,1)}, u32[]{:S(2)}) copy-start(bf16[512,512]{1,0:T(8,128)(2,1)} %param.17) | copy-start | bytes 1572868
  173.1 11.0 copy-start
  180.7 5.7 copy-start.19
  184.0 3.6 copy-start.18
  186.4 2.4 copy-start.21
  193.7 56.1 %copy-start.1 = (f32[512,512]{1,0:T(8,128)}, f32[512,512]{1,0:T(8,128)S(1)}, u32[]{:S(2)}) copy-start(f32[512,512]{1,0:T(8,128)S(1)} %get-tuple-element.37) | copy-start | bytes 3145732
  193.8 46.5 %copy-start.25 = (bf16[512,512]{1,0:T(8,128)(2,1)S(1)}, bf16[512,512]{1,0:T(8,128)(2,1)}, u32[]{:S(2)}) copy-start(bf16[512,512]{1,0:T(8,128)(2,1)} %param.20) | copy-start | bytes 1572868
  240.3 7.0 copy-start.13
  247.3 2.5 copy-start.32
  247.3 2.5 copy-start.33
  254.9 3.6 copy-start.12
  258.5 3.6 copy-start.11
  262.1 3.6 copy-start.10
  266.8 3.6 copy-start.9
  270.4 3.6 copy-start.7
  318.2 18.7 %copy-start.4 = (bf16[512,512]{1,0:T(8,128)(2,1)S(1)}, bf16[512,512]{1,0:T(8,128)(2,1)}, u32[]{:S(2)}) copy-start(bf16[512,512]{1,0:T(8,128)(2,1)} %param.17) | copy-start | bytes 1572868
  336.9 16.6 %copy-start.26 = (bf16[512,512]{1,0:T(8,128)(2,1)S(1)}, bf16[512,512]{1,0:T(8,128)(2,1)}, u32[]{:S(2)}) copy-start(bf16[512,512]{1,0:T(8,128)(2,1)} %param.20) | copy-start | bytes 1572868
  353.5 274.1 %reduce-scatter.11.cloned.1.call-start = ((), (), s32[]{:S(2)}) async-start(), calls=%async_computation.9 | async-start | bytes 4325376 | tf_op jit(solution)/shard_map/reduce_scatter | solution.py:216
  358.6 419.5 %reduce-scatter.9.cloned.1.call-start = ((), (), s32[]{:S(2)}) async-start(), calls=%async_computation.8 | async-start | bytes 8650752 | tf_op jit(solution)/shard_map/reduce_scatter | solution.py:215
  367.7 679.9 %reduce-scatter.7.cloned.1.call-start = ((), (), s32[]{:S(2)}) async-start(), calls=%async_computation.7 | async-start | bytes 29196288 | tf_op jit(solution)/shard_map/reduce_scatter | solution.py:214
  386.2 666.1 %copy-start.14 = (f32[512,512]{1,0:T(8,128)S(1)}, f32[512,512]{1,0:T(8,128)}, u32[]{:S(2)}) copy-start(f32[512,512]{1,0:T(8,128)} %get-tuple-element.35) | copy-start | bytes 3145732
  390.6 705.0 %copy-start.29 = (f32[2,16]{1,0:T(2,128)S(1)}, f32[2,16]{1,0:T(2,128)}, u32[]{:S(2)}) copy-start(f32[2,16]{1,0:T(2,128)} %param.24) | copy-start | bytes 388
  390.6 705.0 %copy-start.30 = (f32[2,16]{1,0:T(2,128)S(1)}, f32[2,16]{1,0:T(2,128)}, u32[]{:S(2)}) copy-start(f32[2,16]{1,0:T(2,128)} %param.28) | copy-start | bytes 388
  390.6 705.1 %copy-start.31 = (f32[2,16]{1,0:T(2,128)S(1)}, f32[2,16]{1,0:T(2,128)}, u32[]{:S(2)}) copy-start(f32[2,16]{1,0:T(2,128)} %param.32) | copy-start | bytes 388
  390.6 705.7 %copy-start.27 = (f32[64,512]{1,0:T(8,128)S(1)}, f32[64,512]{1,0:T(8,128)}, u32[]{:S(2)}) copy-start(f32[64,512]{1,0:T(8,128)} %param.23) | copy-start | bytes 393220
  390.6 709.7 %copy-start.16 = (f32[432,512]{1,0:T(8,128)S(1)}, f32[432,512]{1,0:T(8,128)}, u32[]{:S(2)}) copy-start(f32[432,512]{1,0:T(8,128)} %param.21) | copy-start | bytes 2654212
  1047.6 52.7 %copy-start.15 = (f32[432,512]{1,0:T(8,128)S(1)}, f32[432,512]{1,0:T(8,128)}, u32[]{:S(2)}) copy-start(f32[432,512]{1,0:T(8,128)} %reduce-scatter.7.cloned.1.call-done) | copy-start | bytes 2654212
  (9 other events, 14.9 us)
Sparse Core Ops, SparseCore 0:
  11.6 106.1 all-gather.4
  121.3 60.2 all-gather.6
  185.2 55.0 all-gather.8
  353.6 132.2 reduce-scatter.12
  488.1 139.3 reduce-scatter.10
  629.8 148.1 reduce-scatter.8
  785.6 261.9 reduce-scatter.6
where the time goes:
time: 1120 us; the launch traced here: 1110 us
  waiting for transfers between devices  691 us (62%)
  matrix products  138 us (12%)
  local copies, waits for them, and re-layouts  105 us (9%)
  blocking collectives  83.8 us (7%)
  other arithmetic  74.7 us (7%)
  between operations  19.4 us (2%)
    reduce_scatter x1, waiting for transfers between devices, body(): lax.psum_scatter(grad_mixer, ('dp', 'fsdp'), scatter_dimension=0, tiled=T...  268 us
    reduce_scatter x1, waiting for transfers between devices, body(): lax.psum_scatter(grad_gate_up_weight, ('dp', 'fsdp'), scatter_dimension=0...  149 us
    reduce_scatter x1, waiting for transfers between devices, body(): lax.psum_scatter(grad_down, ('dp', 'fsdp'), scatter_dimension=0, tiled=True)  140 us
    unnamed x8, waiting for transfers between devices  95.4 us
    all_gather x1, blocking collectives, body(): lax.all_gather(masters_low[3], ('dp', 'fsdp'), axis=1, tiled=True)  43.7 us
    psum x1, blocking collectives, body(): grad_norm = jnp.sqrt(lax.psum(squares, ('dp', 'fsdp')))  40.1 us
    all_gather x1, waiting for transfers between devices, body(): lax.all_gather(masters_low[2], ('dp', 'fsdp'), axis=0, tiled=True)  38.3 us
    unnamed x10, matrix products  25.3 us
  transfers between devices with their start and end apart: 7, of which 6 were waited for; matrix products, arithmetic and copies ran while one was open for 17% of the time, Pallas kernels for 0%

commit v1 on v0

v1 whole, which is shorter than its diff:
```python
import math

import jax
import jax.numpy as jnp
import numpy as np
from jax import lax
from jax.experimental import pallas as pl
from jax.experimental.pallas import tpu as pltpu
from jax.sharding import PartitionSpec as P

bf = jnp.bfloat16
f32 = jnp.float32
FILTERS = 24
AR_ORDER = 3
STEP = 10
NORM_EPS = 1e-05
CLIP_LIMIT = 1.0
BETA_ONE = 0.9
BETA_TWO = 0.95
ADAM_EPS = 1e-08
RATE_MATRIX = 0.03
RATE_GAIN = 0.5
DECAY_MATRIX = 0.1
AVERAGE_KEEP = 0.9
CHIPS = ("d0", "d1", "z")
EVERY = CHIPS + ("core",)
NT=(((1,),(1,)),((),())); NN=(((1,),(0,)),((),())); TN=(((0,),(0,)),((),()))
def dot(a,b,d=NN): return lax.dot_general(a,b,d,preferred_element_type=f32)

def seg_of(place, ends_ref, g):
    return sum((place >= ends_ref[g, j]).astype(jnp.int32) for j in range(3))

def causal_mask(ends_ref, g, n, transposed):
    col = lax.broadcasted_iota(jnp.int32, (n, 1), 0); row = lax.broadcasted_iota(jnp.int32, (1, n), 1)
    sc, sr = seg_of(col, ends_ref, g), seg_of(row, ends_ref, g)
    order = (col <= row) if transposed else (col >= row)
    return ((sc == sr) & (sc < 3) & order).astype(f32).astype(bf)

def strip(row, sub):
    x = jnp.broadcast_to(row, (sub, row.shape[-1]))
    return pltpu.roll(x, 0, 1, stride=1, stride_axis=0).astype(bf)

def u_kernel(ends_ref, taps_ref, hat_ref, u_ref, mask, table):
    n = mask.shape[1]; q = n//4; h = n//2; w = hat_ref.shape[2]; per = taps_ref.shape[1]
    @pl.when(pl.program_id(0) == 0)
    def _():
        for g in range(2): mask[g] = causal_mask(ends_ref, g, n, False)
        table[...] = jnp.zeros_like(table)
    for j in range(per):
        s = strip(taps_ref[0, j:j+1, :], q)
        for g in range(2):
            for i in range(4):
                table[g, i*q:(i+1)*q, :(i+1)*q] = s[:, (3-i)*q:] * mask[g, i*q:(i+1)*q, :(i+1)*q]
            u_ref[0, g*n:g*n+h, j*w:(j+1)*w] = dot(table[g, :h, :h], hat_ref[g, :h]).astype(bf)
            u_ref[0, g*n+h:(g+1)*n, j*w:(j+1)*w] = dot(table[g, h:, :], hat_ref[g]).astype(bf)

def u_call(ends, taps, hat, per=3):
    steps = taps.shape[0]//per; n=hat.shape[1]; w=hat.shape[2]
    return pl.pallas_call(u_kernel, grid=(steps,),
        in_specs=[pl.BlockSpec(memory_space=pltpu.SMEM), pl.BlockSpec((1,per,n), lambda i:(i,0,0)), pl.BlockSpec((2,n,w), lambda i:(0,0,0))],
        out_specs=pl.BlockSpec((1,2*n,per*w), lambda i:(i,0,0)),
        out_shape=jax.ShapeDtypeStruct((steps,2*n,per*w), bf),
        scratch_shapes=[pltpu.VMEM((2,n,n),bf), pltpu.VMEM((2,n,n),bf)],
        compiler_params=pltpu.CompilerParams(vmem_limit_bytes=56<<20), name="spread")(ends, taps.reshape(steps,per,n), hat)

def mix_kernel(gain_ref, u_ref, w_ref, m_ref, wide):
    per = wide.shape[1]//w_ref.shape[1]; w=w_ref.shape[1]; d=wide.shape[0]
    for j in range(per):
        wide[:, j*w:(j+1)*w] = (w_ref[j*d:(j+1)*d].astype(f32)*gain_ref[...]).astype(bf)
    r = dot(u_ref[0], wide[...], NT)
    @pl.when(pl.program_id(0) == 0)
    def _(): m_ref[...] = r
    @pl.when(pl.program_id(0) > 0)
    def _(): m_ref[...] += r

def mix_call(gain, u, w):
    steps, t, pw = u.shape; width = w.shape[1]; per = pw//width; d = w.shape[0]//(steps*per)
    return pl.pallas_call(mix_kernel, grid=(steps,),
        in_specs=[pl.BlockSpec((1,width), lambda i:(0,0)), pl.BlockSpec((1,t,pw), lambda i:(i,0,0)), pl.BlockSpec((per*d,width), lambda i:(i,0))],
        out_specs=pl.BlockSpec((t,d), lambda i:(0,0)), out_shape=jax.ShapeDtypeStruct((t,d), f32),
        scratch_shapes=[pltpu.VMEM((d,pw),bf)],
        compiler_params=pltpu.CompilerParams(vmem_limit_bytes=56<<20), name="mix")(gain, u, w)

def dw_kernel(gain_ref, gt_ref, u_ref, o_ref):
    w = gain_ref.shape[1]; d = gt_ref.shape[0]; per = u_ref.shape[2]//w
    r = dot(gt_ref[...], u_ref[0])
    for j in range(per):
        o_ref[j*d:(j+1)*d, :] = (r[:, j*w:(j+1)*w]*gain_ref[...]).astype(bf)

def dw_call(gain, gt, u):
    steps, t, pw = u.shape; w = gain.shape[1]; per = pw//w; d = gt.shape[0]
    return pl.pallas_call(dw_kernel, grid=(steps,),
        in_specs=[pl.BlockSpec((1,w), lambda i:(0,0)), pl.BlockSpec((d,t), lambda i:(0,0)), pl.BlockSpec((1,t,pw), lambda i:(i,0,0))],
        out_specs=pl.BlockSpec((per*d,w), lambda i:(i,0)), out_shape=jax.ShapeDtypeStruct((steps*per*d,w), bf),
        compiler_params=pltpu.CompilerParams(vmem_limit_bytes=56<<20), name="mixer_grad")(gain, gt, u)

def back_kernel(ends_ref, taps_ref, g_ref, w_ref, o_ref, mask, tlo, thi, tb, vlo, vhi):
    n = mask.shape[1]; q=n//4; h=n//2; w=w_ref.shape[1]; per=taps_ref.shape[1]; d=g_ref.shape[1]
    @pl.when(pl.program_id(0) == 0)
    def _():
        for g in range(2): mask[g] = causal_mask(ends_ref, g, n, True)
        tlo[...] = jnp.zeros_like(tlo); tb[...] = jnp.zeros_like(tb)
        o_ref[...] = jnp.zeros_like(o_ref)
    for j in range(per):
        v = dot(g_ref[...], w_ref[j*d:(j+1)*d]).astype(bf)
        for g in range(2):
            vlo[g, j*h:(j+1)*h] = v[g*n:g*n+h]
            vhi[g, j*h:(j+1)*h] = v[g*n+h:(g+1)*n]
        s = strip(taps_ref[0, j:j+1, :], q)
        for g in range(2):
            m = mask[g]
            tlo[g, 0:q, j*h:j*h+q] = s[:, :q]*m[0:q, 0:q]
            tlo[g, 0:q, j*h+q:j*h+h] = s[:, q:2*q]*m[0:q, q:2*q]
            tlo[g, q:h, j*h+q:j*h+h] = s[:, :q]*m[q:h, q:h]
            thi[g, 0:q, j*h:j*h+h] = s[:, 2*q:4*q]*m[0:q, h:]
            thi[g, q:h, j*h:j*h+h] = s[:, q:3*q]*m[q:h, h:]
            tb[g, 0:q, j*h:j*h+h] = s[:, 0:2*q]*m[h:h+q, h:]
            tb[g, q:h, j*h+q:j*h+h] = s[:, 0:q]*m[h+q:, h+q:]
    for g in range(2):
        o_ref[g*n:g*n+h] += dot(tlo[g], vlo[g]) + dot(thi[g], vhi[g])
        o_ref[g*n+h:(g+1)*n] += dot(tb[g], vhi[g])

def back_call(ends, taps, g, w, per=3):
    steps = taps.shape[0]//per; n = taps.shape[1]; t, d = g.shape; width = w.shape[1]
    sc = lambda *s: pltpu.VMEM(s, bf)
    return pl.pallas_call(back_kernel, grid=(steps,),
        in_specs=[pl.BlockSpec(memory_space=pltpu.SMEM), pl.BlockSpec((1,per,n), lambda i:(i,0,0)), pl.BlockSpec((t,d), lambda i:(0,0)), pl.BlockSpec((per*d,width), lambda i:(i,0))],
        out_specs=pl.BlockSpec((t,width), lambda i:(0,0)), out_shape=jax.ShapeDtypeStruct((t,width), f32),
        scratch_shapes=[sc(2,n,n), sc(2,n//2,per*n//2), sc(2,n//2,per*n//2), sc(2,n//2,per*n//2), sc(2,per*n//2,width), sc(2,per*n//2,width)],
        compiler_params=pltpu.CompilerParams(vmem_limit_bytes=56<<20), name="spread_back")(ends, taps.reshape(steps,per,n), g, w)

def ffn_kernel(n2_ref, back_ref, wg_ref, wu_ref, wd_ref, br_ref, gt_ref, dgu_ref, dd_ref):
    n2, bk = n2_ref[...], back_ref[...]
    wg, wu, wd = wg_ref[...], wu_ref[...], wd_ref[...]
    gate = dot(n2, wg, NT); up = dot(n2, wu, NT)
    ga = dot(bk, wd, NT)
    sig = 1.0/(1.0+jnp.exp(-gate)); sw = gate*sig
    act = (sw*up).astype(bf)
    gg = (ga*up*(sig*(1.0+gate*(1.0-sig)))).astype(bf); gu = (ga*sw).astype(bf)
    br = dot(act, wd); gt = dot(gg, wg) + dot(gu, wu)
    @pl.when(pl.program_id(0) == 0)
    def _(): br_ref[...] = br; gt_ref[...] = gt
    @pl.when(pl.program_id(0) > 0)
    def _(): br_ref[...] += br; gt_ref[...] += gt
    dd_ref[...] = dot(act, bk, TN).astype(bf)
    dgu_ref[0] = dot(gg, n2, TN).astype(bf)
    dgu_ref[1] = dot(gu, n2, TN).astype(bf)

def ffn_call(n2, back, wgu, wd, chunk=256):
    t, d = n2.shape; u = wd.shape[0]; steps = u//chunk
    full = pl.BlockSpec((t,d), lambda i:(0,0)); row = pl.BlockSpec((chunk,d), lambda i:(i,0)); row2 = pl.BlockSpec((chunk,d), lambda i:(i+steps,0))
    S = jax.ShapeDtypeStruct
    return pl.pallas_call(ffn_kernel, grid=(steps,), in_specs=[full,full,row,row2,row],
        out_specs=[full,full,pl.BlockSpec((2,chunk,d), lambda i:(0,i,0)),row], out_shape=[S((t,d),f32),S((t,d),f32),S((2,u,d),bf),S((u,d),bf)],
        compiler_params=pltpu.CompilerParams(vmem_limit_bytes=56<<20), name="ffn")(n2, back, wgu, wgu, wd)


def adam_step(weight, grad, first, second, rate, decay):
    first_new = BETA_ONE * first + (1.0 - BETA_ONE) * grad
    second_new = BETA_TWO * second + (1.0 - BETA_TWO) * grad * grad
    corr_one = 1.0 - BETA_ONE**STEP
    corr_two = 1.0 - BETA_TWO**STEP
    update = first_new / corr_one / (jnp.sqrt(second_new / corr_two) + ADAM_EPS)
    return (weight - rate * (update + decay * weight), first_new, second_new)


def swap(v):
    return lax.ppermute(v, "core", [(0, 1), (1, 0)])


def join(mine, other, core, axis=0):
    return jnp.where(
        core == 0,
        jnp.concatenate([mine, other], axis=axis),
        jnp.concatenate([other, mine], axis=axis),
    )


def part(v, index, axis=0):
    size = v.shape[axis] // 2
    return lax.dynamic_slice_in_dim(v, index * size, size, axis)


def trade(v, core, axis=0):
    return join(part(v, core, axis), swap(part(v, 1 - core, axis)), core)


def add_trade(v, core):
    return part(v, core) + swap(part(v, 1 - core))


def body(
    inputs, lengths, filters, cotangent, mixer_weight, gate_up_weight, down_weight, norm_gains,
    mixer_first, gate_up_first, down_first, gains_first,
    mixer_second, gate_up_second, down_second, gains_second, mixer_average,
):
    slots, width = inputs.shape
    core = lax.axis_index("core")
    gather = lambda v: lax.all_gather(v, CHIPS, axis=0, tiled=True)
    scatter = lambda v: lax.psum_scatter(v, CHIPS, scatter_dimension=0, tiled=True)

    mixer_all = gather(trade(mixer_weight.astype(bf), core, 1))
    gate_up_all = gather(trade(gate_up_weight.astype(bf), core))
    down_all = gather(down_weight.astype(bf))
    gains = lax.all_gather(norm_gains.astype(bf), EVERY, axis=1, tiled=True).astype(f32)

    ends = jnp.cumsum(lengths, axis=-1).astype(jnp.int32)
    ends_both = join(ends, swap(ends), core)
    place = jnp.arange(slots, dtype=jnp.int32)
    live = place < ends[0, -1]
    back = jnp.where(live[:, None], cotangent, jnp.zeros((), bf))
    back_both = join(back, swap(back), core)
    taps = jnp.concatenate([filters.astype(f32), jnp.eye(AR_ORDER, slots, dtype=f32)])
    taps_turned = jnp.roll(taps[:, ::-1], 1 - slots // 4, axis=1)

    source = inputs.astype(f32)
    scale_one = lax.rsqrt(jnp.mean(source * source, axis=-1, keepdims=True) + NORM_EPS)
    hat_one = source * scale_one
    hat_both = trade(hat_one.astype(bf), core, 1).reshape(2, slots, width // 2)
    spread = u_call(ends_both, taps_turned, hat_both)
    gain_half = part(gains[0:1], core, 1)
    mixed = add_trade(mix_call(gain_half, spread, mixer_all), core)

    hidden = source + mixed
    scale_two = lax.rsqrt(jnp.mean(hidden * hidden, axis=-1, keepdims=True) + NORM_EPS)
    hat_two = hidden * scale_two
    normed_two = (hat_two * gains[1]).astype(bf)
    normed_both = join(normed_two, swap(normed_two), core)
    branch, grad_two, grad_gate_up, grad_down = ffn_call(normed_both, back_both, gate_up_all, down_all)
    output = (hidden + add_trade(branch, core)).astype(bf)
    grad_two = add_trade(grad_two, core)
    weighted_two = grad_two * gains[1]
    grad_hidden = back.astype(f32) + scale_two * (
        weighted_two - hat_two * jnp.mean(weighted_two * hat_two, axis=-1, keepdims=True)
    )
    grad_low = grad_hidden.astype(bf)
    grad_both = join(grad_low, swap(grad_low), core)
    grad_mixer = dw_call(gain_half, grad_both.T, spread)

    shard_gate_up = trade(scatter(grad_gate_up.reshape(-1, width)).astype(f32), core)
    shard_down = scatter(grad_down).astype(f32)
    pair = scatter(grad_mixer).astype(f32)
    shard_mixer = join(part(pair, core), swap(part(pair, 1 - core)), core, 1)

    grad_half = back_call(ends_both, taps, grad_both, mixer_all)
    grad_one = join(part(grad_half, core), swap(part(grad_half, 1 - core)), core, 1)
    weighted_one = grad_one * gains[0]
    input_grad = grad_hidden + scale_one * (
        weighted_one - hat_one * jnp.mean(weighted_one * hat_one, axis=-1, keepdims=True)
    )
    grad_gains = jnp.stack([jnp.sum(grad_one * hat_one, axis=0), jnp.sum(grad_two * hat_two, axis=0)])
    shard_gains = lax.psum_scatter(grad_gains, EVERY, scatter_dimension=1, tiled=True)

    squares = (
        jnp.sum(shard_mixer * shard_mixer)
        + jnp.sum(shard_gate_up * shard_gate_up)
        + jnp.sum(shard_down * shard_down)
        + jnp.sum(shard_gains * shard_gains)
    )
    grad_norm = jnp.sqrt(lax.psum(squares, EVERY))
    factor = CLIP_LIMIT / jnp.maximum(grad_norm, CLIP_LIMIT)
    mixer_new, mixer_first_new, mixer_second_new = adam_step(
        mixer_weight, shard_mixer * factor, mixer_first, mixer_second, RATE_MATRIX, DECAY_MATRIX
    )
    gate_up_new, gate_up_first_new, gate_up_second_new = adam_step(
        gate_up_weight, shard_gate_up * factor, gate_up_first, gate_up_second, RATE_MATRIX, DECAY_MATRIX
    )
    down_new, down_first_new, down_second_new = adam_step(
        down_weight, shard_down * factor, down_first, down_second, RATE_MATRIX, DECAY_MATRIX
    )
    gains_new, gains_first_new, gains_second_new = adam_step(
        norm_gains, shard_gains * factor, gains_first, gains_second, RATE_GAIN, 0.0
    )
    mixer_average_new = AVERAGE_KEEP * mixer_average + (1.0 - AVERAGE_KEEP) * mixer_new
    return (
        output, input_grad, grad_norm, mixer_new, gate_up_new, down_new, gains_new,
        mixer_first_new, gate_up_first_new, down_first_new, gains_first_new,
        mixer_second_new, gate_up_second_new, down_second_new, gains_second_new, mixer_average_new,
    )


def solution(mesh):
    outer, inner = mesh.shape["dp"], mesh.shape["fsdp"]
    side = math.isqrt(outer)
    if side * side != outer:
        side = 1
    split = jax.sharding.Mesh(
        np.asarray(mesh.devices).reshape(side, outer // side, inner // 2, 2), EVERY
    )
    rows, columns, whole = P(EVERY, None), P(None, EVERY), P()
    return jax.shard_map(
        body,
        mesh=split,
        in_specs=(
            rows, rows, whole, rows, rows, rows, rows, columns,
            rows, rows, rows, columns, rows, rows, rows, columns, rows,
        ),
        out_specs=(
            rows, rows, whole, rows, rows, rows, columns, rows, rows, rows, columns,
            rows, rows, rows, columns, rows,
        ),
        check_vma=False,
    )
```

time: 1120 us -> 766 us (0.68)
  waiting for transfers between devices: 691 us -> 509 us
  matrix products: 138 us -> 0 us
  Pallas kernels: 0 us -> 78.5 us
  local copies, waits for them, and re-layouts: 105 us -> 37 us
  other arithmetic: 74.7 us -> 37.1 us
    reduce_scatter x3, waiting for transfers between devices: 557 us -> 246 us  [body(): lax.psum_scatter(v, CHIPS, scatter_dimension=0, tiled=True)]
    dot_general x19 -> x0, matrix products: 113 us -> none  [the longest x10 22.3 us: pair_sum(): jnp.einsum('kts,skd->td', tiles, values, preferred_element_type=jnp.float32)]
    all_gather x3, waiting for transfers between devices: 38.5 us -> 130 us  [body(): gather = lambda v: lax.all_gather(v, CHIPS, axis=0, tiled=True)]
    pallas_call x0 -> x5, Pallas kernels: none -> 78.5 us  [the longest x1 20.2 us: back_call(): pl.pallas_call(back_kernel, grid=(steps,), in_specs=[pl.BlockSpec(memory_...]
    unnamed x8, waiting for transfers between devices: 95.4 us -> 127 us
    unnamed x10 -> x0, matrix products: 25.3 us -> none
    reshape x4 -> x2, local copies, waits for them, and re-layouts: 24 us -> 1.32 us  [the longest x1 0.66 us: u_call(): taps.reshape(steps, per, n)]
    add x3 -> x0, other arithmetic: 22.1 us -> none  [spectral_back(): total = total + pair_term()]
  transfers between devices with their start and end apart: 7 -> 20, of which waited for: 6 -> 10; matrix products, arithmetic and copies ran while one was open for 17% -> 8% of each run, Pallas kernels for 0% -> 8%
where the time goes in v1:
time: 766 us; the launch traced here: 764 us
  waiting for transfers between devices  509 us (66%)
  blocking collectives  79.8 us (10%)
  Pallas kernels  78.5 us (10%)
  other arithmetic  37.1 us (5%)
  local copies, waits for them, and re-layouts  37 us (5%)
  between operations  19.2 us (3%)
    reduce_scatter x3, waiting for transfers between devices, body(): lax.psum_scatter(v, CHIPS, scatter_dimension=0, tiled=True)  246 us
    all_gather x3, waiting for transfers between devices, body(): gather = lambda v: lax.all_gather(v, CHIPS, axis=0, tiled=True)  130 us
    unnamed x8, waiting for transfers between devices  127 us
    all_gather x1, blocking collectives, body(): lax.all_gather(norm_gains.astype(bf), EVERY, axis=1, tiled=True).astype(f32)  43 us
    psum x1, blocking collectives, body(): grad_norm = jnp.sqrt(lax.psum(squares, EVERY))  36.8 us
    pallas_call x1, Pallas kernels, back_call(): pl.pallas_call(back_kernel, grid=(steps,), in_specs=[pl.BlockSpec(memory_...  20.2 us
    pallas_call x1, Pallas kernels, ffn_call(): pl.pallas_call(ffn_kernel, grid=(steps,), in_specs=[full, full, row, row2...  16.2 us
    pallas_call x1, Pallas kernels, mix_call(): pl.pallas_call(mix_kernel, grid=(steps,), in_specs=[pl.BlockSpec((1, widt...  15.6 us
  transfers between devices with their start and end apart: 20, of which 10 were waited for; matrix products, arithmetic and copies ran while one was open for 8% of the time, Pallas kernels for 8%

profile of v1, /device:TPU:0, one launch (start us, length us, event | category | flops | bytes accessed | tf_op | source)
XLA Modules:
  0.0 763.8 jit_solution(14204943188618563701)
XLA Ops:
  15.2 43.0 %all-gather = bf16[32,16,2]{1,2,0:T(2,128)(2,1)S(1)} all-gather(bf16[1,16,2]{1,2,0:T(2,128)(2,1)S(1)} %convert_bitcast_fusion), channel_id=1, replica_groups=mesh['d0'=2,'d1'=2,'z'=4,'core'=2] {'d0','d1','z','core'}, dimensions={0}, use_global_device_ids=true | all-gather | bytes 2112 | tf_op jit(solution)/shard_map/all_gather | solution.py:205
  61.5 12.0 %spread.1.u_ref = bf16[9,1024,768]{2,1,0:T(8,128)(2,1)} custom-call(s32[2,3]{1,0:T(2,128)} %add_select_fusion.ends_ref, f32[9,3,512]{2,1,0:T(4,128)} %reshape.74.taps_ref, bf16[2,512,256]{2,1,0:T(8,128)(2,1)} %bitcast.19), custom_call_target="tpu_custom_call" | custom-call | tf_op jit(solution)/shard_map/spread/pallas_call | solution.py:59
  73.5 41.9 %all-gather.5.cloned.1.call-done.w_ref = bf16[13824,256]{1,0:T(8,128)(2,1)} async-done(((bf16[864,256]{1,0:T(8,128)(2,1)}), bf16[13824,256]{1,0:T(8,128)(2,1)}) %all-gather.5.cloned.1.call-update) | async-done | bytes 7077904 | tf_op jit(solution)/shard_map/all_gather | solution.py:199
  115.4 15.6 %mix.1 = f32[1024,512]{1,0:T(8,128)} custom-call(f32[1,256]{1,0:T(1,128)} %constant_dynamic-slice_fusion.16.gain_ref, bf16[9,1024,768]{2,1,0:T(8,128)(2,1)} %spread.1.u_ref, bf16[13824,256]{1,0:T(8,128)(2,1)} %all-gather.5.cloned.1.call-done.w_ref), custom_call_target="tpu_custom_call" | custom-call | tf_op jit(solution)/shard_map/mix/pallas_call | solution.py:78
  140.6 1.9 maximum_select_fusion.1
  143.9 2.0 maximum_select_fusion
  147.2 25.1 %all-gather.9.cloned.1.call-done.wd_ref = bf16[1024,512]{1,0:T(8,128)(2,1)} async-done(((bf16[64,512]{1,0:T(8,128)(2,1)}), bf16[1024,512]{1,0:T(8,128)(2,1)}) %all-gather.9.cloned.1.call-update) | async-done | bytes 1048592 | tf_op jit(solution)/shard_map/all_gather | solution.py:199
  172.3 63.0 %all-gather.7.cloned.1.call-done.wg_ref.wu_ref = bf16[2048,512]{1,0:T(8,128)(2,1)} async-done(((bf16[128,512]{1,0:T(8,128)(2,1)}), bf16[2048,512]{1,0:T(8,128)(2,1)}) %all-gather.7.cloned.1.call-update) | async-done | bytes 2097168 | tf_op jit(solution)/shard_map/all_gather | solution.py:199
  235.2 16.2 %ffn.1 = (f32[1024,512]{1,0:T(8,128)}, f32[1024,512]{1,0:T(8,128)}, bf16[2,1024,512]{2,1,0:T(8,128)(2,1)}, bf16[1024,512]{1,0:T(8,128)(2,1)}) custom-call(bf16[1024,512]{1,0:T(8,128)(2,1)} %copy.91.n2_ref, bf16[1024,512]{1,0:T(8,128)(2,1)} %copy.92.back_ref, bf16[2048,512]{1,0:T(8,128)(2,1)} %all-gather.7.cloned.1.call-done.wg_ref.wu_ref, ...), custom_call_target="tpu_custom_call" | custom-call | tf_op jit(solution)/shard_map/ffn/pallas_call | solution.py:153
  252.3 3.0 copy.95
  256.8 2.6 collective-permute-done.8
  261.0 1.8 collective-permute-done.9
  264.0 14.5 %mixer_grad.1 = bf16[13824,256]{1,0:T(8,128)(2,1)} custom-call(f32[1,256]{1,0:T(1,128)} %constant_dynamic-slice_fusion.16.gain_ref, bf16[512,1024]{1,0:T(8,128)(2,1)} %bitcast.18, bf16[9,1024,768]{2,1,0:T(8,128)(2,1)} %spread.1.u_ref), custom_call_target="tpu_custom_call" | custom-call | tf_op jit(solution)/shard_map/mixer_grad/pallas_call | solution.py:92
  279.3 2.3 copy.97.g_ref
  281.6 20.2 %spread_back.1 = f32[1024,256]{1,0:T(8,128)} custom-call(s32[2,3]{1,0:T(2,128)} %add_select_fusion.ends_ref, f32[9,3,512]{2,1,0:T(4,128)} %reshape.75.taps_ref, bf16[1024,512]{1,0:T(8,128)(2,1)} %copy.97.g_ref, bf16[13824,256]{1,0:T(8,128)(2,1)} %all-gather.5.cloned.1.call-done.w_ref), custom_call_target="tpu_custom_call" | custom-call | tf_op jit(solution)/shard_map/spread_back/pallas_call | solution.py:126
  301.7 2.2 constant_dynamic-slice_fusion.4
  304.0 2.0 copy.108
  306.1 2.9 copy.93
  309.0 2.3 constant_dynamic-slice_fusion.7
  311.7 2.0 copy.107
  313.7 15.5 %reduce-scatter.11.cloned.1.call-done = bf16[64,512]{1,0:T(8,128)(2,1)} async-done(((bf16[1024,512]{1,0:T(8,128)(2,1)}), bf16[64,512]{1,0:T(8,128)(2,1)}) %reduce-scatter.11.cloned.1.call-update) | async-done | bytes 65552 | tf_op jit(solution)/shard_map/reduce_scatter | solution.py:200
  330.7 2.0 fusion.8
  334.2 78.0 %reduce-scatter.9.cloned.1.call-done = bf16[128,512]{1,0:T(8,128)(2,1)} async-done(((bf16[2048,512]{1,0:T(8,128)(2,1)}), bf16[128,512]{1,0:T(8,128)(2,1)}) %reduce-scatter.9.cloned.1.call-update) | async-done | bytes 131088 | tf_op jit(solution)/shard_map/reduce_scatter | solution.py:200
  413.8 152.4 %reduce-scatter.7.cloned.1.call-done = bf16[864,256]{1,0:T(8,128)(2,1)} async-done(((bf16[13824,256]{1,0:T(8,128)(2,1)}), bf16[864,256]{1,0:T(8,128)(2,1)}) %reduce-scatter.7.cloned.1.call-update) | async-done | bytes 442384 | tf_op jit(solution)/shard_map/reduce_scatter | solution.py:200
  568.5 3.4 fusion.7
  571.9 2.6 copy.101
  574.5 126.8 %reduce-scatter.13.cloned.1.call-done = f32[16,2]{1,0:T(8,128)} async-done(((f32[512,2]{1,0:T(8,128)}), f32[16,2]{1,0:T(8,128)}) %reduce-scatter.13.cloned.1.call-update) | async-done | bytes 144
  704.4 2.0 multiply_reduce_fusion.3
  710.1 36.8 %psum.7 = f32[]{:T(128)} all-reduce(f32[]{:T(128)S(6)} %add.173), channel_id=1, replica_groups=mesh['d0'=2,'d1'=2,'z'=4,'core'=2] {'d0','d1','z','core'}, use_global_device_ids=true, to_apply=%region_15.16 | all-reduce | flops 1 | bytes 8 | tf_op jit(solution)/shard_map/psum | solution.py:260
  748.3 1.8 multiply_subtract_fusion.2
  750.1 2.1 multiply_subtract_fusion.1
  752.3 3.6 multiply_add_fusion.1
  (149 shorter events, 41.2 us)
Async XLA Ops:
  7.2 108.2 %all-gather.5.cloned.1.call-start = ((), (), s32[]{:S(2)}) async-start(), calls=%async_computation.4 | async-start | bytes 7520256 | tf_op jit(solution)/shard_map/all_gather | solution.py:199
  7.3 5.3 copy-start.10
  8.6 1.6 collective-permute-start.2
  11.2 161.1 %all-gather.9.cloned.1.call-start = ((), (), s32[]{:S(2)}) async-start(), calls=%async_computation.6 | async-start | bytes 1114112 | tf_op jit(solution)/shard_map/all_gather | solution.py:199
  12.0 223.3 %all-gather.7.cloned.1.call-start = ((), (), s32[]{:S(2)}) async-start(), calls=%async_computation.5 | async-start | bytes 2228224 | tf_op jit(solution)/shard_map/all_gather | solution.py:199
  12.1 1.7 collective-permute-start.6
  13.1 47.3 %collective-permute-start.1 = (bf16[512,256]{0,1:T(8,128)(2,1)S(1)}, bf16[512,256]{0,1:T(8,128)(2,1)S(1)}, u32[]{:S(2)}, u32[]{:S(2)}) collective-permute-start(bf16[512,256]{0,1:T(8,128)(2,1)S(1)} %get-tuple-element.117), channel_id=1, source_target_pairs={{0,1},{1,0},{2,3},{3,2},{4,5},{5,4},{6,7},{7,6},{8,9},{9,8},{10,11... | collective-permute-start | bytes 786440 | tf_op jit(solution)/shard_map/ppermute | solution.py:168
  13.5 46.3 %collective-permute-start = (s32[1,3]{1,0:T(1,128)S(1)}, s32[1,3]{1,0:T(1,128)S(1)}, u32[]{:S(2)}, u32[]{:S(2)}) collective-permute-start(s32[1,3]{1,0:T(1,128)S(1)} %reduce_window_sum.11), channel_id=1, source_target_pairs={{0,1},{1,0},{2,3},{3,2},{4,5},{5,4},{6,7},{7,6},{8,9},{9,8},{10,11... | collective-permute-start | bytes 44 | tf_op jit(solution)/shard_map/ppermute | solution.py:168
  14.6 314.6 %reduce-scatter.11.cloned.1.call-start = ((), (), s32[]{:S(2)}) async-start(), calls=%async_computation.9 | async-start | bytes 1114112 | tf_op jit(solution)/shard_map/reduce_scatter | solution.py:200
  134.0 4.2 collective-permute-start.3
  136.5 124.0 %copy-start.18 = (pred[512]{0:T(512)(128)(4,1)}, pred[512]{0:T(512)(128)(4,1)S(1)}, u32[]{:S(2)}) copy-start(pred[512]{0:T(512)(128)(4,1)S(1)} %iota_compare_fusion.1) | copy-start | bytes 1540
  137.4 3.3 collective-permute-start.5
  140.6 3.3 collective-permute-start.4
  251.5 160.7 %reduce-scatter.9.cloned.1.call-start = ((), (), s32[]{:S(2)}) async-start(), calls=%async_computation.8 | async-start | bytes 2228224 | tf_op jit(solution)/shard_map/reduce_scatter | solution.py:200
  252.1 314.2 %reduce-scatter.7.cloned.1.call-start = ((), (), s32[]{:S(2)}) async-start(), calls=%async_computation.7 | async-start | bytes 7520256 | tf_op jit(solution)/shard_map/reduce_scatter | solution.py:200
  256.7 2.7 collective-permute-start.8
  260.8 2.0 collective-permute-start.9
  278.6 422.8 %reduce-scatter.13.cloned.1.call-start = ((), (), s32[]{:S(2)}) async-start(), calls=%async_computation.10 | async-start | bytes 270336
  306.0 24.7 %collective-permute-start.10 = (f32[512,256]{0,1:T(8,128)}, f32[512,256]{0,1:T(8,128)}, u32[]{:S(2)}, u32[]{:S(2)}) collective-permute-start(f32[512,256]{0,1:T(8,128)} %copy.108), channel_id=1, source_target_pairs={{0,1},{1,0},{2,3},{3,2},{4,5},{5,4},{6,7},{7,6},{8,9},{9,8},{10,11... | collective-permute-start | bytes 1572872 | tf_op jit(solution)/shard_map/ppermute | solution.py:168
  309.0 23.7 %copy-start.17 = (f32[512]{0:T(512)S(1)}, f32[512]{0:T(512)}, u32[]{:S(2)}) copy-start(f32[512]{0:T(512)} %get-tuple-element.88) | copy-start | bytes 6148
  311.3 257.2 %collective-permute-start.7 = (f32[512,512]{0,1:T(8,128)}, f32[512,512]{0,1:T(8,128)}, u32[]{:S(2)}, u32[]{:S(2)}) collective-permute-start(f32[512,512]{0,1:T(8,128)} %constant_dynamic-slice_fusion.7), channel_id=1, source_target_pairs={{0,1},{1,0},{2,3},{3,2},{4,5},{5,4},{6,7},{7,6},{8,9},{9,8},{10,11... | collective-permute-start | bytes 3145736 | tf_op jit(solution)/shard_map/ppermute | solution.py:168
  413.8 288.9 %collective-permute-start.12 = (f32[64,512]{1,0:T(8,128)}, f32[64,512]{1,0:T(8,128)}, u32[]{:S(2)}, u32[]{:S(2)}) collective-permute-start(f32[64,512]{1,0:T(8,128)} %get-tuple-element.120), channel_id=1, source_target_pairs={{0,1},{1,0},{2,3},{3,2},{4,5},{5,4},{6,7},{7,6},{8,9},{9,8},{10,11... | collective-permute-start | bytes 393224 | tf_op jit(solution)/shard_map/ppermute | solution.py:168
  568.5 135.9 %collective-permute-start.11 = (f32[432,256]{1,0:T(8,128)}, f32[432,256]{1,0:T(8,128)}, u32[]{:S(2)}, u32[]{:S(2)}) collective-permute-start(f32[432,256]{1,0:T(8,128)} %get-tuple-element.114), channel_id=1, source_target_pairs={{0,1},{1,0},{2,3},{3,2},{4,5},{5,4},{6,7},{7,6},{8,9},{9,8},{10,11... | collective-permute-start | bytes 1327112 | tf_op jit(solution)/shard_map/ppermute | solution.py:168
  571.9 132.5 %copy-start.3 = (f32[432,256]{1,0:T(8,128)S(1)}, f32[432,256]{1,0:T(8,128)}, u32[]{:S(2)}) copy-start(f32[432,256]{1,0:T(8,128)} %get-tuple-element.115) | copy-start | bytes 1327108
  571.9 137.3 %copy-start.5 = (bf16[512,512]{0,1:T(8,128)(2,1)S(1)}, bf16[512,512]{0,1:T(8,128)(2,1)}, u32[]{:S(2)}) copy-start(bf16[512,512]{0,1:T(8,128)(2,1)} %get-tuple-element.111) | copy-start | bytes 1572868
  571.9 175.8 %copy-start.20 = (f32[2,16]{1,0:T(2,128)S(1)}, f32[2,16]{1,0:T(2,128)}, u32[]{:S(2)}) copy-start(f32[2,16]{1,0:T(2,128)} %param.24) | copy-start | bytes 388
  571.9 175.8 %copy-start.21 = (f32[2,16]{1,0:T(2,128)S(1)}, f32[2,16]{1,0:T(2,128)}, u32[]{:S(2)}) copy-start(f32[2,16]{1,0:T(2,128)} %param.28) | copy-start | bytes 388
  571.9 175.8 %copy-start.22 = (f32[2,16]{1,0:T(2,128)S(1)}, f32[2,16]{1,0:T(2,128)}, u32[]{:S(2)}) copy-start(f32[2,16]{1,0:T(2,128)} %param.32) | copy-start | bytes 388
  571.9 176.4 %copy-start.12 = (f32[64,512]{1,0:T(8,128)S(1)}, f32[64,512]{1,0:T(8,128)}, u32[]{:S(2)}) copy-start(f32[64,512]{1,0:T(8,128)} %param.23) | copy-start | bytes 393220
  571.9 178.2 %copy-start.13 = (f32[128,512]{1,0:T(8,128)S(1)}, f32[128,512]{1,0:T(8,128)}, u32[]{:S(2)}) copy-start(f32[128,512]{1,0:T(8,128)} %param.26) | copy-start | bytes 786436
  706.4 45.9 %copy-start.4 = (f32[432,512]{1,0:T(8,128)S(1)}, f32[432,512]{1,0:T(8,128)}, u32[]{:S(2)}) copy-start(f32[432,512]{1,0:T(8,128)} %param.21) | copy-start | bytes 2654212
  706.4 45.9 %copy-start.7 = (f32[432,512]{1,0:T(8,128)S(1)}, f32[432,512]{1,0:T(8,128)}, u32[]{:S(2)}) copy-start(f32[432,512]{1,0:T(8,128)} %param.33) | copy-start | bytes 2654212
  (12 other events, 38.6 us)
Sparse Core Ops, SparseCore 0:
  11.4 104.0 all-gather.4
  118.8 53.4 all-gather.8
  175.7 59.5 all-gather.6
  251.6 77.5 reduce-scatter.10
  331.4 80.7 reduce-scatter.8
  418.3 147.9 reduce-scatter.6
  569.1 132.1 reduce-scatter.12

commit v2 on v1

v2 whole, which is shorter than its diff:
```python
import functools
import math

import jax
import jax.numpy as jnp
import numpy as np
from jax import lax
from jax.experimental import pallas as pl
from jax.experimental.pallas import tpu as pltpu
from jax.sharding import PartitionSpec as P

bf = jnp.bfloat16
f32 = jnp.float32
FILTERS = 24
AR_ORDER = 3
FF = 2048
STEP = 10
NORM_EPS = 1e-05
CLIP_LIMIT = 1.0
BETA_ONE = 0.9
BETA_TWO = 0.95
ADAM_EPS = 1e-08
RATE_MATRIX = 0.03
RATE_GAIN = 0.5
DECAY_MATRIX = 0.1
AVERAGE_KEEP = 0.9
CHIPS = ("d0", "d1", "z")
EVERY = CHIPS + ("core",)


NT = (((1,), (1,)), ((), ()))
NN = (((1,), (0,)), ((), ()))
TN = (((0,), (0,)), ((), ()))


def dot(a, b, dims=NN):
    return lax.dot_general(a, b, dims, preferred_element_type=f32)


def call(kernel, name, flops, moved, **options):
    return pl.pallas_call(
        kernel,
        name=name,
        compiler_params=pltpu.CompilerParams(vmem_limit_bytes=56 << 20),
        cost_estimate=pl.CostEstimate(flops=flops, bytes_accessed=moved, transcendentals=0),
        **options,
    )


def smem():
    return pl.BlockSpec(memory_space=pltpu.SMEM)


def anywhere():
    return pl.BlockSpec(memory_space=pl.ANY)


def segment_of(place, ends_ref, group):
    return sum((place >= ends_ref[group, j]).astype(jnp.int32) for j in range(3))


def causal_mask(ends_ref, group, n, transposed):
    down = lax.broadcasted_iota(jnp.int32, (n, 1), 0)
    along = lax.broadcasted_iota(jnp.int32, (1, n), 1)
    one, two = segment_of(down, ends_ref, group), segment_of(along, ends_ref, group)
    order = (down <= along) if transposed else (down >= along)
    return ((one == two) & (one < 3) & order).astype(f32).astype(bf)


def diagonals(row, count):
    wide = jnp.broadcast_to(row, (count, row.shape[-1]))
    return pltpu.roll(wide, 0, 1, stride=1, stride_axis=0).astype(bf)


def spread_kernel(ends_ref, taps_ref, hat_ref, u_ref, mask, table):
    n = mask.shape[1]
    q, h, w = n // 4, n // 2, hat_ref.shape[2] // 2
    per = taps_ref.shape[1]

    @pl.when(pl.program_id(0) == 0)
    def _():
        for g in range(2):
            mask[g] = causal_mask(ends_ref, g, n, False)
        table[...] = jnp.zeros_like(table)

    for j in range(per):
        strip = diagonals(taps_ref[0, j : j + 1, :], q)
        for g in range(2):
            for i in range(4):
                rows, cols = slice(i * q, (i + 1) * q), slice(0, (i + 1) * q)
                table[g, rows, cols] = strip[:, (3 - i) * q :] * mask[g, rows, cols]
            upper = dot(table[g, :h, :h], hat_ref[g, :h]).astype(bf)
            lower = dot(table[g, h:, :], hat_ref[g]).astype(bf)
            for side in range(2):
                cols = slice(side * w, (side + 1) * w)
                u_ref[side, g * n : g * n + h, j * w : (j + 1) * w] = upper[:, cols]
                u_ref[side, g * n + h : (g + 1) * n, j * w : (j + 1) * w] = lower[:, cols]


def spread_call(ends, taps, hat, per=3):
    count, n = taps.shape
    w = hat.shape[2] // 2
    return call(
        spread_kernel, "spread", 12 * 10**9, 16 * 10**6,
        grid=(count // per,),
        in_specs=[
            smem(),
            pl.BlockSpec((1, per, n), lambda i: (i, 0, 0)),
            pl.BlockSpec((2, n, 2 * w), lambda i: (0, 0, 0)),
        ],
        out_specs=pl.BlockSpec((2, 2 * n, per * w), lambda i: (0, 0, i)),
        out_shape=jax.ShapeDtypeStruct((2, 2 * n, count * w), bf),
        scratch_shapes=[pltpu.VMEM((2, n, n), bf), pltpu.VMEM((2, n, n), bf)],
    )(ends, taps.reshape(count // per, per, n), hat)


def piece_copies(where_ref, piece_refs, held, sem, columns):
    copies, at = [], 0
    for ref in piece_refs:
        blocks, rows = ref.shape[0], ref.shape[1]
        for b in range(blocks):
            start = pl.multiple_of(where_ref[at] * rows, math.gcd(rows, 512))
            copies.append(pltpu.make_async_copy(ref.at[b], held.at[pl.ds(start, rows), columns], sem.at[at]))
            at += 1
    return copies


def mix_kernel(count, width, first, where_ref, gain_ref, u_ref, *refs):
    pieces, refs = refs[:count], refs[count:]
    before, (m_ref, held, wide, sem) = refs[: 0 if first else 1], refs[0 if first else 1 :]
    w = held.shape[1]
    filters = held.shape[0] // width

    @pl.when(pl.program_id(0) == 0)
    def _():
        copies = piece_copies(where_ref, pieces, held, sem, slice(0, w))
        for c in copies:
            c.start()
        for c in copies:
            c.wait()
        for k in range(filters):
            wide[:, k * w : (k + 1) * w] = (held[k * width : (k + 1) * width].astype(f32) * gain_ref[...]).astype(bf)

    result = dot(u_ref[0], wide[...], NT)
    m_ref[...] = result if first else result + before[0][...]


def mix_call(where, gain, u, side, pieces, before=None, parts=2):
    rows, depth = u.shape[1:]
    w = gain.shape[1]
    total = sum(p.shape[0] * p.shape[1] for p in pieces)
    width = total // (depth // w)
    step = rows // parts
    out = pl.BlockSpec((step, width), lambda i: (i, 0))
    extra = () if before is None else (before,)
    return call(
        functools.partial(mix_kernel, len(pieces), width, before is None),
        "mix", 2 * rows * depth * width, 2 * (rows * depth + total * w) + 4 * rows * width,
        grid=(parts,),
        in_specs=[smem(), pl.BlockSpec((1, w), lambda i: (0, 0)), pl.BlockSpec((1, step, depth), lambda i: (side, i, 0))]
        + [anywhere() for _ in pieces] + [out for _ in extra],
        out_specs=out,
        out_shape=jax.ShapeDtypeStruct((rows, width), f32),
        scratch_shapes=[
            pltpu.VMEM((total, w), bf), pltpu.VMEM((width, depth), bf),
            pltpu.SemaphoreType.DMA((where.shape[0],)),
        ],
    )(where, gain, u, *pieces, *extra)


def grad_kernel(gain_ref, turned_ref, u_ref, o_ref):
    w, width = gain_ref.shape[1], turned_ref.shape[0]
    result = dot(turned_ref[...], u_ref[0])
    for j in range(result.shape[1] // w):
        o_ref[j * width : (j + 1) * width, :] = (result[:, j * w : (j + 1) * w] * gain_ref[...]).astype(bf)


def grad_call(gain, turned, u, side, per=9):
    rows, depth = u.shape[1:]
    w, width = gain.shape[1], turned.shape[0]
    count = depth // w
    return call(
        grad_kernel, "mixer_grad", 2 * rows * depth * width, 2 * (rows * depth + count * width * w),
        grid=(count // per,),
        in_specs=[
            pl.BlockSpec((1, w), lambda i: (0, 0)),
            pl.BlockSpec((width, rows), lambda i: (0, 0)),
            pl.BlockSpec((1, rows, per * w), lambda i: (side, 0, i)),
        ],
        out_specs=pl.BlockSpec((per * width, w), lambda i: (i, 0)),
        out_shape=jax.ShapeDtypeStruct((count * width, w), bf),
    )(gain, turned, u)


def back_kernel(count, where_ref, ends_ref, taps_ref, g_ref, *refs):
    sides, (o_ref, held, mask, low_low, low_high, high, v_low, v_high, sem) = refs[: 2 * count], refs[2 * count :]
    n = mask.shape[1]
    q, h, d = n // 4, n // 2, g_ref.shape[1]
    per = taps_ref.shape[1]
    w = held.shape[1] // 2
    step = pl.program_id(0)

    @pl.when(step == 0)
    def _():
        copies = []
        for side in range(2):
            copies += piece_copies(
                where_ref, sides[side * count : (side + 1) * count], held, sem.at[side],
                slice(side * w, (side + 1) * w),
            )
        for c in copies:
            c.start()
        for g in range(2):
            mask[g] = causal_mask(ends_ref, g, n, True)
        low_low[...] = jnp.zeros_like(low_low)
        high[...] = jnp.zeros_like(high)
        o_ref[...] = jnp.zeros_like(o_ref)
        for c in copies:
            c.wait()

    for j in range(per):
        at = pl.multiple_of((step * per + j) * d, d)
        v = dot(g_ref[...], held[pl.ds(at, d), :]).astype(bf)
        for g in range(2):
            v_low[g, j * h : (j + 1) * h] = v[g * n : g * n + h]
            v_high[g, j * h : (j + 1) * h] = v[g * n + h : (g + 1) * n]
        s = diagonals(taps_ref[0, j : j + 1, :], q)
        a = j * h
        for g in range(2):
            m = mask[g]
            low_low[g, 0:q, a : a + q] = s[:, :q] * m[0:q, 0:q]
            low_low[g, 0:q, a + q : a + h] = s[:, q : 2 * q] * m[0:q, q : 2 * q]
            low_low[g, q:h, a + q : a + h] = s[:, :q] * m[q:h, q:h]
            low_high[g, 0:q, a : a + h] = s[:, 2 * q : 4 * q] * m[0:q, h:]
            low_high[g, q:h, a : a + h] = s[:, q : 3 * q] * m[q:h, h:]
            high[g, 0:q, a : a + h] = s[:, 0 : 2 * q] * m[h : h + q, h:]
            high[g, q:h, a + q : a + h] = s[:, 0:q] * m[h + q :, h + q :]
    for g in range(2):
        o_ref[g * n : g * n + h] += dot(low_low[g], v_low[g]) + dot(low_high[g], v_high[g])
        o_ref[g * n + h : (g + 1) * n] += dot(high[g], v_high[g])


def back_call(where, ends, taps, g, sides, per=3):
    count, n = taps.shape
    rows, d = g.shape
    pieces = [p for side in sides for p in side]
    total = sum(p.shape[0] * p.shape[1] for p in sides[0])
    width = 2 * sides[0][0].shape[-1]
    scratch = lambda *s: pltpu.VMEM(s, bf)
    return call(
        functools.partial(back_kernel, len(sides[0])), "spread_back",
        2 * rows * width * (total + count * n), 2 * total * width + 10**7,
        grid=(count // per,),
        in_specs=[
            smem(), smem(), pl.BlockSpec((1, per, n), lambda i: (i, 0, 0)), pl.BlockSpec((rows, d), lambda i: (0, 0)),
        ] + [anywhere() for _ in pieces],
        out_specs=pl.BlockSpec((rows, width), lambda i: (0, 0)),
        out_shape=jax.ShapeDtypeStruct((rows, width), f32),
        scratch_shapes=[
            scratch(total, width), scratch(2, n, n), scratch(2, n // 2, per * n // 2),
            scratch(2, n // 2, per * n // 2), scratch(2, n // 2, per * n // 2),
            scratch(2, per * n // 2, width), scratch(2, per * n // 2, width),
            pltpu.SemaphoreType.DMA((2, where.shape[0])),
        ],
    )(where, ends, taps.reshape(count // per, per, n), g, *pieces)


def flat(v):
    return v.reshape(-1, v.shape[-1])


def ffn_kernel(normed_ref, back_ref, gate_ref, up_ref, down_ref, branch_ref, two_ref, grads_ref):
    normed, back = normed_ref[...], back_ref[...]
    w_gate, w_up, w_down = flat(gate_ref[...]), flat(up_ref[...]), flat(down_ref[...])
    step = pl.program_id(0)
    gate, up = dot(normed, w_gate, NT), dot(normed, w_up, NT)
    grad_act = dot(back, w_down, NT)
    sigma = 1.0 / (1.0 + jnp.exp(-gate))
    swish = gate * sigma
    act = (swish * up).astype(bf)
    grad_gate = (grad_act * up * (sigma * (1.0 + gate * (1.0 - sigma)))).astype(bf)
    grad_up = (grad_act * swish).astype(bf)
    branch = dot(act, w_down)
    two = dot(grad_gate, w_gate) + dot(grad_up, w_up)

    @pl.when(step == 0)
    def _():
        branch_ref[...] = branch
        two_ref[...] = two

    @pl.when(step > 0)
    def _():
        branch_ref[...] += branch
        two_ref[...] += two

    half = grads_ref.shape[0] // 2
    chips, units, width = gate_ref.shape
    down_chips, down_units = down_ref.shape[0], down_ref.shape[1]
    put = lambda v: v.astype(bf).reshape(chips, units, width)
    grads_ref[pl.ds(step * chips, chips), 0:units] = put(dot(grad_gate, normed, TN))
    grads_ref[pl.ds(half + step * chips, chips), 0:units] = put(dot(grad_up, normed, TN))
    grads_ref[pl.ds(step * down_chips, down_chips), units : units + down_units] = (
        dot(act, back, TN).astype(bf).reshape(down_chips, down_units, width)
    )


def ffn_call(normed, back, packed, units, chunk=256):
    rows, d = normed.shape
    chips = packed.shape[0]
    own = chunk // units
    steps = chips // 2 // own
    full = pl.BlockSpec((rows, d), lambda i: (0, 0))
    shape = jax.ShapeDtypeStruct
    return call(
        ffn_kernel, "ffn", 10**10, 10**7,
        grid=(steps,),
        in_specs=[
            full, full,
            pl.BlockSpec((own, units, d), lambda i: (i, 0, 0)),
            pl.BlockSpec((own, units, d), lambda i: (i + steps, 0, 0)),
            pl.BlockSpec((2 * own, units // 2, d), lambda i: (i, 2, 0)),
        ],
        out_specs=[full, full, pl.BlockSpec((chips, units + units // 2, d), lambda i: (0, 0, 0))],
        out_shape=[shape((rows, d), f32), shape((rows, d), f32), shape((chips, units + units // 2, d), bf)],
    )(normed, back, packed, packed, packed)


def adam_step(weight, grad, first, second, rate, decay):
    first_new = BETA_ONE * first + (1.0 - BETA_ONE) * grad
    second_new = BETA_TWO * second + (1.0 - BETA_TWO) * grad * grad
    corr_one = 1.0 - BETA_ONE**STEP
    corr_two = 1.0 - BETA_TWO**STEP
    update = first_new / corr_one / (jnp.sqrt(second_new / corr_two) + ADAM_EPS)
    return (weight - rate * (update + decay * weight), first_new, second_new)


def flip(v, axis, bits=1):
    size = lax.axis_size(axis)
    return lax.ppermute(v, axis, [(i, i ^ bits) for i in range(size)])


def swap(v):
    return flip(v, "core")


def join(mine, other, core, axis=0):
    return jnp.where(
        core == 0,
        jnp.concatenate([mine, other], axis=axis),
        jnp.concatenate([other, mine], axis=axis),
    )


def part(v, index, axis=0):
    size = v.shape[axis] // 2
    return lax.dynamic_slice_in_dim(v, index * size, size, axis)


def trade(v, core, axis=0):
    return join(part(v, core, axis), swap(part(v, 1 - core, axis)), core)


def add_trade(v, core):
    return part(v, core) + swap(part(v, 1 - core))


class Whole:
    def __init__(self):
        self.chips = lax.axis_size("d0") * lax.axis_size("d1") * lax.axis_size("z")

    def gather(self, block):
        return [lax.all_gather(block, CHIPS, axis=0, tiled=True)[None]]

    def where(self):
        return jnp.zeros((1,), jnp.int32)

    def scatter(self, grad):
        return lax.psum_scatter(grad, CHIPS, scatter_dimension=0, tiled=True).astype(f32)

    def total(self, v):
        return lax.psum(v, EVERY)


class Cube(Whole):
    def __init__(self):
        super().__init__()
        self.size = lax.axis_size("z")
        self.y, self.x, self.z = (lax.axis_index(a) for a in CHIPS)

    def gather(self, block):
        line = jnp.stack([block] + [flip(block, "z", s) for s in range(1, self.size)])
        half = self.size // 2
        from_x, from_y = flip(line, "d1"), flip(line, "d0")
        return [line, from_x, from_y, flip(from_y[:half], "d1"), flip(from_x[half:], "d0")]

    def where(self):
        places = []
        for dy, dx in ((0, 0), (0, 1), (1, 0), (1, 1)):
            for s in range(self.size):
                places.append((((self.y ^ dy) * 2 + (self.x ^ dx)) * self.size) + (self.z ^ s))
        return jnp.stack(places).astype(jnp.int32)

    def scatter(self, grad):
        rows = grad.shape[0] // self.chips
        blocks = grad.reshape(2, 2, self.size, rows, grad.shape[1])
        half = self.size // 2

        def pick(dy, dx):
            return lax.dynamic_slice(blocks, (self.y ^ dy, self.x ^ dx, 0, 0, 0), (1, 1) + blocks.shape[2:])[0, 0]

        far, to_x, to_y, own = pick(1, 1), pick(0, 1), pick(1, 0), pick(0, 0)
        by_x, by_y = flip(far[:half], "d1"), flip(far[half:], "d0")
        low = lambda v: v.astype(bf)
        wide = lambda v: v.astype(f32)
        to_y = jnp.concatenate([low(wide(to_y[:half]) + wide(by_x)), to_y[half:]])
        to_x = jnp.concatenate([to_x[:half], low(wide(to_x[half:]) + wide(by_y))])
        line = wide(own) + wide(flip(to_x, "d1")) + wide(flip(to_y, "d0"))
        at = lambda s: lax.dynamic_index_in_dim(line, self.z ^ s, 0, keepdims=False)
        result = at(0)
        for s in range(1, self.size):
            result = result + wide(flip(low(at(s)), "z", s))
        return result

    def total(self, v):
        for axis, bits in (("core", 1), ("d1", 1), ("d0", 1)):
            v = v + flip(v, axis, bits)
        bits = 1
        while bits < self.size:
            v = v + flip(v, "z", bits)
            bits *= 2
        return v


def body(
    inputs, lengths, filters, cotangent, mixer_weight, gate_up_weight, down_weight, norm_gains,
    mixer_first, gate_up_first, down_first, gains_first,
    mixer_second, gate_up_second, down_second, gains_second, mixer_average,
):
    slots, width = inputs.shape
    core = lax.axis_index("core")
    depth = lax.axis_size("z")
    cube = lax.axis_size("d0") == 2 and lax.axis_size("d1") == 2 and depth & (depth - 1) == 0 and depth > 1
    links = Cube() if cube else Whole()
    chips = links.chips
    units = gate_up_weight.shape[0]
    own_gains = norm_gains.shape[1]
    spot = (lax.axis_index("d0") * lax.axis_size("d1") + lax.axis_index("d1")) * depth + lax.axis_index("z")

    mixer_block = trade(mixer_weight.astype(bf), core, 1)
    quarter = mixer_block.shape[1] // 2
    sides = [links.gather(mixer_block[:, s * quarter : (s + 1) * quarter]) for s in range(2)]
    gains_low = norm_gains.astype(bf)
    gains_row = join(gains_low, swap(gains_low), core, 1)
    gains_row = jnp.pad(gains_row, ((0, 14), (0, width - 2 * own_gains)))
    block = jnp.concatenate([trade(gate_up_weight.astype(bf), core), down_weight.astype(bf), gains_row])
    packed = lax.all_gather(block, CHIPS, axis=0, tiled=False)
    gains = packed[:, units + units // 2 :, : 2 * own_gains][:, :2]
    gains = gains.transpose(1, 0, 2).reshape(2, width).astype(f32)
    groups = 2 * FF // 256
    if chips != groups:
        gate_up_all = packed[:, :units].reshape(groups, -1, width)
        down_all = packed[:, units : units + units // 2].reshape(groups, -1, width)
        packed = jnp.concatenate([gate_up_all, down_all], axis=1)

    ends = jnp.cumsum(lengths, axis=-1).astype(jnp.int32)
    ends_both = join(ends, swap(ends), core)
    place = jnp.arange(slots, dtype=jnp.int32)
    live = place < ends[0, -1]
    back = jnp.where(live[:, None], cotangent, jnp.zeros((), bf))
    back_both = join(back, swap(back), core)
    taps = jnp.concatenate([filters.astype(f32), jnp.eye(AR_ORDER, slots, dtype=f32)])
    taps_turned = jnp.roll(taps[:, ::-1], 1 - slots // 4, axis=1)

    source = inputs.astype(f32)
    scale_one = lax.rsqrt(jnp.mean(source * source, axis=-1, keepdims=True) + NORM_EPS)
    hat_one = source * scale_one
    hat_both = trade(hat_one.astype(bf), core, 1).reshape(2, slots, width // 2)
    spread = spread_call(ends_both, taps_turned, hat_both)
    gain_half = part(gains[0:1], core, 1)
    gain_sides = [gain_half[:, s * quarter : (s + 1) * quarter] for s in range(2)]
    where = links.where()
    mixed = mix_call(where, gain_sides[0], spread, 0, sides[0])
    mixed = mix_call(where, gain_sides[1], spread, 1, sides[1], mixed)
    mixed = add_trade(mixed, core)

    hidden = source + mixed
    scale_two = lax.rsqrt(jnp.mean(hidden * hidden, axis=-1, keepdims=True) + NORM_EPS)
    hat_two = hidden * scale_two
    normed_two = (hat_two * gains[1]).astype(bf)
    normed_both = join(normed_two, swap(normed_two), core)
    branch, grad_two, grad_ffn = ffn_call(normed_both, back_both, packed, 2 * FF // groups // 2)
    if chips == groups:
        shard_ffn = lax.psum_scatter(flat(grad_ffn), CHIPS, scatter_dimension=0, tiled=True).astype(f32)
        shard_gate_up, shard_down = shard_ffn[:units], shard_ffn[units:]
    else:
        wide = 2 * FF // groups // 2
        shard_gate_up = Whole().scatter(flat(grad_ffn[:, :wide]))
        shard_down = Whole().scatter(flat(grad_ffn[:, wide:]))
    shard_gate_up = trade(shard_gate_up, core)

    grad_two = add_trade(grad_two, core)
    weighted_two = grad_two * gains[1]
    grad_hidden = back.astype(f32) + scale_two * (
        weighted_two - hat_two * jnp.mean(weighted_two * hat_two, axis=-1, keepdims=True)
    )
    grad_low = grad_hidden.astype(bf)
    grad_both = join(grad_low, swap(grad_low), core)
    turned = grad_both.T
    pairs = [links.scatter(grad_call(gain_sides[s], turned, spread, s)) for s in range(2)]
    pair = jnp.concatenate(pairs, axis=1)
    shard_mixer = join(part(pair, core), swap(part(pair, 1 - core)), core, 1)

    output = (hidden + add_trade(branch, core)).astype(bf)
    grad_half = back_call(where, ends_both, taps, grad_both, sides)
    grad_one = join(part(grad_half, core), swap(part(grad_half, 1 - core)), core, 1)
    weighted_one = grad_one * gains[0]
    input_grad = grad_hidden + scale_one * (
        weighted_one - hat_one * jnp.mean(weighted_one * hat_one, axis=-1, keepdims=True)
    )
    grad_gains = jnp.stack([jnp.sum(grad_one * hat_one, axis=0), jnp.sum(grad_two * hat_two, axis=0)])
    grad_gains = links.total(grad_gains)
    shard_gains = lax.dynamic_slice_in_dim(grad_gains, (spot * 2 + core) * own_gains, own_gains, 1)

    squares = (
        jnp.sum(shard_mixer * shard_mixer)
        + jnp.sum(shard_gate_up * shard_gate_up)
        + jnp.sum(shard_down * shard_down)
        + jnp.sum(shard_gains * shard_gains)
    )
    grad_norm = jnp.sqrt(links.total(squares))
    factor = CLIP_LIMIT / jnp.maximum(grad_norm, CLIP_LIMIT)
    mixer_new, mixer_first_new, mixer_second_new = adam_step(
        mixer_weight, shard_mixer * factor, mixer_first, mixer_second, RATE_MATRIX, DECAY_MATRIX
    )
    gate_up_new, gate_up_first_new, gate_up_second_new = adam_step(
        gate_up_weight, shard_gate_up * factor, gate_up_first, gate_up_second, RATE_MATRIX, DECAY_MATRIX
    )
    down_new, down_first_new, down_second_new = adam_step(
        down_weight, shard_down * factor, down_first, down_second, RATE_MATRIX, DECAY_MATRIX
    )
    gains_new, gains_first_new, gains_second_new = adam_step(
        norm_gains, shard_gains * factor, gains_first, gains_second, RATE_GAIN, 0.0
    )
    mixer_average_new = AVERAGE_KEEP * mixer_average + (1.0 - AVERAGE_KEEP) * mixer_new
    return (
        output, input_grad, grad_norm, mixer_new, gate_up_new, down_new, gains_new,
        mixer_first_new, gate_up_first_new, down_first_new, gains_first_new,
        mixer_second_new, gate_up_second_new, down_second_new, gains_second_new, mixer_average_new,
    )


def solution(mesh):
    outer, inner = mesh.shape["dp"], mesh.shape["fsdp"]
    side = math.isqrt(outer)
    if side * side != outer:
        side = 1
    split = jax.sharding.Mesh(
        np.asarray(mesh.devices).reshape(side, outer // side, inner // 2, 2), EVERY
    )
    rows, columns, whole = P(EVERY, None), P(None, EVERY), P()
    return jax.shard_map(
        body,
        mesh=split,
        in_specs=(
            rows, rows, whole, rows, rows, rows, rows, columns,
            rows, rows, rows, columns, rows, rows, rows, columns, rows,
        ),
        out_specs=(
            rows, rows, whole, rows, rows, rows, columns, rows, rows, rows, columns,
            rows, rows, rows, columns, rows,
        ),
        check_vma=False,
    )
```

time: 766 us -> 411 us (0.54)
  waiting for transfers between devices: 509 us -> 157 us
  blocking collectives: 79.8 us -> 0 us
  starting transfers between devices: 3.3 us -> 66.2 us
  Pallas kernels: 78.5 us -> 89.9 us
    reduce_scatter x3 -> x1, waiting for transfers between devices: 246 us -> 0.01 us  [body(): lax.psum_scatter(flat(grad_ffn), CHIPS, scatter_dimension=0, tiled=True)]
    unnamed x8 -> x2, waiting for transfers between devices: 127 us -> 0.03 us
    ppermute x13 -> x52, waiting for transfers between devices: 5.55 us -> 128 us  [flip(): return lax.ppermute(v, axis, [(i, i ^ bits) for i in range(size)])]
    all_gather x3 -> x1, waiting for transfers between devices: 130 us -> 29.6 us  [body(): packed = lax.all_gather(block, CHIPS, axis=0, tiled=False)]
    ppermute x13 -> x52, starting transfers between devices: 2.83 us -> 66.1 us  [flip(): return lax.ppermute(v, axis, [(i, i ^ bits) for i in range(size)])]
    all_gather x1 -> x0, blocking collectives: 43 us -> none  [body(): lax.all_gather(norm_gains.astype(bf), EVERY, axis=1, tiled=True).astype(f32)]
    psum x1 -> x0, blocking collectives: 36.8 us -> none  [body(): grad_norm = jnp.sqrt(lax.psum(squares, EVERY))]
    pallas_call x5 -> x7, Pallas kernels: 78.5 us -> 89.9 us  [the longest x1 22.9 us: back_call(): call(functools.partial(back_kernel, len(sides[0])), 'spread_back', 2 * ro...]
  transfers between devices with their start and end apart: 20 -> 54, of which waited for: 10 -> 24; matrix products, arithmetic and copies ran while one was open for 8% -> 12% of each run, Pallas kernels for 8% -> 15%
where the time goes in v2:
time: 411 us; the launch traced here: 410 us
  waiting for transfers between devices  157 us (38%)
  Pallas kernels  89.9 us (22%)
  starting transfers between devices  66.2 us (16%)
  local copies, waits for them, and re-layouts  41.5 us (10%)
  other arithmetic  33.3 us (8%)
  between operations  21.6 us (5%)
    ppermute x52, waiting for transfers between devices, flip(): return lax.ppermute(v, axis, [(i, i ^ bits) for i in range(size)])  128 us
    ppermute x52, starting transfers between devices, flip(): return lax.ppermute(v, axis, [(i, i ^ bits) for i in range(size)])  66.1 us
    all_gather x1, waiting for transfers between devices, body(): packed = lax.all_gather(block, CHIPS, axis=0, tiled=False)  29.6 us
    pallas_call x1, Pallas kernels, back_call(): call(functools.partial(back_kernel, len(sides[0])), 'spread_back', 2 * ro...  22.9 us
    pallas_call x2, Pallas kernels, mix_call(): call(functools.partial(mix_kernel, len(pieces), width, before is None), '...  21.2 us
    pallas_call x1, Pallas kernels, ffn_call(): call(ffn_kernel, 'ffn', 10 ** 10, 10 ** 7, grid=(steps,), in_specs=[full,...  16.9 us
    pallas_call x2, Pallas kernels, grad_call(): call(grad_kernel, 'mixer_grad', 2 * rows * depth * width, 2 * (rows * dep...  16.4 us
    unnamed x70, local copies, waits for them, and re-layouts  13 us
  transfers between devices with their start and end apart: 54, of which 24 were waited for; matrix products, arithmetic and copies ran while one was open for 12% of the time, Pallas kernels for 15%

profile of v2, /device:TPU:0, one launch (start us, length us, event | category | flops | bytes accessed | tf_op | source)
XLA Modules:
  0.0 409.9 jit_solution(2350729317357145243)
XLA Ops:
  15.1 2.8 collective-permute-start.12
  19.2 2.6 collective-permute-start.13
  23.3 3.5 collective-permute-start.6
  28.2 3.7 collective-permute-start.7
  33.1 8.4 %collective-permute-done.13 = bf16[864,128]{1,0:T(8,128)(2,1)S(1)} collective-permute-done((bf16[864,128]{1,0:T(8,128)(2,1)}, bf16[864,128]{1,0:T(8,128)(2,1)S(1)}, u32[]{:S(2)}, u32[]{:S(2)}) %collective-permute-start.13) | collective-permute-done | bytes 221216 | tf_op jit(solution)/shard_map/ppermute | solution.py:339
  44.8 16.9 %collective-permute-done.6 = bf16[864,128]{1,0:T(8,128)(2,1)} collective-permute-done((bf16[864,128]{1,0:T(8,128)(2,1)}, bf16[864,128]{1,0:T(8,128)(2,1)}, u32[]{:S(2)}, u32[]{:S(2)}) %collective-permute-start.6) | collective-permute-done | bytes 221216 | tf_op jit(solution)/shard_map/ppermute | solution.py:339
  66.0 12.6 %spread.1.u_ref = bf16[2,1024,3456]{2,1,0:T(8,128)(2,1)} custom-call(s32[2,3]{1,0:T(2,128)} %add_select_fusion.ends_ref, f32[9,3,512]{2,1,0:T(4,128)} %reshape.116.taps_ref, bf16[2,512,256]{2,1,0:T(8,128)(2,1)} %bitcast.114), custom_call_target="tpu_custom_call" | custom-call | flops 12000000000 | bytes 16000000 | tf_op jit(solution)/shard_map/spread/pallas_call | solution.py:103
  81.4 4.2 %collective-permute-done.9.refs_2_.refs_7_ = bf16[4,864,128]{2,1,0:T(8,128)(2,1)S(1)} collective-permute-done((bf16[4,864,128]{2,1,0:T(8,128)(2,1)S(1)}, bf16[4,864,128]{2,1,0:T(8,128)(2,1)S(1)}, u32[]{:S(2)}, u32[]{:S(2)}) %collective-permute-start.9) | collective-permute-done | bytes 884768 | tf_op jit(solution)/shard_map/ppermute | solution.py:339
  91.4 29.6 %all-gather.3.cloned.1.call-done = bf16[3328,512]{1,0:T(8,128)(2,1)} async-done(((bf16[208,512]{1,0:T(8,128)(2,1)}), bf16[3328,512]{1,0:T(8,128)(2,1)}) %all-gather.3.cloned.1.call-update) | async-done | bytes 3407888 | tf_op jit(solution)/shard_map/all_gather | solution.py:456
  122.5 10.3 %mix.2.refs_5_ = f32[1024,512]{1,0:T(8,128)} custom-call(s32[16]{0:T(128)} %stack.106.where_ref, f32[1,128]{1,0:T(1,128)} %get-tuple-element.101.gain_ref, bf16[2,1024,3456]{2,1,0:T(8,128)(2,1)} %spread.1.u_ref, bf16[4,864,128]{2,1,0:T(8,128)(2,1)} %copy-done.9, bf16[4,864,128]{2,1,0:T(8,128)(2,1)} %copy-done.16, bf16[4,864,128]{2,1,0:T(8,128)(2,1)} %copy-done.15, ...), custom_call_target="tpu_custom_call" | custom-call | flops 3623878656 | bytes 12713984 | tf_op jit(solution)/shard_map/mix/pallas_call | solution.py:156
  132.8 10.9 %mix.3 = f32[1024,512]{1,0:T(8,128)} custom-call(s32[16]{0:T(128)} %stack.106.where_ref, f32[1,128]{1,0:T(1,128)} %get-tuple-element.102.gain_ref, bf16[2,1024,3456]{2,1,0:T(8,128)(2,1)} %spread.1.u_ref, bf16[4,864,128]{2,1,0:T(8,128)(2,1)} %copy-done.10, bf16[4,864,128]{2,1,0:T(8,128)(2,1)} %copy-done.18, bf16[4,864,128]{2,1,0:T(8,128)(2,1)} %copy-done.17, ...), custom_call_target="tpu_custom_call" | custom-call | flops 3623878656 | bytes 12713984 | tf_op jit(solution)/shard_map/mix/pallas_call | solution.py:156
  160.0 16.9 %ffn.1 = (f32[1024,512]{1,0:T(8,128)}, f32[1024,512]{1,0:T(8,128)}, bf16[16,192,512]{2,1,0:T(8,128)(2,1)}) custom-call(bf16[1024,512]{1,0:T(8,128)(2,1)} %copy.38.normed_ref, bf16[1024,512]{1,0:T(8,128)(2,1)} %copy.39.back_ref, bf16[16,208,512]{2,1,0:T(8,128)(2,1)} %bitcast.128, bf16[16,208,512]{2,1,0:T(8,128)(2,1)} %bitcast.129, bf16[16,208,512]{2,1,0:T(8,128)(2,1)} %bitcast.130), custom_call_target="tpu_custom_call" | custom-call | flops 10000000000 | bytes 10000000 | tf_op jit(solution)/shard_map/ffn/pallas_call | solution.py:314
  176.8 2.9 copy.42
  187.0 2.9 copy.40
  193.3 22.9 %spread_back.1 = f32[1024,256]{1,0:T(8,128)} custom-call(s32[16]{0:T(128)} %stack.106.where_ref, s32[2,3]{1,0:T(2,128)} %add_select_fusion.ends_ref, f32[9,3,512]{2,1,0:T(4,128)} %reshape.117.taps_ref, bf16[1024,512]{1,0:T(8,128)(2,1)} %copy.44.g_ref, bf16[4,864,128]{2,1,0:T(8,128)(2,1)} %copy-done.9, bf16[4,864,128]{2,1,0:T(8,128)(2,1)} %copy-done.16, ...), custom_call_target="tpu_custom_call" | custom-call | flops 14495514624 | bytes 17077888 | tf_op jit(solution)/shard_map/spread_back/pallas_call | solution.py:250
  221.8 8.2 %mixer_grad.3 = bf16[13824,128]{1,0:T(8,128)(2,1)} custom-call(f32[1,128]{1,0:T(1,128)} %get-tuple-element.102.gain_ref, bf16[512,1024]{1,0:T(8,128)(2,1)} %bitcast.105, bf16[2,1024,3456]{2,1,0:T(8,128)(2,1)} %spread.1.u_ref), custom_call_target="tpu_custom_call" | custom-call | flops 3623878656 | bytes 10616832 | tf_op jit(solution)/shard_map/mixer_grad/pallas_call | solution.py:182
  233.7 8.2 %mixer_grad.2 = bf16[13824,128]{1,0:T(8,128)(2,1)} custom-call(f32[1,128]{1,0:T(1,128)} %get-tuple-element.101.gain_ref, bf16[512,1024]{1,0:T(8,128)(2,1)} %bitcast.106, bf16[2,1024,3456]{2,1,0:T(8,128)(2,1)} %spread.1.u_ref), custom_call_target="tpu_custom_call" | custom-call | flops 3623878656 | bytes 10616832 | tf_op jit(solution)/shard_map/mixer_grad/pallas_call | solution.py:182
  249.2 9.3 %collective-permute-done.26 = bf16[2,864,128]{2,1,0:T(8,128)(2,1)S(1)} collective-permute-done((bf16[2,864,128]{2,1,0:T(8,128)(2,1)S(1)}, bf16[2,864,128]{2,1,0:T(8,128)(2,1)S(1)}, u32[]{:S(2)}, u32[]{:S(2)}) %collective-permute-start.26) | collective-permute-done | bytes 442400 | tf_op jit(solution)/shard_map/ppermute | solution.py:339
  264.3 37.5 %collective-permute-done.43 = f32[2,512]{1,0:T(2,128)S(1)} collective-permute-done((f32[2,512]{1,0:T(2,128)S(1)}, f32[2,512]{1,0:T(2,128)S(1)}, u32[]{:S(2)}, u32[]{:S(2)}) %collective-permute-start.43) | collective-permute-done | bytes 4128 | tf_op jit(solution)/shard_map/ppermute | solution.py:339
  302.8 2.7 collective-permute-done.44
  305.6 4.6 %collective-permute-start.45 = (f32[2,512]{1,0:T(2,128)S(1)}, f32[2,512]{1,0:T(2,128)S(1)}, u32[]{:S(2)}, u32[]{:S(2)}) collective-permute-start(f32[2,512]{1,0:T(2,128)S(1)} %add.404), channel_id=1, source_target_pairs={{0,2},{2,0},{4,6},{6,4},{1,3},{3,1},{5,7},{7,5},{8,10},{10,8},{12,... | collective-permute-start | bytes 12296 | tf_op jit(solution)/shard_map/ppermute | solution.py:339
  311.7 3.1 collective-permute-start.46
  317.2 2.5 collective-permute-start.39
  320.1 9.5 %collective-permute-done.37 = bf16[864,128]{1,0:T(8,128)(2,1)S(1)} collective-permute-done((bf16[864,128]{1,0:T(8,128)(2,1)S(1)}, bf16[864,128]{1,0:T(8,128)(2,1)S(1)}, u32[]{:S(2)}, u32[]{:S(2)}) %collective-permute-start.37) | collective-permute-done | bytes 221216 | tf_op jit(solution)/shard_map/ppermute | solution.py:339
  329.6 7.8 %collective-permute-done.38 = bf16[864,128]{1,0:T(8,128)(2,1)S(1)} collective-permute-done((bf16[864,128]{1,0:T(8,128)(2,1)S(1)}, bf16[864,128]{1,0:T(8,128)(2,1)S(1)}, u32[]{:S(2)}, u32[]{:S(2)}) %collective-permute-start.38) | collective-permute-done | bytes 221216 | tf_op jit(solution)/shard_map/ppermute | solution.py:339
  338.5 3.3 collective-permute-done.30
  341.8 14.6 %collective-permute-done.31 = bf16[864,128]{1,0:T(8,128)(2,1)S(1)} collective-permute-done((bf16[864,128]{1,0:T(8,128)(2,1)S(1)}, bf16[864,128]{1,0:T(8,128)(2,1)S(1)}, u32[]{:S(2)}, u32[]{:S(2)}) %collective-permute-start.31) | collective-permute-done | bytes 221216 | tf_op jit(solution)/shard_map/ppermute | solution.py:339
  359.2 2.6 copy.48
  373.5 2.6 collective-permute-start.48
  377.8 2.6 collective-permute-start.49
  382.2 6.3 %collective-permute-start.50 = (f32[]{:T(128)}, f32[]{:T(128)}, u32[]{:S(2)}, u32[]{:S(2)}) collective-permute-start(f32[]{:T(128)} %add.412), channel_id=1, source_target_pairs={{0,2},{2,0},{4,6},{6,4},{1,3},{3,1},{5,7},{7,5},{8,10},{10,8},{12,... | collective-permute-start | bytes 20 | tf_op jit(solution)/shard_map/ppermute | solution.py:339
  389.4 3.2 collective-permute-start.51
  (251 shorter events, 108.6 us)
Async XLA Ops:
  7.2 113.8 %all-gather.3.cloned.1.call-start = ((), (), s32[]{:S(2)}) async-start(), calls=%async_computation.2 | async-start | bytes 3620864 | tf_op jit(solution)/shard_map/all_gather | solution.py:456
  11.5 352.0 %reduce-scatter.2.cloned.1.call-start = ((), (), s32[]{:S(2)}) async-start(), calls=%async_computation.1 | async-start | bytes 3342336 | tf_op jit(solution)/shard_map/reduce_scatter | solution.py:493
  19.2 22.3 %collective-permute-start.13 = (bf16[864,128]{1,0:T(8,128)(2,1)}, bf16[864,128]{1,0:T(8,128)(2,1)S(1)}, u32[]{:S(2)}, u32[]{:S(2)}) collective-permute-start(bf16[864,128]{1,0:T(8,128)(2,1)} %get-tuple-element.92), channel_id=1, source_target_pairs={{0,4},{2,6},{4,0},{6,2},{1,5},{3,7},{5,1},{7,3},{8,12},{10,14},{12... | collective-permute-start | bytes 663560 | tf_op jit(solution)/shard_map/ppermute | solution.py:339
  21.8 19.8 %collective-permute-start.14 = (bf16[864,128]{1,0:T(8,128)(2,1)}, bf16[864,128]{1,0:T(8,128)(2,1)S(1)}, u32[]{:S(2)}, u32[]{:S(2)}) collective-permute-start(bf16[864,128]{1,0:T(8,128)(2,1)} %get-tuple-element.92), channel_id=1, source_target_pairs={{0,6},{2,4},{4,2},{6,0},{1,7},{3,5},{5,3},{7,1},{8,14},{10,12},{12... | collective-permute-start | bytes 663560 | tf_op jit(solution)/shard_map/ppermute | solution.py:339
  22.4 22.4 %collective-permute-start.5 = (bf16[864,128]{1,0:T(8,128)(2,1)}, bf16[864,128]{1,0:T(8,128)(2,1)S(1)}, u32[]{:S(2)}, u32[]{:S(2)}) collective-permute-start(bf16[864,128]{1,0:T(8,128)(2,1)} %get-tuple-element.93), channel_id=1, source_target_pairs={{0,2},{2,0},{4,6},{6,4},{1,3},{3,1},{5,7},{7,5},{8,10},{10,8},{12,... | collective-permute-start | bytes 663560 | tf_op jit(solution)/shard_map/ppermute | solution.py:339
  23.3 38.5 %collective-permute-start.6 = (bf16[864,128]{1,0:T(8,128)(2,1)}, bf16[864,128]{1,0:T(8,128)(2,1)}, u32[]{:S(2)}, u32[]{:S(2)}) collective-permute-start(bf16[864,128]{1,0:T(8,128)(2,1)} %get-tuple-element.93), channel_id=1, source_target_pairs={{0,4},{2,6},{4,0},{6,2},{1,5},{3,7},{5,1},{7,3},{8,12},{10,14},{12... | collective-permute-start | bytes 663560 | tf_op jit(solution)/shard_map/ppermute | solution.py:339
  28.2 33.5 %collective-permute-start.7 = (bf16[864,128]{1,0:T(8,128)(2,1)}, bf16[864,128]{1,0:T(8,128)(2,1)}, u32[]{:S(2)}, u32[]{:S(2)}) collective-permute-start(bf16[864,128]{1,0:T(8,128)(2,1)} %get-tuple-element.93), channel_id=1, source_target_pairs={{0,6},{2,4},{4,2},{6,0},{1,7},{3,5},{5,3},{7,1},{8,14},{10,12},{12... | collective-permute-start | bytes 663560 | tf_op jit(solution)/shard_map/ppermute | solution.py:339
  41.7 36.9 %collective-permute-start.16 = (bf16[4,864,128]{2,1,0:T(8,128)(2,1)S(1)}, bf16[4,864,128]{2,1,0:T(8,128)(2,1)S(1)}, u32[]{:S(2)}, u32[]{:S(2)}) collective-permute-start(bf16[4,864,128]{2,1,0:T(8,128)(2,1)S(1)} %pad_maximum_fusion.1.refs_0_), channel_id=1, source_target_pairs={{0,16},{16,0},{1,17},{17,1},{2,18},{18,2},{3,19},{19,3},{4,20},{20... | collective-permute-start | bytes 2654216 | tf_op jit(solution)/shard_map/ppermute | solution.py:339
  43.3 36.7 %collective-permute-start.15 = (bf16[4,864,128]{2,1,0:T(8,128)(2,1)S(1)}, bf16[4,864,128]{2,1,0:T(8,128)(2,1)S(1)}, u32[]{:S(2)}, u32[]{:S(2)}) collective-permute-start(bf16[4,864,128]{2,1,0:T(8,128)(2,1)S(1)} %pad_maximum_fusion.1.refs_0_), channel_id=1, source_target_pairs={{0,8},{8,0},{1,9},{9,1},{2,10},{10,2},{3,11},{11,3},{4,12},{12,4},... | collective-permute-start | bytes 2654216 | tf_op jit(solution)/shard_map/ppermute | solution.py:339
  62.9 22.6 %collective-permute-start.9 = (bf16[4,864,128]{2,1,0:T(8,128)(2,1)S(1)}, bf16[4,864,128]{2,1,0:T(8,128)(2,1)S(1)}, u32[]{:S(2)}, u32[]{:S(2)}) collective-permute-start(bf16[4,864,128]{2,1,0:T(8,128)(2,1)S(1)} %pad_maximum_fusion.refs_0_.refs_5_), channel_id=1, source_target_pairs={{0,16},{16,0},{1,17},{17,1},{2,18},{18,2},{3,19},{19,3},{4,20},{20... | collective-permute-start | bytes 2654216 | tf_op jit(solution)/shard_map/ppermute | solution.py:339
  64.5 23.8 %collective-permute-start.8 = (bf16[4,864,128]{2,1,0:T(8,128)(2,1)S(1)}, bf16[4,864,128]{2,1,0:T(8,128)(2,1)S(1)}, u32[]{:S(2)}, u32[]{:S(2)}) collective-permute-start(bf16[4,864,128]{2,1,0:T(8,128)(2,1)S(1)} %pad_maximum_fusion.refs_0_.refs_5_), channel_id=1, source_target_pairs={{0,8},{8,0},{1,9},{9,1},{2,10},{10,2},{3,11},{11,3},{4,12},{12,4},... | collective-permute-start | bytes 2654216 | tf_op jit(solution)/shard_map/ppermute | solution.py:339
  79.5 43.0 %collective-permute-start.17 = (bf16[2,864,128]{2,1,0:T(8,128)(2,1)}, bf16[2,864,128]{2,1,0:T(8,128)(2,1)}, u32[]{:S(2)}, u32[]{:S(2)}) collective-permute-start(bf16[2,864,128]{2,1,0:T(8,128)(2,1)} %slice.177), channel_id=1, source_target_pairs={{0,8},{8,0},{1,9},{9,1},{2,10},{10,2},{3,11},{11,3},{4,12},{12,4},... | collective-permute-start | bytes 1327112 | tf_op jit(solution)/shard_map/ppermute | solution.py:339
  80.9 41.6 %collective-permute-start.18 = (bf16[2,864,128]{2,1,0:T(8,128)(2,1)}, bf16[2,864,128]{2,1,0:T(8,128)(2,1)}, u32[]{:S(2)}, u32[]{:S(2)}) collective-permute-start(bf16[2,864,128]{2,1,0:T(8,128)(2,1)} %slice.178), channel_id=1, source_target_pairs={{0,16},{16,0},{1,17},{17,1},{2,18},{18,2},{3,19},{19,3},{4,20},{20... | collective-permute-start | bytes 1327112 | tf_op jit(solution)/shard_map/ppermute | solution.py:339
  86.4 46.4 %collective-permute-start.10 = (bf16[2,864,128]{2,1,0:T(8,128)(2,1)}, bf16[2,864,128]{2,1,0:T(8,128)(2,1)}, u32[]{:S(2)}, u32[]{:S(2)}) collective-permute-start(bf16[2,864,128]{2,1,0:T(8,128)(2,1)} %slice.174), channel_id=1, source_target_pairs={{0,8},{8,0},{1,9},{9,1},{2,10},{10,2},{3,11},{11,3},{4,12},{12,4},... | collective-permute-start | bytes 1327112 | tf_op jit(solution)/shard_map/ppermute | solution.py:339
  89.9 42.8 %collective-permute-start.11 = (bf16[2,864,128]{2,1,0:T(8,128)(2,1)}, bf16[2,864,128]{2,1,0:T(8,128)(2,1)}, u32[]{:S(2)}, u32[]{:S(2)}) collective-permute-start(bf16[2,864,128]{2,1,0:T(8,128)(2,1)} %slice.175), channel_id=1, source_target_pairs={{0,16},{16,0},{1,17},{17,1},{2,18},{18,2},{3,19},{19,3},{4,20},{20... | collective-permute-start | bytes 1327112 | tf_op jit(solution)/shard_map/ppermute | solution.py:339
  220.4 40.0 %collective-permute-start.25 = (f32[512,256]{0,1:T(8,128)}, f32[512,256]{0,1:T(8,128)S(1)}, u32[]{:S(2)}, u32[]{:S(2)}) collective-permute-start(f32[512,256]{0,1:T(8,128)} %copy.53), channel_id=1, source_target_pairs={{0,1},{1,0},{2,3},{3,2},{4,5},{5,4},{6,7},{7,6},{8,9},{9,8},{10,11... | collective-permute-start | bytes 1572872 | tf_op jit(solution)/shard_map/ppermute | solution.py:339
  231.6 14.1 %collective-permute-start.33 = (bf16[2,864,128]{2,1,0:T(8,128)(2,1)S(1)}, bf16[2,864,128]{2,1,0:T(8,128)(2,1)S(1)}, u32[]{:S(2)}, u32[]{:S(2)}) collective-permute-start(bf16[2,864,128]{2,1,0:T(8,128)(2,1)S(1)} %get-tuple-element.63), channel_id=1, source_target_pairs={{0,16},{16,0},{1,17},{17,1},{2,18},{18,2},{3,19},{19,3},{4,20},{20... | collective-permute-start | bytes 1327112 | tf_op jit(solution)/shard_map/ppermute | solution.py:339
  233.2 13.5 %collective-permute-start.35 = (bf16[2,864,128]{2,1,0:T(8,128)(2,1)S(1)}, bf16[2,864,128]{2,1,0:T(8,128)(2,1)S(1)}, u32[]{:S(2)}, u32[]{:S(2)}) collective-permute-start(bf16[2,864,128]{2,1,0:T(8,128)(2,1)S(1)} %get-tuple-element.65), channel_id=1, source_target_pairs={{0,8},{8,0},{1,9},{9,1},{2,10},{10,2},{3,11},{11,3},{4,12},{12,4},... | collective-permute-start | bytes 1327112 | tf_op jit(solution)/shard_map/ppermute | solution.py:339
  243.6 14.9 %collective-permute-start.26 = (bf16[2,864,128]{2,1,0:T(8,128)(2,1)S(1)}, bf16[2,864,128]{2,1,0:T(8,128)(2,1)S(1)}, u32[]{:S(2)}, u32[]{:S(2)}) collective-permute-start(bf16[2,864,128]{2,1,0:T(8,128)(2,1)S(1)} %get-tuple-element.69), channel_id=1, source_target_pairs={{0,16},{16,0},{1,17},{17,1},{2,18},{18,2},{3,19},{19,3},{4,20},{20... | collective-permute-start | bytes 1327112 | tf_op jit(solution)/shard_map/ppermute | solution.py:339
  245.1 15.0 %collective-permute-start.28 = (bf16[2,864,128]{2,1,0:T(8,128)(2,1)S(1)}, bf16[2,864,128]{2,1,0:T(8,128)(2,1)S(1)}, u32[]{:S(2)}, u32[]{:S(2)}) collective-permute-start(bf16[2,864,128]{2,1,0:T(8,128)(2,1)S(1)} %get-tuple-element.71), channel_id=1, source_target_pairs={{0,8},{8,0},{1,9},{9,1},{2,10},{10,2},{3,11},{11,3},{4,12},{12,4},... | collective-permute-start | bytes 1327112 | tf_op jit(solution)/shard_map/ppermute | solution.py:339
  247.0 64.7 %collective-permute-start.34 = (bf16[4,864,128]{2,1,0:T(8,128)(2,1)S(1)}, bf16[4,864,128]{2,1,0:T(8,128)(2,1)S(1)}, u32[]{:S(2)}, u32[]{:S(2)}) collective-permute-start(bf16[4,864,128]{2,1,0:T(8,128)(2,1)S(1)} %pad_maximum_fusion.4), channel_id=1, source_target_pairs={{0,8},{8,0},{1,9},{9,1},{2,10},{10,2},{3,11},{11,3},{4,12},{12,4},... | collective-permute-start | bytes 2654216 | tf_op jit(solution)/shard_map/ppermute | solution.py:339
  247.8 67.1 %collective-permute-start.36 = (bf16[4,864,128]{2,1,0:T(8,128)(2,1)S(1)}, bf16[4,864,128]{2,1,0:T(8,128)(2,1)S(1)}, u32[]{:S(2)}, u32[]{:S(2)}) collective-permute-start(bf16[4,864,128]{2,1,0:T(8,128)(2,1)S(1)} %pad_maximum_fusion.5), channel_id=1, source_target_pairs={{0,16},{16,0},{1,17},{17,1},{2,18},{18,2},{3,19},{19,3},{4,20},{20... | collective-permute-start | bytes 2654216 | tf_op jit(solution)/shard_map/ppermute | solution.py:339
  261.0 54.3 %collective-permute-start.27 = (bf16[4,864,128]{2,1,0:T(8,128)(2,1)S(1)}, bf16[4,864,128]{2,1,0:T(8,128)(2,1)S(1)}, u32[]{:S(2)}, u32[]{:S(2)}) collective-permute-start(bf16[4,864,128]{2,1,0:T(8,128)(2,1)S(1)} %pad_maximum_fusion.2), channel_id=1, source_target_pairs={{0,8},{8,0},{1,9},{9,1},{2,10},{10,2},{3,11},{11,3},{4,12},{12,4},... | collective-permute-start | bytes 2654216 | tf_op jit(solution)/shard_map/ppermute | solution.py:339
  262.1 39.8 %collective-permute-start.43 = (f32[2,512]{1,0:T(2,128)S(1)}, f32[2,512]{1,0:T(2,128)S(1)}, u32[]{:S(2)}, u32[]{:S(2)}) collective-permute-start(f32[2,512]{1,0:T(2,128)S(1)} %fusion.38), channel_id=1, source_target_pairs={{0,8},{8,0},{1,9},{9,1},{2,10},{10,2},{3,11},{11,3},{4,12},{12,4},... | collective-permute-start | bytes 12296 | tf_op jit(solution)/shard_map/ppermute | solution.py:339
  263.2 54.0 %collective-permute-start.29 = (bf16[4,864,128]{2,1,0:T(8,128)(2,1)S(1)}, bf16[4,864,128]{2,1,0:T(8,128)(2,1)S(1)}, u32[]{:S(2)}, u32[]{:S(2)}) collective-permute-start(bf16[4,864,128]{2,1,0:T(8,128)(2,1)S(1)} %pad_maximum_fusion.3), channel_id=1, source_target_pairs={{0,16},{16,0},{1,17},{17,1},{2,18},{18,2},{3,19},{19,3},{4,20},{20... | collective-permute-start | bytes 2654216 | tf_op jit(solution)/shard_map/ppermute | solution.py:339
  311.7 45.7 %collective-permute-start.22 = (f32[512,512]{0,1:T(8,128)S(1)}, f32[512,512]{0,1:T(8,128)S(1)}, u32[]{:S(2)}, u32[]{:S(2)}) collective-permute-start(f32[512,512]{0,1:T(8,128)S(1)} %constant_dynamic-slice_fusion.8), channel_id=1, source_target_pairs={{0,1},{1,0},{2,3},{3,2},{4,5},{5,4},{6,7},{7,6},{8,9},{9,8},{10,11... | collective-permute-start | bytes 3145736 | tf_op jit(solution)/shard_map/ppermute | solution.py:339
  311.7 51.1 %collective-permute-start.46 = (f32[2,512]{1,0:T(2,128)S(1)}, f32[2,512]{1,0:T(2,128)S(1)}, u32[]{:S(2)}, u32[]{:S(2)}) collective-permute-start(f32[2,512]{1,0:T(2,128)S(1)} %add.405), channel_id=1, source_target_pairs={{0,4},{2,6},{4,0},{6,2},{1,5},{3,7},{5,1},{7,3},{8,12},{10,14},{12... | collective-permute-start | bytes 12296 | tf_op jit(solution)/shard_map/ppermute | solution.py:339
  315.2 14.4 %collective-permute-start.37 = (bf16[864,128]{1,0:T(8,128)(2,1)S(1)}, bf16[864,128]{1,0:T(8,128)(2,1)S(1)}, u32[]{:S(2)}, u32[]{:S(2)}) collective-permute-start(bf16[864,128]{1,0:T(8,128)(2,1)S(1)} %get-tuple-element.76), channel_id=1, source_target_pairs={{0,2},{2,0},{4,6},{6,4},{1,3},{3,1},{5,7},{7,5},{8,10},{10,8},{12,... | collective-permute-start | bytes 663560 | tf_op jit(solution)/shard_map/ppermute | solution.py:339
  315.3 22.1 %collective-permute-start.38 = (bf16[864,128]{1,0:T(8,128)(2,1)S(1)}, bf16[864,128]{1,0:T(8,128)(2,1)S(1)}, u32[]{:S(2)}, u32[]{:S(2)}) collective-permute-start(bf16[864,128]{1,0:T(8,128)(2,1)S(1)} %get-tuple-element.78), channel_id=1, source_target_pairs={{0,4},{2,6},{4,0},{6,2},{1,5},{3,7},{5,1},{7,3},{8,12},{10,14},{12... | collective-permute-start | bytes 663560 | tf_op jit(solution)/shard_map/ppermute | solution.py:339
  317.2 20.2 %collective-permute-start.39 = (bf16[864,128]{1,0:T(8,128)(2,1)S(1)}, bf16[864,128]{1,0:T(8,128)(2,1)S(1)}, u32[]{:S(2)}, u32[]{:S(2)}) collective-permute-start(bf16[864,128]{1,0:T(8,128)(2,1)S(1)} %get-tuple-element.77), channel_id=1, source_target_pairs={{0,6},{2,4},{4,2},{6,0},{1,7},{3,5},{5,3},{7,1},{8,14},{10,12},{12... | collective-permute-start | bytes 663560 | tf_op jit(solution)/shard_map/ppermute | solution.py:339
  337.5 19.0 %collective-permute-start.31 = (bf16[864,128]{1,0:T(8,128)(2,1)S(1)}, bf16[864,128]{1,0:T(8,128)(2,1)S(1)}, u32[]{:S(2)}, u32[]{:S(2)}) collective-permute-start(bf16[864,128]{1,0:T(8,128)(2,1)S(1)} %get-tuple-element.81), channel_id=1, source_target_pairs={{0,4},{2,6},{4,0},{6,2},{1,5},{3,7},{5,1},{7,3},{8,12},{10,14},{12... | collective-permute-start | bytes 663560 | tf_op jit(solution)/shard_map/ppermute | solution.py:339
  337.5 18.9 %collective-permute-start.32 = (bf16[864,128]{1,0:T(8,128)(2,1)S(1)}, bf16[864,128]{1,0:T(8,128)(2,1)S(1)}, u32[]{:S(2)}, u32[]{:S(2)}) collective-permute-start(bf16[864,128]{1,0:T(8,128)(2,1)S(1)} %get-tuple-element.80), channel_id=1, source_target_pairs={{0,6},{2,4},{4,2},{6,0},{1,7},{3,5},{5,3},{7,1},{8,14},{10,12},{12... | collective-permute-start | bytes 663560 | tf_op jit(solution)/shard_map/ppermute | solution.py:339
  (52 other events, 661.9 us)
Sparse Core Ops, SparseCore 0:
  11.6 109.3 all-gather.2
  187.2 150.7 reduce-scatter.1

commit v3 on v1

v3 whole, which is shorter than its diff:
```python
import functools
import math

import jax
import jax.numpy as jnp
import numpy as np
from jax import lax
from jax.experimental import pallas as pl
from jax.experimental.pallas import tpu as pltpu
from jax.sharding import PartitionSpec as P

bf = jnp.bfloat16
f32 = jnp.float32
FILTERS = 24
AR_ORDER = 3
FF = 2048
STEP = 10
NORM_EPS = 1e-05
CLIP_LIMIT = 1.0
BETA_ONE = 0.9
BETA_TWO = 0.95
ADAM_EPS = 1e-08
RATE_MATRIX = 0.03
RATE_GAIN = 0.5
DECAY_MATRIX = 0.1
AVERAGE_KEEP = 0.9
CHIPS = ("d0", "d1", "z")
EVERY = CHIPS + ("core",)


NT = (((1,), (1,)), ((), ()))
NN = (((1,), (0,)), ((), ()))
TN = (((0,), (0,)), ((), ()))


def dot(a, b, dims=NN):
    return lax.dot_general(a, b, dims, preferred_element_type=f32)


class Chain:
    def __init__(self):
        self.token = None

    def call(self, kernel, name, args, in_specs, out_specs, out_shape, waits=(), through=(), **options):
        count, single = len(args), not isinstance(out_shape, (list, tuple)) and not through
        if single:
            out_specs, out_shape = [out_specs], [out_shape]
        made = len(out_shape)
        aliases = options.pop("input_output_aliases", {})
        aliases = {**aliases, **{count + i: made + i for i in range(len(through))}}
        last = tuple(through) + tuple(waits) + (() if self.token is None else (self.token,))

        def whole(*refs):
            first = count + len(last)
            kernel(*refs[:count], *refs[first : first + made], *refs[first + made + len(through) + 1 :])

        *outs, self.token = pl.pallas_call(
            whole,
            name=name,
            in_specs=list(in_specs) + [anywhere() for _ in last],
            out_specs=list(out_specs) + [anywhere() for _ in through] + [anywhere()],
            out_shape=list(out_shape) + [shaped(v.shape, v.dtype) for v in through] + [shaped((8, 128), f32)],
            input_output_aliases=aliases,
            compiler_params=pltpu.CompilerParams(vmem_limit_bytes=64 << 20),
            cost_estimate=pl.CostEstimate(flops=1, bytes_accessed=1, transcendentals=0),
            **options,
        )(*args, *last)
        return outs[0] if single else outs

    def pause(self, *waits):
        self.call(lambda: None, "pause", (), [], [], [], waits=waits)


def smem():
    return pl.BlockSpec(memory_space=pltpu.SMEM)


def anywhere():
    return pl.BlockSpec(memory_space=pl.ANY)


def fixed(*shape):
    return pl.BlockSpec(shape, lambda i: (0,) * len(shape))


NOTE = 16


def shaped(shape, dtype):
    return jax.ShapeDtypeStruct(tuple(shape), dtype)


def segment_of(place, ends_ref, group):
    return sum((place >= ends_ref[group, j]).astype(jnp.int32) for j in range(3))


def causal_mask(ends_ref, group, n, transposed):
    down = lax.broadcasted_iota(jnp.int32, (n, 1), 0)
    along = lax.broadcasted_iota(jnp.int32, (1, n), 1)
    one, two = segment_of(down, ends_ref, group), segment_of(along, ends_ref, group)
    order = (down <= along) if transposed else (down >= along)
    return ((one == two) & (one < 3) & order).astype(f32).astype(bf)


def diagonals(row, count):
    wide = jnp.broadcast_to(row, (count, row.shape[-1]))
    return pltpu.roll(wide, 0, 1, stride=1, stride_axis=0).astype(bf)


def spread_kernel(lengths_ref, came_ref, taps_ref, own_ref, other_ref, *refs):
    u_ref, mask, table, ends = refs[-4:]
    n = mask.shape[1]
    q, h, w = n // 4, n // 2, own_ref.shape[1] // 2
    per = taps_ref.shape[1]

    @pl.when(pl.program_id(0) == 0)
    def _():
        find_ends(ends, lengths_ref, came_ref)
        for g in range(2):
            mask[g] = causal_mask(ends, g, n, False)
        table[...] = jnp.zeros_like(table)

    for j in range(per):
        strip = diagonals(taps_ref[0, j : j + 1, :], q)
        for g, tokens in enumerate((own_ref, other_ref)):
            for i in range(4):
                rows, cols = slice(i * q, (i + 1) * q), slice(0, (i + 1) * q)
                table[g, rows, cols] = strip[:, (3 - i) * q :] * mask[g, rows, cols]
            upper = dot(table[g, :h, :h], tokens[:h]).astype(bf)
            lower = dot(table[g, h:, :], tokens[...]).astype(bf)
            for side in range(2):
                cols = slice(side * w, (side + 1) * w)
                u_ref[side, g * n : g * n + h, j * w : (j + 1) * w] = upper[:, cols]
                u_ref[side, g * n + h : (g + 1) * n, j * w : (j + 1) * w] = lower[:, cols]


def find_ends(ends, lengths_ref, came_ref):
    for g, ref in enumerate((lengths_ref, came_ref)):
        total = ref[0, 0]
        ends[g, 0] = total
        for j in range(1, 3):
            total = total + ref[0, j]
            ends[g, j] = total


def spread_call(chain, lengths, taps, own, other, first, steps, into=None):
    blocks, per, n = taps.shape
    w = own.shape[1] // 2
    args = [*lengths, taps, own, other]
    specs = [smem()] * 2 + [pl.BlockSpec((1, per, n), lambda i: (i + first, 0, 0)), fixed(n, 2 * w), fixed(n, 2 * w)]
    options = {}
    if into is not None:
        options = dict(input_output_aliases={len(args): 0})
        args, specs = args + [into], specs + [anywhere()]
    return chain.call(
        spread_kernel, "spread", args, specs,
        pl.BlockSpec((2, 2 * n, per * w), lambda i: (0, 0, i + first)),
        shaped((2, 2 * n, blocks * per * w), bf),
        grid=(steps,),
        scratch_shapes=[pltpu.VMEM((2, n, n), bf), pltpu.VMEM((2, n, n), bf), pltpu.SMEM((2, 3), jnp.int32)],
        **options,
    )


def run_copies(copies):
    for c in copies:
        c.start()
    for c in copies:
        c.wait()


def chip_of(spot_ref, slot, size):
    if isinstance(slot, int):
        return slot
    dy, dx, dz, fixed_z = slot
    return ((spot_ref[0] ^ dy) * 2 + (spot_ref[1] ^ dx)) * size + (dz if fixed_z else spot_ref[2] ^ dz)


def collect(spot_ref, pieces, plan, size, held, sem, columns):
    copies = []
    for at, (piece, row, rows, slot, half) in enumerate(plan):
        place = chip_of(spot_ref, slot, size)
        if half is not None:
            place = place * 2 + (spot_ref[3] ^ half)
        start = pl.multiple_of(place * rows, math.gcd(rows, 512))
        copies.append(
            pltpu.make_async_copy(pieces[piece].at[pl.ds(row, rows)], held.at[pl.ds(start, rows), columns], sem.at[at])
        )
    return copies


def mix_kernel(count, plan, notes, size, width, side, spot_ref, u_ref, *refs):
    pieces, refs = refs[:count], refs[count:]
    first = side == 0
    before, refs = refs[: 0 if first else 2], refs[0 if first else 2 :]
    if notes:
        own_ref, other_ref, gains_ref, held, wide, sem, tiles = refs
    else:
        gains_ref, own_ref, other_ref, held, wide, sem = refs
    w = held.shape[1]
    filters = held.shape[0] // width
    step = pl.program_id(0)

    @pl.when(step == 0)
    def _():
        copies = collect(spot_ref, pieces, plan, size, held, sem, slice(0, w))
        for at, (piece, row, slot) in enumerate(notes):
            copies.append(
                pltpu.make_async_copy(
                    pieces[piece].at[pl.ds(row, NOTE)], tiles.at[chip_of(spot_ref, slot, size)], sem.at[len(plan) + at]
                )
            )
        run_copies(copies)
        if notes:
            lanes = width // len(notes)
            for b in range(width // 128):
                block = jnp.zeros((NOTE, 128), f32)
                for j in range(128 // lanes):
                    tile = tiles[b * (128 // lanes) + j].astype(f32)
                    block = block + (pltpu.roll(tile, j * lanes, 1) if j else tile)
                gains_ref[:, b * 128 : (b + 1) * 128] = block
        gain = gains_ref[0:1, pl.ds(pl.multiple_of((spot_ref[3] * 2 + side) * w, w), w)]
        for k in range(filters):
            wide[:, k * w : (k + 1) * w] = (held[k * width : (k + 1) * width].astype(f32) * gain).astype(bf)

    result = dot(u_ref[0], wide[...], NT)
    for g, out in enumerate((own_ref, other_ref)):

        @pl.when(step == g)
        def _():
            out[...] = result if first else result + before[g][...]


def mix_call(chain, spot, u, side, pieces, plan, notes, gains, size, width, before=()):
    rows, depth = u.shape[1:]
    w = pieces[0].shape[-1]
    total = depth // w * width
    step = rows // 2
    out = fixed(step, width)
    note = fixed(NOTE, width)
    given = () if notes else (gains,)
    return chain.call(
        functools.partial(mix_kernel, len(pieces), plan, notes, size, width, side), "mix",
        (spot, u, *pieces, *before, *given),
        [smem(), pl.BlockSpec((1, step, depth), lambda i: (side, i, 0))] + [anywhere() for _ in pieces]
        + [out for _ in before] + [note for _ in given],
        [out, out] + [note for _ in range(1 - len(given))],
        [shaped((step, width), f32)] * 2 + [shaped((NOTE, width), f32) for _ in range(1 - len(given))],
        grid=(2,),
        scratch_shapes=[
            pltpu.VMEM((total, w), bf), pltpu.VMEM((width, depth), bf), pltpu.SemaphoreType.DMA((len(plan) + len(notes),)),
        ] + [pltpu.VMEM((len(notes), NOTE, 128), bf)] * (1 - len(given)),
    )


def hidden_kernel(source_ref, own_ref, came_ref, gain_ref, hidden_ref, normed_ref):
    hidden = source_ref[...].astype(f32) + (own_ref[...] + came_ref[...])
    scale = lax.rsqrt(jnp.mean(hidden * hidden, axis=-1, keepdims=True) + NORM_EPS)
    hidden_ref[...] = hidden
    normed_ref[...] = (hidden * scale * gain_ref[1:2]).astype(bf)


def hidden_call(chain, source, own, came, gain, parts=4):
    rows, width = source.shape
    block = pl.BlockSpec((rows // parts, width), lambda i: (i, 0))
    return chain.call(
        hidden_kernel, "hidden", (source, own, came, gain), [block, block, block, fixed(NOTE, width)],
        [block, block], [shaped((rows, width), f32), shaped((rows, width), bf)],
        grid=(parts,),
    )


def norm_back(grad, hat, scale, gain):
    weighted = grad * gain
    return scale * (weighted - hat * jnp.mean(weighted * hat, axis=-1, keepdims=True))


def add_rows(ref, values, step):
    total = jnp.sum(values, axis=0, keepdims=True)

    @pl.when(step == 0)
    def _():
        ref[...] = total

    @pl.when(step > 0)
    def _():
        ref[...] += total


def turn_kernel(lengths_ref, hidden_ref, back_ref, own_ref, came_ref, gain_ref, grad_ref, low_ref, gains_ref):
    hidden = hidden_ref[...]
    scale = lax.rsqrt(jnp.mean(hidden * hidden, axis=-1, keepdims=True) + NORM_EPS)
    hat = hidden * scale
    two = own_ref[...] + came_ref[...]
    back = live_rows(back_ref[...].astype(f32), lengths_ref, pl.program_id(0) * hidden.shape[0])
    grad = back + norm_back(two, hat, scale, gain_ref[1:2])
    grad_ref[...] = grad
    low_ref[...] = grad.astype(bf)
    add_rows(gains_ref, two * hat, pl.program_id(0))


def turn_call(chain, lengths, hidden, back, own, came, gain, parts=4):
    rows, width = hidden.shape
    block = pl.BlockSpec((rows // parts, width), lambda i: (i, 0))
    return chain.call(
        turn_kernel, "turn", (lengths, hidden, back, own, came, gain), [smem()] + [block] * 4 + [fixed(NOTE, width)],
        [block, block, fixed(1, width)],
        [shaped((rows, width), f32), shaped((rows, width), bf), shaped((1, width), f32)],
        grid=(parts,),
    )


def output_kernel(hidden_ref, own_ref, came_ref, out_ref):
    out_ref[...] = (hidden_ref[...] + (own_ref[...] + came_ref[...])).astype(bf)


def output_call(chain, hidden, own, came, parts=4):
    rows, width = hidden.shape
    block = pl.BlockSpec((rows // parts, width), lambda i: (i, 0))
    return chain.call(
        output_kernel, "output", (hidden, own, came), [block] * 3, block, shaped((rows, width), bf), grid=(parts,),
    )


def last_kernel(spot_ref, grad_ref, source_ref, own_ref, came_ref, gain_ref, out_ref, gains_ref, one):
    half = own_ref.shape[1]
    core = spot_ref[3]
    one[:, pl.ds(pl.multiple_of(core * half, half), half)] = own_ref[...]
    one[:, pl.ds(pl.multiple_of((1 - core) * half, half), half)] = came_ref[...]
    source = source_ref[...].astype(f32)
    scale = lax.rsqrt(jnp.mean(source * source, axis=-1, keepdims=True) + NORM_EPS)
    hat = source * scale
    grad = one[...]
    out_ref[...] = grad_ref[...] + norm_back(grad, hat, scale, gain_ref[0:1])
    add_rows(gains_ref, grad * hat, pl.program_id(0))


def last_call(chain, spot, grad_hidden, source, own, came, gain, waits, parts=4):
    rows, width = source.shape
    block = pl.BlockSpec((rows // parts, width), lambda i: (i, 0))
    thin = pl.BlockSpec((rows // parts, width // 2), lambda i: (i, 0))
    return chain.call(
        last_kernel, "last", (spot, grad_hidden, source, own, came, gain),
        [smem(), block, block, thin, thin, fixed(NOTE, width)],
        [block, fixed(1, width)], [shaped((rows, width), f32), shaped((1, width), f32)],
        grid=(parts,),
        scratch_shapes=[pltpu.VMEM((rows // parts, width), f32)],
        waits=waits,
    )


def grad_kernel(slots, size, side, spot_ref, gains_ref, own_ref, other_ref, u_ref, *refs):
    outs, (turned, held, sem) = refs[:-3], refs[-3:]
    n, width = own_ref.shape
    w = held.shape[1]
    per = u_ref.shape[2] // w
    step = pl.program_id(0)

    @pl.when(step == 0)
    def _():
        turned[:, :n] = own_ref[...].T
        turned[:, n:] = other_ref[...].T

    gain = gains_ref[0:1, pl.ds(pl.multiple_of((spot_ref[3] * 2 + side) * w, w), w)]
    result = dot(turned[...], u_ref[0])
    for j in range(per):
        at = pl.multiple_of((step * per + j) * width, width)
        held[pl.ds(at, width), :] = (result[:, j * w : (j + 1) * w] * gain).astype(bf)

    @pl.when(step == pl.num_programs(0) - 1)
    def _():
        rows = held.shape[0] // len(slots)
        copies, at = [], 0
        for ref in outs:
            for b in range(ref.shape[0] // rows):
                start = pl.multiple_of(chip_of(spot_ref, slots[at], size) * rows, math.gcd(rows, 512))
                copies.append(
                    pltpu.make_async_copy(held.at[pl.ds(start, rows)], ref.at[pl.ds(b * rows, rows)], sem.at[at])
                )
                at += 1
        run_copies(copies)


def grad_call(chain, spot, gains, own, other, u, side, w, blocks, slots, size, per=9):
    rows, depth = u.shape[1:]
    n, width = own.shape
    count = depth // w
    each = count * width // len(slots)
    return chain.call(
        functools.partial(grad_kernel, slots, size, side), "mixer_grad", (spot, gains, own, other, u),
        [smem(), fixed(NOTE, width), fixed(n, width), fixed(n, width), pl.BlockSpec((1, rows, per * w), lambda i: (side, 0, i))],
        [anywhere() for _ in blocks], [shaped((b * each, w), bf) for b in blocks],
        grid=(count // per,),
        scratch_shapes=[
            pltpu.VMEM((width, rows), bf), pltpu.VMEM((count * width, w), bf), pltpu.SemaphoreType.DMA((len(slots),)),
        ],
    )


def back_kernel(count, plans, size, first, spot_ref, lengths_ref, came_ref, taps_ref, own_ref, other_ref, *refs):
    sides, refs = refs[: 2 * count], refs[2 * count :]
    before, refs = refs[: 2 if first else 0], refs[2 if first else 0 :]
    own_out, other_out, held, mask, low_low, low_high, high, v_low, v_high, ends, sem = refs
    n = mask.shape[1]
    q, h, d = n // 4, n // 2, own_ref.shape[1]
    per = taps_ref.shape[1]
    w = held.shape[1] // 2
    step = pl.program_id(0)

    @pl.when(step == 0)
    def _():
        copies = []
        for side in range(2):
            copies += collect(
                spot_ref, sides[side * count : (side + 1) * count], plans[side], size, held, sem.at[side],
                slice(side * w, (side + 1) * w),
            )
        for c in copies:
            c.start()
        find_ends(ends, lengths_ref, came_ref)
        for g in range(2):
            mask[g] = causal_mask(ends, g, n, True)
        low_low[...] = jnp.zeros_like(low_low)
        high[...] = jnp.zeros_like(high)
        for g, ref in enumerate((own_out, other_out)):
            ref[...] = before[g][...] if first else jnp.zeros_like(ref)
        for c in copies:
            c.wait()

    for j in range(per):
        at = pl.multiple_of(((step + first) * per + j) * d, d)
        weight = held[pl.ds(at, d), :]
        s = diagonals(taps_ref[0, j : j + 1, :], q)
        a = j * h
        for g, grad in enumerate((own_ref, other_ref)):
            v = dot(grad[...], weight).astype(bf)
            v_low[g, a : a + h] = v[:h]
            v_high[g, a : a + h] = v[h:]
            m = mask[g]
            low_low[g, 0:q, a : a + q] = s[:, :q] * m[0:q, 0:q]
            low_low[g, 0:q, a + q : a + h] = s[:, q : 2 * q] * m[0:q, q : 2 * q]
            low_low[g, q:h, a + q : a + h] = s[:, :q] * m[q:h, q:h]
            low_high[g, 0:q, a : a + h] = s[:, 2 * q : 4 * q] * m[0:q, h:]
            low_high[g, q:h, a : a + h] = s[:, q : 3 * q] * m[q:h, h:]
            high[g, 0:q, a : a + h] = s[:, 0 : 2 * q] * m[h : h + q, h:]
            high[g, q:h, a + q : a + h] = s[:, 0:q] * m[h + q :, h + q :]
    for g, out in enumerate((own_out, other_out)):
        out[:h] += dot(low_low[g], v_low[g]) + dot(low_high[g], v_high[g])
        out[h:] += dot(high[g], v_high[g])


def back_call(chain, spot, lengths, taps, own, other, sides, plans, size, first, steps, before=()):
    blocks, per, n = taps.shape
    rows, d = own.shape
    pieces = [p for side in sides for p in side]
    total = blocks * per * d
    width = 2 * sides[0][0].shape[-1]
    scratch = lambda *s: pltpu.VMEM(s, bf)
    return chain.call(
        functools.partial(back_kernel, len(sides[0]), plans, size, first), "spread_back",
        (spot, *lengths, taps, own, other, *pieces, *before),
        [smem()] * 3 + [pl.BlockSpec((1, per, n), lambda i: (i + first, 0, 0)), fixed(rows, d), fixed(rows, d)]
        + [anywhere() for _ in pieces] + [fixed(rows, width) for _ in before],
        [fixed(rows, width)] * 2, [shaped((rows, width), f32)] * 2,
        grid=(steps,),
        scratch_shapes=[
            scratch(total, width), scratch(2, n, n), scratch(2, n // 2, per * n // 2),
            scratch(2, n // 2, per * n // 2), scratch(2, n // 2, per * n // 2),
            scratch(2, per * n // 2, width), scratch(2, per * n // 2, width),
            pltpu.SMEM((2, 3), jnp.int32), pltpu.SemaphoreType.DMA((2, len(plans[0]))),
        ],
    )


def flat(v):
    return v.reshape(-1, v.shape[-1])


def ffn_kernel(count, outs, steps, slots, size, crossed, spot_ref, lengths_ref, came_ref, *refs):
    turned = spot_ref[3] if crossed else 0
    tokens, pieces, refs = refs[:4], refs[4 : 4 + count], refs[4 + count :]
    results, grads, (held, dealt, normed, back, sem) = refs[:4], refs[4 : 4 + outs], refs[4 + outs :]
    n = tokens[0].shape[0]
    chips, units, width = held.shape[0], held.shape[1] * 2 // 3, held.shape[2]
    own, half = chips // 2 // steps, units // 2
    step = pl.program_id(0)

    @pl.when(step == 0)
    def _():
        copies, at = [], 0
        for ref in pieces:
            for b in range(ref.shape[0]):
                chip = chip_of(spot_ref, slots[at], size)
                copies.append(
                    pltpu.make_async_copy(ref.at[b, pl.ds(0, units)], held.at[chip, pl.ds(0, units)], sem.at[0, at])
                )
                copies.append(
                    pltpu.make_async_copy(
                        ref.at[b, pl.ds(units, half)], held.at[chip ^ turned, pl.ds(units, half)], sem.at[1, at]
                    )
                )
                at += 1
        for c in copies:
            c.start()
        normed[:n], normed[n:] = tokens[0][...], tokens[1][...]
        back[:n] = live_rows(tokens[2][...].astype(f32), lengths_ref).astype(bf)
        back[n:] = live_rows(tokens[3][...].astype(f32), came_ref).astype(bf)
        for c in copies:
            c.wait()

    w_gate = flat(held[pl.ds(step * own, own), 0:units])
    w_up = flat(held[pl.ds(chips // 2 + step * own, own), 0:units])
    w_down = flat(held[pl.ds(step * 2 * own, 2 * own), units : units + half])
    gate, up = dot(normed[...], w_gate, NT), dot(normed[...], w_up, NT)
    grad_act = dot(back[...], w_down, NT)
    sigma = 1.0 / (1.0 + jnp.exp(-gate))
    swish = gate * sigma
    act = (swish * up).astype(bf)
    grad_gate = (grad_act * up * (sigma * (1.0 + gate * (1.0 - sigma)))).astype(bf)
    grad_up = (grad_act * swish).astype(bf)
    branch = dot(act, w_down)
    two = dot(grad_gate, w_gate) + dot(grad_up, w_up)
    values = (branch[:n], branch[n:], two[:n], two[n:])

    @pl.when(step == 0)
    def _():
        for ref, value in zip(results, values):
            ref[...] = value

    @pl.when(step > 0)
    def _():
        for ref, value in zip(results, values):
            ref[...] += value

    put = lambda v: v.astype(bf).reshape(own, units, width)
    dealt[pl.ds(step * own, own), 0:units] = put(dot(grad_gate, normed[...], TN))
    dealt[pl.ds(chips // 2 + step * own, own), 0:units] = put(dot(grad_up, normed[...], TN))
    grad_down = dot(act, back[...], TN).astype(bf)
    for b in range(2 * own):
        dealt[(step * 2 * own + b) ^ turned, units : units + half] = grad_down[b * half : (b + 1) * half]

    @pl.when(step == steps - 1)
    def _():
        copies, at = [], 0
        for ref in grads:
            for b in range(ref.shape[0]):
                copies.append(
                    pltpu.make_async_copy(dealt.at[chip_of(spot_ref, slots[at], size)], ref.at[b], sem.at[0, at])
                )
                at += 1
        run_copies(copies)


def ffn_call(chain, spot, lengths, tokens, pieces, blocks, slots, size, crossed, chunk=256):
    n, d = tokens[0].shape
    chips, rows = len(slots), pieces[0].shape[1]
    units = rows * 2 // 3
    steps = chips // 2 * units // chunk
    return chain.call(
        functools.partial(ffn_kernel, len(pieces), len(blocks), steps, slots, size, crossed), "ffn",
        (spot, *lengths, *tokens, *pieces),
        [smem()] * 3 + [fixed(n, d)] * 4 + [anywhere() for _ in pieces],
        [fixed(n, d)] * 4 + [anywhere() for _ in blocks],
        [shaped((n, d), f32)] * 4 + [shaped((b, rows, d), bf) for b in blocks],
        grid=(steps,),
        scratch_shapes=[
            pltpu.VMEM((chips, rows, d), bf), pltpu.VMEM((chips, rows, d), bf),
            pltpu.VMEM((2 * n, d), bf), pltpu.VMEM((2 * n, d), bf), pltpu.SemaphoreType.DMA((2, chips)),
        ],
    )


def normed_kernel(spot_ref, own_ref, other_ref, own_out, other_out, full):
    half = own_out.shape[1]
    cols = pl.ds(pl.multiple_of(spot_ref[3] * half, half), half)
    for ref, out in ((own_ref, own_out), (other_ref, other_out)):
        source = ref[...].astype(f32)
        scale = lax.rsqrt(jnp.mean(source * source, axis=-1, keepdims=True) + NORM_EPS)
        full[...] = (source * scale).astype(bf)
        out[...] = full[:, cols]


def normed_call(chain, spot, own, other, parts=2):
    rows, width = own.shape
    block = pl.BlockSpec((rows // parts, width), lambda i: (i, 0))
    thin = pl.BlockSpec((rows // parts, width // 2), lambda i: (i, 0))
    return chain.call(
        normed_kernel, "normed", (spot, own, other), [smem(), block, block],
        [thin] * 2, [shaped((rows, width // 2), bf)] * 2,
        grid=(parts,), scratch_shapes=[pltpu.VMEM((rows // parts, width), bf)],
    )


def live_rows(values, lengths_ref, first=0):
    total = lengths_ref[0, 0] + lengths_ref[0, 1] + lengths_ref[0, 2]
    place = lax.broadcasted_iota(jnp.int32, (values.shape[0], 1), 0) + first
    return jnp.where(place < total, values, jnp.zeros((), values.dtype))


def pack_kernel(
    spot_ref, mixer_ref, gate_up_ref, down_ref, gains_ref, mixer_mine, mixer_theirs, gate_mine, gate_theirs, down_low, note
):
    half, units, core = mixer_mine.shape[1], gate_mine.shape[0], spot_ref[3]
    for ref, cols, rows, c in ((mixer_mine, half, units, core), (mixer_theirs, half, units, 1 - core)):
        ref[...] = mixer_ref[:, pl.ds(pl.multiple_of(c * half, half), half)].astype(bf)
    for ref, c in ((gate_mine, core), (gate_theirs, 1 - core)):
        ref[:units] = gate_up_ref[pl.ds(pl.multiple_of(c * units, units), units), :].astype(bf)
    count, own = gains_ref.shape
    note[...] = jnp.zeros_like(note)
    note[:count, :own] = gains_ref[...].astype(bf)
    gate_theirs[units:] = jnp.zeros((note.shape[0], gate_theirs.shape[1]), bf)
    gate_theirs[units:, : note.shape[1]] = note[...]
    down_low[...] = down_ref[...].astype(bf)


def pack_call(chain, spot, mixer, gate_up, down, gains):
    (rows, width), (units, _), (half, _) = mixer.shape, gate_up.shape, down.shape
    shapes = [(rows, width // 2)] * 2 + [(units // 2, width), (units // 2 + NOTE, width), (half, width), (NOTE, 128)]
    return chain.call(
        pack_kernel, "pack", (spot, mixer, gate_up, down, gains),
        [smem(), fixed(rows, width), fixed(units, width), fixed(half, width), fixed(*gains.shape)],
        [fixed(*s) for s in shapes], [shaped(s, bf) for s in shapes], grid=(1,),
    )


def block_kernel(own_gains, spot_ref, mine_ref, came_ref, note_ref, gate_ref, all_ref, copies_ref):
    rows, w = mine_ref.shape[0], all_ref.shape[1]
    mine = note_ref[...].astype(f32)
    came = gate_ref[gate_ref.shape[0] - NOTE :, :w].astype(f32)
    turned = lambda v: pltpu.roll(v, own_gains, 1)
    note = jnp.where(spot_ref[3] == 0, mine + turned(came), came + turned(mine)).astype(bf)
    at = 0
    for side in range(2):
        cols = slice(side * w, (side + 1) * w)
        all_ref[at : at + rows] = mine_ref[:, cols]
        all_ref[at + rows : at + 2 * rows] = came_ref[:, cols]
        all_ref[at + 2 * rows : at + 2 * rows + NOTE] = note
        at += 2 * rows + NOTE
    count = 2 * rows + NOTE
    for c in range(copies_ref.shape[0] // count):
        copies_ref[c * count : (c + 1) * count] = all_ref[:count]


def block_call(chain, spot, mine, came, note, gate_came, own_gains, copies, waits):
    rows, width = mine.shape
    w = width // 2
    each = 2 * rows + NOTE
    return chain.call(
        functools.partial(block_kernel, own_gains), "block", (spot, mine, came, note, gate_came),
        [smem()] + [fixed(*v.shape) for v in (mine, came, note, gate_came)],
        [fixed(2 * each, w), fixed(copies * each, w)], [shaped((2 * each, w), bf), shaped((copies * each, w), bf)],
        grid=(1,), waits=waits,
    )


def stack_kernel(count, moves, spot_ref, *refs):
    for i, a, rows, o, b in moves:
        if not isinstance(a, int):
            stride, distance, first = a
            a = pl.multiple_of((spot_ref[2] ^ distance) * stride + first, NOTE)
        refs[count + o][b : b + rows] = refs[i][pl.ds(a, rows)]


def stack_call(chain, spot, arrays, rows, moves, waits=()):
    like = {o: arrays[i] for i, _, _, o, _ in moves}
    shapes = [(r,) + like[o].shape[1:] for o, r in enumerate(rows)]
    return chain.call(
        functools.partial(stack_kernel, len(arrays), moves), "stack", (spot, *arrays),
        [smem()] + [fixed(*v.shape) for v in arrays],
        [fixed(*s) for s in shapes], [shaped(s, like[o].dtype) for o, s in enumerate(shapes)], grid=(1,), waits=waits,
    )


def corner_kernel(cut, extra, x_ref, y_ref, to_x_ref, to_y_ref):
    rows = x_ref.shape[0]
    to_x_ref[:cut] = y_ref[:cut]
    if extra:
        to_x_ref[cut:] = y_ref[rows - extra :]
    to_y_ref[...] = x_ref[cut : rows - extra]


def corner_call(chain, from_x, from_y, extra):
    total, width = from_x.shape
    cut = (total - extra) // 2
    shapes = [(cut + extra, width), (cut, width)]
    return chain.call(
        functools.partial(corner_kernel, cut, extra), "corner", (from_x, from_y), [fixed(total, width)] * 2,
        [fixed(*s) for s in shapes], [shaped(s, bf) for s in shapes], grid=(1,),
    )


def near_kernel(to_x_ref, to_y_ref, by_x_ref, by_y_ref, new_x_ref, new_y_ref):
    new_x_ref[...] = (to_x_ref[...].astype(f32) + by_y_ref[...].astype(f32)).astype(bf)
    new_y_ref[...] = (to_y_ref[...].astype(f32) + by_x_ref[...].astype(f32)).astype(bf)


def near_call(chain, to_x, to_y, by_x, by_y, parts=2, **options):
    rows, width = by_x.shape
    block = (rows // parts, width)
    low, high = pl.BlockSpec(block, lambda i: (i, 0)), pl.BlockSpec(block, lambda i: (i + parts, 0))
    return chain.call(
        near_kernel, "near", (to_x, to_y, by_x, by_y), [high, low, low, low], [high, low],
        [shaped(to_x.shape, bf), shaped(to_y.shape, bf)], grid=(parts,), input_output_aliases={0: 0, 1: 1}, **options,
    )


def line_kernel(count, *refs):
    parts, refs = refs[:count], refs[count:]
    total = parts[0][...].astype(f32)
    for ref in parts[1:]:
        total = total + ref[...].astype(f32)
    if len(refs) == 1:
        refs[0][...] = total.astype(bf)
        return
    for s, ref in enumerate(refs):

        @pl.when(pl.program_id(0) == s)
        def _():
            ref[...] = total.astype(ref.dtype)


def line_call(chain, parts, size, apart, **options):
    quarters = 4 if len(parts) == 1 else 1
    rows, width = parts[0].shape[0] // quarters // size, parts[0].shape[1]
    block = pl.BlockSpec((rows, width), lambda i: (i, 0))
    ins = [pl.BlockSpec((rows, width), lambda i, q=q: (i + q * size, 0)) for q in range(quarters)]
    ins = ins if quarters > 1 else [block] * len(parts)
    parts = parts * quarters
    if apart:
        specs = [fixed(rows, width)] * size
        shapes = [shaped((rows, width), f32)] + [shaped((rows, width), bf)] * (size - 1)
    else:
        specs, shapes = [block], [shaped((size * rows, width), bf)]
    return chain.call(
        functools.partial(line_kernel, len(parts)), "line", parts, ins, specs, shapes, grid=(size,), **options
    )


def finish_kernel(cuts, count, note, spot_ref, first_ref, *refs):
    came, more, outs, squares_ref, total = (
        refs[:count], refs[count : -len(cuts) - 2], refs[-len(cuts) - 2 : -2], refs[-2], refs[-1]
    )
    rows = total.shape[0]
    result = first_ref[:rows].astype(f32)
    for b in range(1, first_ref.shape[0] // rows):
        result = result + first_ref[b * rows : (b + 1) * rows].astype(f32)
    for ref in came:
        result = result + ref[...].astype(f32)
    total[...] = result
    squares = jnp.sum(result * result, axis=0, keepdims=True)
    if note:
        whole = jnp.sum(squares, axis=1, keepdims=True)
        for ref in more[:-1]:
            whole = whole + jnp.sum(ref[...], axis=1, keepdims=True)
        gains = more[-1][...]
        whole = whole + jnp.sum(jnp.sum(gains * gains, axis=1, keepdims=True), axis=0, keepdims=True)
        squares = jnp.broadcast_to(whole, squares_ref.shape)
    squares_ref[...] = squares
    for ref, start in zip(outs, cuts):
        rows = ref.shape[0]
        if not isinstance(start, int):
            start = pl.multiple_of((spot_ref[3] ^ start[0]) * rows, rows & -rows)
        ref[...] = total[pl.ds(start, rows), :]


def finish_call(chain, spot, first, came, blocks, cuts, note=0, more=()):
    rows, width = first.shape[0] // blocks, first.shape[1]
    shapes = [(r, width) for _, r in cuts] + [(note, 128) if note else (1, width)]
    return chain.call(
        functools.partial(finish_kernel, [c for c, _ in cuts], len(came), note), "finish", (spot, first, *came, *more),
        [smem(), fixed(*first.shape)] + [fixed(rows, width)] * len(came) + [fixed(*v.shape) for v in more],
        [fixed(*s) for s in shapes], [shaped(s, f32) for s in shapes],
        grid=(1,), scratch_shapes=[pltpu.VMEM((rows, width), f32)],
    )


def adam_step(weight, grad, first, second, rate, decay):
    first_new = BETA_ONE * first + (1.0 - BETA_ONE) * grad
    second_new = BETA_TWO * second + (1.0 - BETA_TWO) * grad * grad
    corr_one = 1.0 - BETA_ONE**STEP
    corr_two = 1.0 - BETA_TWO**STEP
    update = first_new / corr_one / (jnp.sqrt(second_new / corr_two) + ADAM_EPS)
    return (weight - rate * (update + decay * weight), first_new, second_new)


def adam_kernel(spot_ref, note_ref, *refs):
    ins, outs, wide, tall = refs[:21], refs[21:35], refs[35], refs[36]
    mixer, gate_up, down, gains, parts = ins[:4], ins[4:7], ins[7:10], ins[10:13], ins[13:]
    mixer_out, gate_up_out, down_out, gains_out, norm_out = outs[:4], outs[4:7], outs[7:10], outs[10:13], outs[13]
    core, quarter = spot_ref[3], parts[0].shape[1]
    norm = jnp.sqrt(jnp.sum(note_ref[...], axis=0, keepdims=True)[:, :1])
    factor = CLIP_LIMIT / jnp.maximum(norm, CLIP_LIMIT)

    for s in range(2):
        mine = pl.multiple_of(core * 2 * quarter, quarter) + s * quarter
        came = pl.multiple_of((1 - core) * 2 * quarter, quarter) + s * quarter
        wide[:, pl.ds(pl.multiple_of(mine, quarter), quarter)] = parts[s][...]
        wide[:, pl.ds(pl.multiple_of(came, quarter), quarter)] = parts[2 + s][...]
    old, first, second, average = (r[...] for r in mixer)
    new, first, second = adam_step(old, wide[...] * factor, first, second, RATE_MATRIX, DECAY_MATRIX)
    average = AVERAGE_KEEP * average + (1.0 - AVERAGE_KEEP) * new
    for ref, value in zip(mixer_out, (new, first, second, average)):
        ref[...] = value

    @pl.when(pl.program_id(0) == 0)
    def _():
        half = parts[4].shape[0]
        tall[pl.ds(pl.multiple_of(core * half, half), half), :] = parts[4][...]
        tall[pl.ds(pl.multiple_of((1 - core) * half, half), half), :] = parts[5][...]
        for olds, news, grad, rate, decay in (
            (gate_up, gate_up_out, tall[...], RATE_MATRIX, DECAY_MATRIX),
            (down, down_out, parts[6][...], RATE_MATRIX, DECAY_MATRIX),
            (gains, gains_out, parts[7][...], RATE_GAIN, 0.0),
        ):
            old, first, second = (r[...] for r in olds)
            scale = factor if rate == RATE_MATRIX else factor[:, :1]
            for ref, value in zip(news, adam_step(old, grad * scale, first, second, rate, decay)):
                ref[...] = value
        norm_out[...] = norm


def adam_call(chain, spot, note, mixer, gate_up, down, gains, parts, blocks=6):
    rows, width = mixer[0].shape
    step = rows // blocks
    block = pl.BlockSpec((step, width), lambda i: (i, 0))
    piece = pl.BlockSpec((step, parts[0].shape[1]), lambda i: (i, 0))
    whole = lambda v: fixed(*v.shape)
    others = [*gate_up, *down, *gains]
    shapes = [v.shape for v in (*mixer, *others)] + [(1, 1)]
    return chain.call(
        adam_kernel, "adam", (spot, note, *mixer, *others, *parts),
        [smem(), whole(note)] + [block] * 4 + [whole(v) for v in others] + [piece] * 4
        + [whole(v) for v in parts[4:]],
        [block] * 4 + [whole(v) for v in others] + [fixed(1, 1)], [shaped(s, f32) for s in shapes],
        grid=(blocks,),
        scratch_shapes=[pltpu.VMEM((step, width), f32), pltpu.VMEM(gate_up[0].shape, f32)],
    )


def flip(v, axis, bits=1):
    size = lax.axis_size(axis)
    return lax.ppermute(v, axis, [(i, i ^ bits) for i in range(size)])


def swap(v):
    return flip(v, "core")


def join(mine, other, core, axis=0):
    return jnp.where(
        core == 0,
        jnp.concatenate([mine, other], axis=axis),
        jnp.concatenate([other, mine], axis=axis),
    )


def part(v, index, axis=0):
    size = v.shape[axis] // 2
    return lax.dynamic_slice_in_dim(v, index * size, size, axis)


def low(v):
    return v.astype(bf)


def wide(v):
    return v.astype(f32)


class Whole:
    crossed = False
    mixer_slots = ((0,), (0,))
    mixer_blocks = (1,)

    def __init__(self, spot, groups):
        self.spot, self.core = spot, spot[3]
        self.size = lax.axis_size("z")
        self.chips = lax.axis_size("d0") * lax.axis_size("d1") * self.size
        self.ffn_slots, self.ffn_blocks = tuple(range(groups)), (groups,)

    def gather(self, chain, mixer, gate_up, down, gains, waits):
        def trade(v, axis):
            return join(part(v, self.core, axis), swap(part(v, 1 - self.core, axis)), self.core)

        everything = lambda v: lax.all_gather(v, CHIPS, axis=0, tiled=True)
        mixer_block = trade(low(mixer), 1)
        w, groups = mixer_block.shape[1] // 2, len(self.ffn_slots)
        sides = []
        for s in range(2):
            whole = everything(mixer_block[:, s * w : (s + 1) * w])
            sides.append(([whole], ((0, 0, whole.shape[0], 0, None),), ()))
        ffn = [everything(v).reshape(groups, -1, v.shape[1]) for v in (trade(low(gate_up), 0), low(down))]
        ffn = [jnp.concatenate(ffn, axis=1)]
        gains = lax.all_gather(wide(low(gains)), EVERY, axis=1, tiled=True)
        yield jnp.pad(gains, ((0, NOTE - 2), (0, 0)))
        while True:
            yield sides, ffn

    def scatter(self, chain, parts, cuts, groups=1, apart=False):
        grads = parts[0].reshape(groups, -1, parts[0].shape[-1])
        rows = grads.shape[1] * 2 // 3
        if groups > 1:
            shards = [grads[:, :rows], grads[:, rows:]]
        else:
            shards = [grads]
        shards = [wide(lax.psum_scatter(flat(v), CHIPS, scatter_dimension=0, tiled=True)) for v in shards]
        outs = [part(shards[0], self.core), part(shards[0], 1 - self.core)] + shards[1:]
        squares = sum(jnp.sum(v * v, axis=0, keepdims=True) for v in shards)
        if groups == 1:
            yield
            yield ()
        through = yield
        yield (), through
        yield
        yield outs + [squares]

    def scatter_gains(self, grad):
        return lax.psum_scatter(grad, EVERY, scatter_dimension=1, tiled=True)

    def total(self, v):
        return lax.psum(v, EVERY)


class Cube(Whole):
    crossed = True
    near = ((0, 0), (0, 1), (1, 0), (1, 1))

    def __init__(self, spot, groups):
        super().__init__(spot, groups)
        slots = lambda fixed_z: tuple((y, x, s, fixed_z) for y, x in self.near for s in range(self.size))
        self.mixer_slots = slots(True), slots(False)
        self.mixer_blocks = (self.size,) * 3 + (self.size // 2,) * 2

    def lines(self, block):
        return [flip(block, "z", s) for s in range(1, self.size)]

    def gather(self, chain, mixer, gate_up, down, gains, waits):
        spot = self.spot
        mixer_mine, mixer_theirs, gate_mine, gate_theirs, down_low, note = pack_call(
            chain, spot, mixer, gate_up, down, gains
        )
        gate_came = swap(gate_theirs)
        size = self.size
        own, block = block_call(
            chain, spot, mixer_mine, swap(mixer_theirs), note, gate_came, gains.shape[1], size, waits
        )
        line = self.along_z(block)
        own_x, own_y = flip(own, "d1"), flip(own, "d0")
        yield None
        rows = own.shape[0] // 2 - NOTE
        half = rows // 2
        sides = []

        def spread_out(line):
            return line, flip(line, "d1"), flip(line, "d0")

        def turn_corner(from_x, from_y, extra=0):
            to_x, to_y = corner_call(chain, from_x, from_y, extra)
            return flip(to_x, "d1"), flip(to_y, "d0")

        def plan(side):
            found = [(p, side * (rows + NOTE) + h * half, half, near + (0, False), h) for p, near in enumerate(self.near[:3]) for h in range(2)]
            found += [(3, h * half, half, (1, 1, 0, False), h) for h in range(2)]
            last = (size - 1) * 2
            for at in range(last):
                s, h = at // 2 + 1, at % 2
                found += [(4 + p, at * half, half, near + (s, False), h) for p, near in enumerate(self.near[:3])]
                found.append((7 + (at >= last // 2), at % (last // 2) * half, half, (1, 1, s, False), h))
            return tuple(found)

        corner = turn_corner(own_x, own_y)
        yield
        chain.pause(*corner)
        others, line_rows = range(1, size), (size - 1) * rows
        moves = [(0, (rows + NOTE, s, 0), rows, 0, (s - 1) * rows) for s in others]
        moves += [(0, (rows + NOTE, s, rows), NOTE, 0, line_rows + (s - 1) * NOTE) for s in others]
        moves += [(1, rows + NOTE, rows, 1, s * rows) for s in range(size)]
        line, block = stack_call(
            chain, spot, (line, own), (line_rows + (size - 1) * NOTE, size * rows), tuple(moves)
        )
        first = spread_out(line)
        line = self.along_z(block)
        yield
        first_corner = turn_corner(*first[1:], (size - 1) * NOTE)
        chain.pause(*first_corner)
        notes = [(p, rows, near + (0, False)) for p, near in enumerate(self.near)]
        for s in others:
            notes += [(4 + p, line_rows + (s - 1) * NOTE, near + (s, False)) for p, near in enumerate(self.near[:3])]
            notes.append((7, line_rows // 2 + (s - 1) * NOTE, (1, 1, s, False)))
        sides.append(([own, own_x, own_y, corner[0], *first, *first_corner], plan(0), tuple(notes)))
        units, count = gate_mine.shape[0], down_low.shape[0]
        ffn_rows = 2 * units + count
        moves = [(0, (rows, s, 0), rows, 0, (s - 1) * rows) for s in others]
        for s in range(size):
            at = s * ffn_rows
            moves += [(1, 0, units, 1, at), (2, 0, units, 1, at + units), (3, 0, count, 1, at + 2 * units)]
        line, block = stack_call(
            chain, spot, (line, gate_mine, gate_came, down_low), (line_rows, size * ffn_rows), tuple(moves)
        )
        second = spread_out(line)
        line = self.along_z(block)
        yield sides, None
        second_corner = turn_corner(*second[1:])
        chain.pause(*second_corner)
        sides.append(([own, own_x, own_y, corner[1], *second, *second_corner], plan(1), ()))
        count = size * ffn_rows
        (block,) = stack_call(
            chain, spot, (line,), (4 * count,), tuple((0, 0, count, 0, c * count) for c in range(4))
        )
        ffn = lax.all_to_all(block, ("d0", "d1"), 0, 0, tiled=True)
        yield sides, [ffn.reshape(-1, ffn_rows, ffn.shape[-1])]

    def along_z(self, v):
        return lax.all_to_all(v, "z", 0, 0, tiled=True)

    def scatter(self, chain, parts, cuts, groups=1, apart=False):
        if groups > 1:
            came = (lax.all_to_all(flat(parts[0]), ("d0", "d1"), 0, 0, tiled=True),)
        else:
            own, to_x, to_y, far_low, far_high = (flat(v) for v in parts)
            by_x, by_y = flip(far_low, "d1"), flip(far_high, "d0")
            yield
            to_x, to_y = yield near_call(chain, to_x, to_y, by_x, by_y)
            came = own, flip(to_x, "d1"), flip(to_y, "d0")
        through = yield
        outs = line_call(chain, came, self.size, apart, through=through)
        count = self.size if apart else 1
        first, *rest = yield outs[:count], outs[count:]
        if apart:
            came = [flip(v, "z", s + 1) for s, v in enumerate(rest)]
        else:
            first, came = self.along_z(first), ()
        more = yield
        yield finish_call(
            chain, self.spot, first, came, 1 if apart else self.size, cuts, 2 * self.chips if more else 0, more or ()
        )

    def everyone(self, rows):
        count, length = rows.shape
        rows = jnp.pad(rows, ((0, 0), (0, -length % 128)))
        return lax.all_to_all(rows, EVERY, 0, 0, tiled=True)[:, :length]

    def scatter_gains(self, grad):
        devices = 2 * self.chips
        rows = grad.reshape(2, devices, -1).transpose(1, 0, 2).reshape(devices, -1)
        return jnp.sum(self.everyone(rows), axis=0).reshape(2, -1)


def body(
    inputs, lengths, filters, cotangent, mixer_weight, gate_up_weight, down_weight, norm_gains,
    mixer_first, gate_up_first, down_first, gains_first,
    mixer_second, gate_up_second, down_second, gains_second, mixer_average,
):
    slots, width = inputs.shape
    size = lax.axis_size("z")
    groups = 2 * FF // 256
    cube = lax.axis_size("d0") == 2 and lax.axis_size("d1") == 2 and size == 4
    spot = jnp.stack([lax.axis_index(a) for a in EVERY]).astype(jnp.int32)
    core = spot[3]
    links = (Cube if cube else Whole)(spot, groups)
    units = gate_up_weight.shape[0]
    chain = Chain()

    sums = lengths, swap(lengths)
    source_other, cotangent_other = swap(inputs), swap(cotangent)
    taps = jnp.concatenate([wide(filters), jnp.eye(AR_ORDER, slots, dtype=f32)])
    taps_turned = jnp.roll(taps[:, ::-1], 1 - slots // 4, axis=1)
    taps, taps_turned = (v.reshape(-1, 3, slots) for v in (taps, taps_turned))

    weights = links.gather(
        chain, mixer_weight, gate_up_weight, down_weight, norm_gains, (sums[1], source_other, cotangent_other)
    )
    gains = next(weights)
    tokens = normed_call(chain, spot, inputs, source_other)
    blocks = taps.shape[0]
    cuts, spread = (0, blocks * 5 // 9, blocks * 7 // 9, blocks), None
    for at in range(3):
        spread = spread_call(chain, sums, taps_turned, *tokens, cuts[at], cuts[at + 1] - cuts[at], spread)
        sides = next(weights)
    sides, _ = sides
    quarter = sides[0][0][0].shape[1]
    *mixed, gains = (*mix_call(chain, spot, spread, 0, *sides[0], gains, size, width), gains)[:3]
    sides, ffn = next(weights)
    mixed_own, mixed_other = mix_call(chain, spot, spread, 1, *sides[1], gains, size, width, mixed)

    hidden, normed_two = hidden_call(chain, inputs, mixed_own, swap(mixed_other), gains)
    tokens = (normed_two, swap(normed_two), cotangent, cotangent_other)
    branch_own, branch_other, two_own, two_other, *grad_ffn = ffn_call(
        chain, spot, sums, tokens, ffn, links.ffn_blocks, links.ffn_slots, size, links.crossed
    )
    ffn_sum = links.scatter(chain, grad_ffn, ((0, units // 2), (units // 2, units // 2), (units, units // 2)), groups)
    next(ffn_sum)
    grad_hidden, grad_low, gains_two = turn_call(
        chain, lengths, hidden, cotangent, two_own, swap(two_other), gains
    )
    grad_other = swap(grad_low)
    output = output_call(chain, hidden, branch_own, swap(branch_other))
    rows = mixer_weight.shape[0]
    cuts = (((0,), rows), ((1,), rows))
    grads_of = lambda s: grad_call(
        chain, spot, gains, grad_low, grad_other, spread, s, quarter, links.mixer_blocks, links.mixer_slots[s], size
    )
    first_sum = links.scatter(chain, grads_of(0), cuts)
    next(first_sum)
    second_sum = links.scatter(chain, grads_of(1), cuts, apart=True)
    next(second_sum)
    early = blocks // 2
    backward = lambda *how: back_call(
        chain, spot, sums, taps, grad_low, grad_other, [s[0] for s in sides], [s[1] for s in sides], size, *how
    )
    one = backward(0, early)
    outs, held = ffn_sum.send(next(first_sum))
    first_sum.send(held)
    ffn_sum.send(outs)
    second_sum.send(next(second_sum))
    one_own, one_other = backward(early, blocks - early, one)
    gate_up_mine, gate_up_theirs, shard_down, *squares = ffn_sum.send(())
    gate_up_came = swap(gate_up_theirs)
    outs, held = first_sum.send(())
    first_sum.send(outs)
    input_grad, gains_one = last_call(
        chain, spot, grad_hidden, inputs, one_own, swap(one_other), gains, (gate_up_came,)
    )
    first_mine, first_theirs, square = first_sum.send(())
    first_came = swap(first_theirs)
    squares.append(square)
    outs, held = second_sum.send((gains_one, gains_two))
    second_sum.send(outs)
    shard_gains = links.scatter_gains(jnp.concatenate(held))
    chain.pause(first_came)
    second_mine, second_theirs, note = second_sum.send((*squares, shard_gains))
    second_came = swap(second_theirs)
    mixer = mixer_weight, mixer_first, mixer_second, mixer_average
    gate_up, down = (gate_up_weight, gate_up_first, gate_up_second), (down_weight, down_first, down_second)
    gain = norm_gains, gains_first, gains_second
    if cube:
        (
            mixer_new, mixer_first_new, mixer_second_new, mixer_average_new, gate_up_new, gate_up_first_new,
            gate_up_second_new, down_new, down_first_new, down_second_new, gains_new, gains_first_new, gains_second_new,
            grad_norm,
        ) = adam_call(
            chain, spot, links.everyone(note), mixer, gate_up, down, gain,
            (first_mine, second_mine, first_came, second_came, gate_up_mine, gate_up_came, shard_down, shard_gains),
        )
        grad_norm = grad_norm[0, 0]
    else:
        squares = sum(jnp.sum(v) for v in (*squares, note)) + jnp.sum(shard_gains * shard_gains)
        grad_norm = jnp.sqrt(links.total(squares))
        factor = CLIP_LIMIT / jnp.maximum(grad_norm, CLIP_LIMIT)
        shard_mixer = join(
            jnp.concatenate([first_mine, second_mine], axis=1), jnp.concatenate([first_came, second_came], axis=1), core, 1
        )
        shard_gate_up = join(gate_up_mine, gate_up_came, core)
        step = lambda old, grad: adam_step(old[0], grad * factor, old[1], old[2], RATE_MATRIX, DECAY_MATRIX)
        mixer_new, mixer_first_new, mixer_second_new = step(mixer, shard_mixer)
        gate_up_new, gate_up_first_new, gate_up_second_new = step(gate_up, shard_gate_up)
        down_new, down_first_new, down_second_new = step(down, shard_down)
        gains_new, gains_first_new, gains_second_new = adam_step(
            gain[0], shard_gains * factor, gain[1], gain[2], RATE_GAIN, 0.0
        )
        mixer_average_new = AVERAGE_KEEP * mixer_average + (1.0 - AVERAGE_KEEP) * mixer_new
    return (
        output, input_grad, grad_norm, mixer_new, gate_up_new, down_new, gains_new,
        mixer_first_new, gate_up_first_new, down_first_new, gains_first_new,
        mixer_second_new, gate_up_second_new, down_second_new, gains_second_new, mixer_average_new,
    )


def solution(mesh):
    outer, inner = mesh.shape["dp"], mesh.shape["fsdp"]
    side = math.isqrt(outer)
    if side * side != outer:
        side = 1
    split = jax.sharding.Mesh(
        np.asarray(mesh.devices).reshape(side, outer // side, inner // 2, 2), EVERY
    )
    rows, columns, whole = P(EVERY, None), P(None, EVERY), P()
    return jax.shard_map(
        body,
        mesh=split,
        in_specs=(
            rows, rows, whole, rows, rows, rows, rows, columns,
            rows, rows, rows, columns, rows, rows, rows, columns, rows,
        ),
        out_specs=(
            rows, rows, whole, rows, rows, rows, columns, rows, rows, rows, columns,
            rows, rows, rows, columns, rows,
        ),
        check_vma=False,
    )
```

time: 766 us -> 358 us (0.47)
  waiting for transfers between devices: 509 us -> 83.1 us
  Pallas kernels: 78.5 us -> 174 us
  starting transfers between devices: 3.3 us -> 64.1 us
  blocking collectives: 79.8 us -> 27.8 us
  other arithmetic: 37.1 us -> 3.03 us
  local copies, waits for them, and re-layouts: 37 us -> 3.03 us
  between operations: 19.2 us -> 1.09 us
    reduce_scatter x3 -> x0, waiting for transfers between devices: 246 us -> none  [body(): lax.psum_scatter(v, CHIPS, scatter_dimension=0, tiled=True)]
    all_gather x3 -> x0, waiting for transfers between devices: 130 us -> none  [body(): gather = lambda v: lax.all_gather(v, CHIPS, axis=0, tiled=True)]
    unnamed x8 -> x0, waiting for transfers between devices: 127 us -> none
    pallas_call x5 -> x36, Pallas kernels: 78.5 us -> 174 us  [call(): pl.pallas_call(whole, name=name, in_specs=list(in_specs) + [anywhere() fo...]
    ppermute x13 -> x37, waiting for transfers between devices: 5.55 us -> 62.3 us  [flip(): return lax.ppermute(v, axis, [(i, i ^ bits) for i in range(size)])]
    all_gather x1 -> x0, blocking collectives: 43 us -> none  [body(): lax.all_gather(norm_gains.astype(bf), EVERY, axis=1, tiled=True).astype(f32)]
    psum x1 -> x0, blocking collectives: 36.8 us -> none  [body(): grad_norm = jnp.sqrt(lax.psum(squares, EVERY))]
    all_to_all x0 -> x7, starting transfers between devices: none -> 35.2 us  [the longest x5 25.4 us: along_z(): return lax.all_to_all(v, 'z', 0, 0, tiled=True)]
  transfers between devices with their start and end apart: 20 -> 44, of which waited for: 10 -> 17; matrix products, arithmetic and copies ran while one was open for 8% -> 2% of each run, Pallas kernels for 8% -> 34%
where the time goes in v3:
time: 358 us; the launch traced here: 356 us
  Pallas kernels  174 us (49%)
  waiting for transfers between devices  83.1 us (23%)
  starting transfers between devices  64.1 us (18%)
  blocking collectives  27.8 us (8%)
    pallas_call x36, Pallas kernels, call(): pl.pallas_call(whole, name=name, in_specs=list(in_specs) + [anywhere() fo...  174 us
    ppermute x37, waiting for transfers between devices, flip(): return lax.ppermute(v, axis, [(i, i ^ bits) for i in range(size)])  62.3 us
    ppermute x37, starting transfers between devices, flip(): return lax.ppermute(v, axis, [(i, i ^ bits) for i in range(size)])  28.9 us
    all_to_all x2, blocking collectives, everyone(): return lax.all_to_all(rows, EVERY, 0, 0, tiled=True)[:, :length]  27.8 us
    all_to_all x5, starting transfers between devices, along_z(): return lax.all_to_all(v, 'z', 0, 0, tiled=True)  25.4 us
    all_to_all x5, waiting for transfers between devices, along_z(): return lax.all_to_all(v, 'z', 0, 0, tiled=True)  12 us
    all_to_all x1, waiting for transfers between devices, gather(): ffn = lax.all_to_all(block, ('d0', 'd1'), 0, 0, tiled=True)  8.8 us
  transfers between devices with their start and end apart: 44, of which 17 were waited for; matrix products, arithmetic and copies ran while one was open for 2% of the time, Pallas kernels for 34%

profile of v3, /device:TPU:0, one launch (start us, length us, event | category | flops | bytes accessed | tf_op | source)
XLA Modules:
  0.0 355.7 jit_solution(370272700571292892)
XLA Ops:
  8.4 6.2 %all-to-all-start = ((bf16[4,880,128]{2,1,0:T(8,128)(2,1)}), bf16[4,880,128]{2,1,0:T(8,128)(2,1)}, u32[]{:S(2)}, u32[]{:S(2)}) async-start(bf16[4,880,128]{2,1,0:T(8,128)(2,1)} %bitcast.31), calls=%async_computation | async-start | bytes 1802240 | tf_op jit(solution)/shard_map/all_to_all | solution.py:1014
  22.2 8.1 %spread.3 = (bf16[2,1024,3456]{2,1,0:T(8,128)(2,1)}, f32[8,128]{1,0:T(8,128)}) custom-call(s32[1,3]{1,0:T(1,128)} %refs_1_.9, s32[1,3]{1,0:T(1,128)} %collective-permute-done.refs_5_.refs_1_.refs_2_, f32[9,3,512]{2,1,0:T(4,128)} %reshape.71.refs_2_, bf16[512,256]{1,0:T(8,128)(2,1)} %get-tuple-element.147.refs_3_, ...), custom_call_target="tpu_custom_call" | custom-call | flops 1 | bytes 1 | tf_op jit(solution)/shard_map/spread/pallas_call | solution.py:57
  33.2 4.7 %spread.4 = (bf16[2,1024,3456]{2,1,0:T(8,128)(2,1)}, f32[8,128]{1,0:T(8,128)}) custom-call(s32[1,3]{1,0:T(1,128)} %refs_1_.9, s32[1,3]{1,0:T(1,128)} %collective-permute-done.refs_5_.refs_1_.refs_2_, f32[9,3,512]{2,1,0:T(4,128)} %reshape.71.refs_2_, bf16[512,256]{1,0:T(8,128)(2,1)} %get-tuple-element.147.refs_3_, ...), custom_call_target="tpu_custom_call", output_to_operand_aliasing={{0}: (5, {})} | custom-call | flops 1 | bytes 1 | tf_op jit(solution)/shard_map/spread/pallas_call | solution.py:57
  42.1 4.8 %all-to-all-start.1 = ((bf16[4,864,128]{2,1,0:T(8,128)(2,1)}), bf16[4,864,128]{2,1,0:T(8,128)(2,1)}, u32[]{:S(2)}, u32[]{:S(2)}) async-start(bf16[4,864,128]{2,1,0:T(8,128)(2,1)} %bitcast.32), calls=%async_computation.1 | async-start | bytes 1769472 | tf_op jit(solution)/shard_map/all_to_all | solution.py:1014
  48.9 4.7 %spread.5 = (bf16[2,1024,3456]{2,1,0:T(8,128)(2,1)}, f32[8,128]{1,0:T(8,128)}) custom-call(s32[1,3]{1,0:T(1,128)} %refs_1_.9, s32[1,3]{1,0:T(1,128)} %collective-permute-done.refs_5_.refs_1_.refs_2_, f32[9,3,512]{2,1,0:T(4,128)} %reshape.71.refs_2_, bf16[512,256]{1,0:T(8,128)(2,1)} %get-tuple-element.147.refs_3_, ...), custom_call_target="tpu_custom_call", output_to_operand_aliasing={{0}: (5, {})} | custom-call | flops 1 | bytes 1 | tf_op jit(solution)/shard_map/spread/pallas_call | solution.py:57
  53.5 8.4 %collective-permute-done.9.refs_0_.refs_7_.refs_11_ = bf16[2640,128]{1,0:T(8,128)(2,1)} collective-permute-done((bf16[2640,128]{1,0:T(8,128)(2,1)}, bf16[2640,128]{1,0:T(8,128)(2,1)}, u32[]{:S(2)}, u32[]{:S(2)}) %collective-permute-start.9) | collective-permute-done | bytes 675872 | tf_op jit(solution)/shard_map/ppermute | solution.py:842
  66.6 6.7 %collective-permute-done.12.refs_1_.refs_10_.refs_14_ = bf16[1296,128]{1,0:T(8,128)(2,1)} collective-permute-done((bf16[1296,128]{1,0:T(8,128)(2,1)}, bf16[1296,128]{1,0:T(8,128)(2,1)}, u32[]{:S(2)}, u32[]{:S(2)}) %collective-permute-start.12) | collective-permute-done | bytes 331808 | tf_op jit(solution)/shard_map/ppermute | solution.py:842
  75.7 4.8 %all-to-all-start.2 = ((bf16[4,192,512]{2,1,0:T(8,128)(2,1)}), bf16[4,192,512]{2,1,0:T(8,128)(2,1)}, u32[]{:S(2)}, u32[]{:S(2)}) async-start(bf16[4,192,512]{2,1,0:T(8,128)(2,1)} %bitcast.35), calls=%async_computation.2 | async-start | bytes 1572864 | tf_op jit(solution)/shard_map/all_to_all | solution.py:1014
  82.8 11.4 %mix.2 = (f32[512,512]{1,0:T(8,128)}, f32[512,512]{1,0:T(8,128)}, f32[16,512]{1,0:T(8,128)}, f32[8,128]{1,0:T(8,128)}) custom-call(s32[4]{0:T(128)} %pad_add_fusion.refs_0_, bf16[2,1024,3456]{2,1,0:T(8,128)(2,1)} %get-tuple-element.160.refs_1_.refs_4_, bf16[1760,128]{1,0:T(8,128)(2,1)} %get-tuple-element.151.refs_2_.refs_6_.refs_15_, ...), custom_call_target="tpu_custom_call" | custom-call | flops 1 | bytes 1 | tf_op jit(solution)/shard_map/mix/pallas_call | solution.py:57
  98.1 5.7 %collective-permute-done.15.refs_0_.refs_9_.refs_22_ = bf16[1296,128]{1,0:T(8,128)(2,1)} collective-permute-done((bf16[1296,128]{1,0:T(8,128)(2,1)}, bf16[1296,128]{1,0:T(8,128)(2,1)}, u32[]{:S(2)}, u32[]{:S(2)}) %collective-permute-start.15) | collective-permute-done | bytes 331808 | tf_op jit(solution)/shard_map/ppermute | solution.py:842
  107.4 4.8 %all-to-all-start.3 = ((bf16[4,768,512]{2,1,0:T(8,128)(2,1)}), bf16[4,768,512]{2,1,0:T(8,128)(2,1)}, u32[]{:S(2)}, u32[]{:S(2)}) async-start(bf16[4,768,512]{2,1,0:T(8,128)(2,1)} %bitcast.30), calls=%async_computation.3 | async-start | bytes 6291456 | tf_op jit(solution)/shard_map/all_to_all | solution.py:1010
  112.2 11.6 %mix.3 = (f32[512,512]{1,0:T(8,128)}, f32[512,512]{1,0:T(8,128)}, f32[8,128]{1,0:T(8,128)}) custom-call(s32[4]{0:T(128)} %pad_add_fusion.refs_0_, bf16[2,1024,3456]{2,1,0:T(8,128)(2,1)} %get-tuple-element.160.refs_1_.refs_4_, bf16[1760,128]{1,0:T(8,128)(2,1)} %get-tuple-element.151.refs_2_.refs_6_.refs_15_, ...), custom_call_target="tpu_custom_call" | custom-call | flops 1 | bytes 1 | tf_op jit(solution)/shard_map/mix/pallas_call | solution.py:57
  126.8 3.8 %hidden.1 = (f32[512,512]{1,0:T(8,128)}, bf16[512,512]{1,0:T(8,128)(2,1)}, f32[8,128]{1,0:T(8,128)}) custom-call(bf16[512,512]{1,0:T(8,128)(2,1)} %refs_2_.6, f32[512,512]{1,0:T(8,128)} %get-tuple-element.180.refs_1_, f32[512,512]{1,0:T(8,128)} %collective-permute-done.17.refs_2_, f32[16,512]{1,0:T(8,128)} %get-tuple-element.176.refs_13_.refs_3_.refs_5_.refs_1_, ...), custom_call_target="tpu_custom_call" | custom-call | flops 1 | bytes 1 | tf_op jit(solution)/shard_map/hidden/pallas_call | solution.py:57
  132.9 8.8 %all-to-all-done.3 = bf16[4,768,512]{2,1,0:T(8,128)(2,1)} async-done(((bf16[4,768,512]{2,1,0:T(8,128)(2,1)}), bf16[4,768,512]{2,1,0:T(8,128)(2,1)}, u32[]{:S(2)}, u32[]{:S(2)}) %all-to-all-start.3) | async-done | bytes 3145760 | tf_op jit(solution)/shard_map/all_to_all | solution.py:1010
  141.7 20.6 %ffn.1 = (f32[512,512]{1,0:T(8,128)}, f32[512,512]{1,0:T(8,128)}, f32[512,512]{1,0:T(8,128)}, f32[512,512]{1,0:T(8,128)}, bf16[16,192,512]{2,1,0:T(8,128)(2,1)}, /*index=5*/f32[8,128]{1,0:T(8,128)}) custom-call(s32[4]{0:T(128)} %pad_add_fusion.refs_0_, s32[1,3]{1,0:T(1,128)} %refs_1_.9, s32[1,3]{1,0:T(1,128)} %collective-permute-done.refs_5_.refs_1_.refs_2_, ...), custom_call_target="tpu_custom_call" | custom-call | flops 1 | bytes 1 | tf_op jit(solution)/shard_map/ffn/pallas_call | solution.py:57
  162.3 5.0 %all-to-all-start.4 = ((bf16[4,768,512]{2,1,0:T(8,128)(2,1)}), bf16[4,768,512]{2,1,0:T(8,128)(2,1)}, u32[]{:S(2)}, u32[]{:S(2)}) async-start(bf16[4,768,512]{2,1,0:T(8,128)(2,1)} %bitcast.29), calls=%async_computation.4 | async-start | bytes 6291456 | tf_op jit(solution)/shard_map/all_to_all | solution.py:1018
  170.8 4.4 %turn.1 = (f32[512,512]{1,0:T(8,128)}, bf16[512,512]{1,0:T(8,128)(2,1)}, f32[1,512]{1,0:T(1,128)}, f32[8,128]{1,0:T(8,128)}) custom-call(s32[1,3]{1,0:T(1,128)} %refs_1_.9, f32[512,512]{1,0:T(8,128)} %get-tuple-element.183.refs_1_.refs_0_, bf16[512,512]{1,0:T(8,128)(2,1)} %refs_2_.5, f32[512,512]{1,0:T(8,128)} %get-tuple-element.189.refs_3_, ...), custom_call_target="tpu_custom_call" | custom-call | flops 1 | bytes 1 | tf_op jit(solution)/shard_map/turn/pallas_call | solution.py:57
  179.1 9.1 %mixer_grad.2 = (bf16[3456,128]{1,0:T(8,128)(2,1)}, bf16[3456,128]{1,0:T(8,128)(2,1)}, bf16[3456,128]{1,0:T(8,128)(2,1)}, bf16[1728,128]{1,0:T(8,128)(2,1)}, bf1...) custom-call(s32[4]{0:T(128)} %pad_add_fusion.refs_0_, f32[16,512]{1,0:T(8,128)} %get-tuple-element.176.refs_13_.refs_3_.refs_5_.refs_1_, ...), custom_call_target="tpu_custom_call" | custom-call | flops 1 | bytes 1 | tf_op jit(solution)/shard_map/mixer_grad/pallas_call | solution.py:57
  193.7 9.1 %mixer_grad.3 = (bf16[3456,128]{1,0:T(8,128)(2,1)}, bf16[3456,128]{1,0:T(8,128)(2,1)}, bf16[3456,128]{1,0:T(8,128)(2,1)}, bf16[1728,128]{1,0:T(8,128)(2,1)}, bf1...) custom-call(s32[4]{0:T(128)} %pad_add_fusion.refs_0_, f32[16,512]{1,0:T(8,128)} %get-tuple-element.176.refs_13_.refs_3_.refs_5_.refs_1_, ...), custom_call_target="tpu_custom_call" | custom-call | flops 1 | bytes 1 | tf_op jit(solution)/shard_map/mixer_grad/pallas_call | solution.py:57
  202.8 12.4 %spread_back.2 = (f32[512,256]{1,0:T(8,128)}, f32[512,256]{1,0:T(8,128)}, f32[8,128]{1,0:T(8,128)}) custom-call(s32[4]{0:T(128)} %pad_add_fusion.refs_0_, s32[1,3]{1,0:T(1,128)} %refs_1_.9, s32[1,3]{1,0:T(1,128)} %collective-permute-done.refs_5_.refs_1_.refs_2_, f32[9,3,512]{2,1,0:T(4,128)} %reshape.73.refs_3_, ...), custom_call_target="tpu_custom_call" | custom-call | flops 1 | bytes 1 | tf_op jit(solution)/shard_map/spread_back/pallas_call | solution.py:57
  217.6 4.0 %line.3 = (bf16[768,512]{1,0:T(8,128)(2,1)}, bf16[3456,128]{1,0:T(8,128)(2,1)}, bf16[3456,128]{1,0:T(8,128)(2,1)}, f32[8,128]{1,0:T(8,128)}) custom-call(bf16[3072,512]{1,0:T(8,128)(2,1)} %bitcast.13.refs_0_.refs_1_.refs_2_.refs_3_, bf16[3072,512]{1,0:T(8,128)(2,1)} %bitcast.13.refs_0_.refs_1_.refs_2_.refs_3_, ...), custom_call_target="tpu_custom_call", output_to_operand_aliasing={{1}: (4, {}), {2}: (5, {})} | custom-call | flops 1 | bytes 1 | tf_op jit(solution)/shard_map/line/pallas_call | solution.py:57
  221.5 4.8 %all-to-all-start.5 = ((bf16[4,192,512]{2,1,0:T(8,128)(2,1)}), bf16[4,192,512]{2,1,0:T(8,128)(2,1)}, u32[]{:S(2)}, u32[]{:S(2)}) async-start(bf16[4,192,512]{2,1,0:T(8,128)(2,1)} %bitcast.34), calls=%async_computation.5 | async-start | bytes 1572864 | tf_op jit(solution)/shard_map/all_to_all | solution.py:1014
  230.4 26.8 %collective-permute-done.22.refs_2_ = bf16[1728,128]{1,0:T(8,128)(2,1)} collective-permute-done((bf16[1728,128]{1,0:T(8,128)(2,1)}, bf16[1728,128]{1,0:T(8,128)(2,1)}, u32[]{:S(2)}, u32[]{:S(2)}) %collective-permute-start.22) | collective-permute-done | bytes 442400 | tf_op jit(solution)/shard_map/ppermute | solution.py:842
  259.8 14.3 %spread_back.3 = (f32[512,256]{1,0:T(8,128)}, f32[512,256]{1,0:T(8,128)}, f32[8,128]{1,0:T(8,128)}) custom-call(s32[4]{0:T(128)} %pad_add_fusion.refs_0_, s32[1,3]{1,0:T(1,128)} %refs_1_.9, s32[1,3]{1,0:T(1,128)} %collective-permute-done.refs_5_.refs_1_.refs_2_, f32[9,3,512]{2,1,0:T(4,128)} %reshape.73.refs_3_, ...), custom_call_target="tpu_custom_call" | custom-call | flops 1 | bytes 1 | tf_op jit(solution)/shard_map/spread_back/pallas_call | solution.py:57
  276.1 3.8 %line.4 = (bf16[3456,128]{1,0:T(8,128)(2,1)}, f32[8,128]{1,0:T(8,128)}) custom-call(bf16[3456,128]{1,0:T(8,128)(2,1)} %get-tuple-element.221.refs_0_, bf16[3456,128]{1,0:T(8,128)(2,1)} %collective-permute-done.28.refs_1_, bf16[3456,128]{1,0:T(8,128)(2,1)} %collective-permute-done.29.refs_2_, f32[8,128]{1,0:T(8,128)} %get-tuple-element.224.refs_3_), custom_call_target="tpu_custom_call" | custom-call | flops 1 | bytes 1 | tf_op jit(solution)/shard_map/line/pallas_call | solution.py:57
  279.9 4.8 %all-to-all-start.6 = ((bf16[4,864,128]{2,1,0:T(8,128)(2,1)}), bf16[4,864,128]{2,1,0:T(8,128)(2,1)}, u32[]{:S(2)}, u32[]{:S(2)}) async-start(bf16[4,864,128]{2,1,0:T(8,128)(2,1)} %bitcast.33), calls=%async_computation.6 | async-start | bytes 1769472 | tf_op jit(solution)/shard_map/all_to_all | solution.py:1014
  289.2 4.1 %last.1 = (f32[512,512]{1,0:T(8,128)}, f32[1,512]{1,0:T(1,128)}, f32[8,128]{1,0:T(8,128)}) custom-call(s32[4]{0:T(128)} %pad_add_fusion.refs_0_, f32[512,512]{1,0:T(8,128)} %get-tuple-element.194.refs_1_, bf16[512,512]{1,0:T(8,128)(2,1)} %refs_2_.6, f32[512,256]{1,0:T(8,128)} %get-tuple-element.216.refs_3_, f32[512,256]{1,0:T(8,128)} %collective-permute-done.26.refs_4_, ...), custom_call_target="tpu_custom_call" | custom-call | flops 1 | bytes 1 | tf_op jit(solution)/shard_map/last/pallas_call | solution.py:57
  293.3 12.0 %all-to-all-done.6 = bf16[4,864,128]{2,1,0:T(8,128)(2,1)} async-done(((bf16[4,864,128]{2,1,0:T(8,128)(2,1)}), bf16[4,864,128]{2,1,0:T(8,128)(2,1)}, u32[]{:S(2)}, u32[]{:S(2)}) %all-to-all-start.6) | async-done | bytes 884768 | tf_op jit(solution)/shard_map/all_to_all | solution.py:1014
  307.4 3.8 %line.5 = (f32[864,128]{1,0:T(8,128)}, bf16[864,128]{1,0:T(8,128)(2,1)}, bf16[864,128]{1,0:T(8,128)(2,1)}, bf16[864,128]{1,0:T(8,128)(2,1)}, f32[1,512]{1,0:T(1,...) custom-call(bf16[3456,128]{1,0:T(8,128)(2,1)} %get-tuple-element.227.refs_0_, ...), custom_call_target="tpu_custom_call", output_to_operand_aliasing={{4}: (3, {}), {5}: (4, {})} | custom-call | flops 1 | bytes 1 | tf_op jit(solution)/shard_map/line/pallas_call | solution.py:57
  316.6 17.6 %all_to_all.98 = f32[32,1,128]{2,1,0:T(1,128)S(1)} all-to-all(f32[32,1,128]{2,1,0:T(1,128)S(1)} %copy.45), channel_id=1, replica_groups=mesh['d0'=2,'d1'=2,'z'=4,'core'=2] {'d0','d1','z','core'}, dimensions={0} | all-to-all | bytes 32768 | tf_op jit(solution)/shard_map/all_to_all | solution.py:1041
  337.2 10.1 %all_to_all.99 = f32[32,1,128]{2,1,0:T(1,128)} all-to-all(f32[32,1,128]{2,1,0:T(1,128)} %bitcast.41), channel_id=1, replica_groups=mesh['d0'=2,'d1'=2,'z'=4,'core'=2] {'d0','d1','z','core'}, dimensions={0} | all-to-all | bytes 32768 | tf_op jit(solution)/shard_map/all_to_all | solution.py:1041
  347.4 8.2 %adam.1 = (f32[432,512]{1,0:T(8,128)}, f32[432,512]{1,0:T(8,128)}, f32[432,512]{1,0:T(8,128)}, f32[432,512]{1,0:T(8,128)}, f32[128,512]{1,0:T(8,128)}, /*index=5...) custom-call(s32[4]{0:T(128)} %pad_add_fusion.refs_0_, ...), custom_call_target="tpu_custom_call" | custom-call | flops 1 | bytes 1 | tf_op jit(solution)/shard_map/adam/pallas_call | solution.py:57
  (119 shorter events, 85.4 us)
Async XLA Ops:
  8.4 31.1 %all-to-all-start = ((bf16[4,880,128]{2,1,0:T(8,128)(2,1)}), bf16[4,880,128]{2,1,0:T(8,128)(2,1)}, u32[]{:S(2)}, u32[]{:S(2)}) async-start(bf16[4,880,128]{2,1,0:T(8,128)(2,1)} %bitcast.31), calls=%async_computation | async-start | bytes 1802240 | tf_op jit(solution)/shard_map/all_to_all | solution.py:1014
  15.3 14.9 %collective-permute-start.5 = (bf16[1760,128]{1,0:T(8,128)(2,1)}, bf16[1760,128]{1,0:T(8,128)(2,1)}, u32[]{:S(2)}, u32[]{:S(2)}) collective-permute-start(bf16[1760,128]{1,0:T(8,128)(2,1)} %get-tuple-element.151.refs_2_.refs_6_.refs_15_), channel_id=1, source_target_pairs={{0,8},{8,0},{1,9},{9,1},{2,10},{10,2},{3,11},{11,3},{4,12},{12,4},... | collective-permute-start | bytes 1351688 | tf_op jit(solution)/shard_map/ppermute | solution.py:842
  16.8 13.4 %collective-permute-start.6 = (bf16[1760,128]{1,0:T(8,128)(2,1)}, bf16[1760,128]{1,0:T(8,128)(2,1)}, u32[]{:S(2)}, u32[]{:S(2)}) collective-permute-start(bf16[1760,128]{1,0:T(8,128)(2,1)} %get-tuple-element.151.refs_2_.refs_6_.refs_15_), channel_id=1, source_target_pairs={{0,16},{16,0},{1,17},{17,1},{2,18},{18,2},{3,19},{19,3},{4,20},{20... | collective-permute-start | bytes 1351688 | tf_op jit(solution)/shard_map/ppermute | solution.py:842
  32.2 7.1 %collective-permute-start.7 = (bf16[880,128]{1,0:T(8,128)(2,1)}, bf16[880,128]{1,0:T(8,128)(2,1)}, u32[]{:S(2)}, u32[]{:S(2)}) collective-permute-start(bf16[880,128]{1,0:T(8,128)(2,1)} %get-tuple-element.156), channel_id=1, source_target_pairs={{0,8},{8,0},{1,9},{9,1},{2,10},{10,2},{3,11},{11,3},{4,12},{12,4},... | collective-permute-start | bytes 675848 | tf_op jit(solution)/shard_map/ppermute | solution.py:842
  42.1 31.2 %all-to-all-start.1 = ((bf16[4,864,128]{2,1,0:T(8,128)(2,1)}), bf16[4,864,128]{2,1,0:T(8,128)(2,1)}, u32[]{:S(2)}, u32[]{:S(2)}) async-start(bf16[4,864,128]{2,1,0:T(8,128)(2,1)} %bitcast.32), calls=%async_computation.1 | async-start | bytes 1769472 | tf_op jit(solution)/shard_map/all_to_all | solution.py:1014
  46.9 15.1 %collective-permute-start.9 = (bf16[2640,128]{1,0:T(8,128)(2,1)}, bf16[2640,128]{1,0:T(8,128)(2,1)}, u32[]{:S(2)}, u32[]{:S(2)}) collective-permute-start(bf16[2640,128]{1,0:T(8,128)(2,1)} %get-tuple-element.164.refs_6_.refs_10_), channel_id=1, source_target_pairs={{0,8},{8,0},{1,9},{9,1},{2,10},{10,2},{3,11},{11,3},{4,12},{12,4},... | collective-permute-start | bytes 2027528 | tf_op jit(solution)/shard_map/ppermute | solution.py:842
  48.4 14.7 %collective-permute-start.10 = (bf16[2640,128]{1,0:T(8,128)(2,1)}, bf16[2640,128]{1,0:T(8,128)(2,1)}, u32[]{:S(2)}, u32[]{:S(2)}) collective-permute-start(bf16[2640,128]{1,0:T(8,128)(2,1)} %get-tuple-element.164.refs_6_.refs_10_), channel_id=1, source_target_pairs={{0,16},{16,0},{1,17},{17,1},{2,18},{18,2},{3,19},{19,3},{4,20},{20... | collective-permute-start | bytes 2027528 | tf_op jit(solution)/shard_map/ppermute | solution.py:842
  65.3 8.0 %collective-permute-start.11 = (bf16[1344,128]{1,0:T(8,128)(2,1)}, bf16[1344,128]{1,0:T(8,128)(2,1)}, u32[]{:S(2)}, u32[]{:S(2)}) collective-permute-start(bf16[1344,128]{1,0:T(8,128)(2,1)} %get-tuple-element.166), channel_id=1, source_target_pairs={{0,8},{8,0},{1,9},{9,1},{2,10},{10,2},{3,11},{11,3},{4,12},{12,4},... | collective-permute-start | bytes 1032200 | tf_op jit(solution)/shard_map/ppermute | solution.py:842
  65.9 7.4 %collective-permute-start.12 = (bf16[1296,128]{1,0:T(8,128)(2,1)}, bf16[1296,128]{1,0:T(8,128)(2,1)}, u32[]{:S(2)}, u32[]{:S(2)}) collective-permute-start(bf16[1296,128]{1,0:T(8,128)(2,1)} %get-tuple-element.167), channel_id=1, source_target_pairs={{0,16},{16,0},{1,17},{17,1},{2,18},{18,2},{3,19},{19,3},{4,20},{20... | collective-permute-start | bytes 995336 | tf_op jit(solution)/shard_map/ppermute | solution.py:842
  75.7 28.7 %all-to-all-start.2 = ((bf16[4,192,512]{2,1,0:T(8,128)(2,1)}), bf16[4,192,512]{2,1,0:T(8,128)(2,1)}, u32[]{:S(2)}, u32[]{:S(2)}) async-start(bf16[4,192,512]{2,1,0:T(8,128)(2,1)} %bitcast.35), calls=%async_computation.2 | async-start | bytes 1572864 | tf_op jit(solution)/shard_map/all_to_all | solution.py:1014
  80.5 13.7 %collective-permute-start.13 = (bf16[2592,128]{1,0:T(8,128)(2,1)}, bf16[2592,128]{1,0:T(8,128)(2,1)}, u32[]{:S(2)}, u32[]{:S(2)}) collective-permute-start(bf16[2592,128]{1,0:T(8,128)(2,1)} %get-tuple-element.169.refs_6_.refs_19_), channel_id=1, source_target_pairs={{0,8},{8,0},{1,9},{9,1},{2,10},{10,2},{3,11},{11,3},{4,12},{12,4},... | collective-permute-start | bytes 1990664 | tf_op jit(solution)/shard_map/ppermute | solution.py:842
  81.9 12.3 %collective-permute-start.14 = (bf16[2592,128]{1,0:T(8,128)(2,1)}, bf16[2592,128]{1,0:T(8,128)(2,1)}, u32[]{:S(2)}, u32[]{:S(2)}) collective-permute-start(bf16[2592,128]{1,0:T(8,128)(2,1)} %get-tuple-element.169.refs_6_.refs_19_), channel_id=1, source_target_pairs={{0,16},{16,0},{1,17},{17,1},{2,18},{18,2},{3,19},{19,3},{4,20},{20... | collective-permute-start | bytes 1990664 | tf_op jit(solution)/shard_map/ppermute | solution.py:842
  96.4 7.4 %collective-permute-start.15 = (bf16[1296,128]{1,0:T(8,128)(2,1)}, bf16[1296,128]{1,0:T(8,128)(2,1)}, u32[]{:S(2)}, u32[]{:S(2)}) collective-permute-start(bf16[1296,128]{1,0:T(8,128)(2,1)} %get-tuple-element.172), channel_id=1, source_target_pairs={{0,8},{8,0},{1,9},{9,1},{2,10},{10,2},{3,11},{11,3},{4,12},{12,4},... | collective-permute-start | bytes 995336 | tf_op jit(solution)/shard_map/ppermute | solution.py:842
  96.9 7.4 %collective-permute-start.16 = (bf16[1296,128]{1,0:T(8,128)(2,1)}, bf16[1296,128]{1,0:T(8,128)(2,1)}, u32[]{:S(2)}, u32[]{:S(2)}) collective-permute-start(bf16[1296,128]{1,0:T(8,128)(2,1)} %get-tuple-element.173), channel_id=1, source_target_pairs={{0,16},{16,0},{1,17},{17,1},{2,18},{18,2},{3,19},{19,3},{4,20},{20... | collective-permute-start | bytes 995336 | tf_op jit(solution)/shard_map/ppermute | solution.py:842
  107.4 34.3 %all-to-all-start.3 = ((bf16[4,768,512]{2,1,0:T(8,128)(2,1)}), bf16[4,768,512]{2,1,0:T(8,128)(2,1)}, u32[]{:S(2)}, u32[]{:S(2)}) async-start(bf16[4,768,512]{2,1,0:T(8,128)(2,1)} %bitcast.30), calls=%async_computation.3 | async-start | bytes 6291456 | tf_op jit(solution)/shard_map/all_to_all | solution.py:1010
  162.3 55.3 %all-to-all-start.4 = ((bf16[4,768,512]{2,1,0:T(8,128)(2,1)}), bf16[4,768,512]{2,1,0:T(8,128)(2,1)}, u32[]{:S(2)}, u32[]{:S(2)}) async-start(bf16[4,768,512]{2,1,0:T(8,128)(2,1)} %bitcast.29), calls=%async_computation.4 | async-start | bytes 6291456 | tf_op jit(solution)/shard_map/all_to_all | solution.py:1018
  167.4 8.1 %collective-permute-start.19 = (f32[512,512]{1,0:T(8,128)}, f32[512,512]{1,0:T(8,128)}, u32[]{:S(2)}, u32[]{:S(2)}) collective-permute-start(f32[512,512]{1,0:T(8,128)} %get-tuple-element.188), channel_id=1, source_target_pairs={{0,1},{1,0},{2,3},{3,2},{4,5},{5,4},{6,7},{7,6},{8,9},{9,8},{10,11... | collective-permute-start | bytes 3145736 | tf_op jit(solution)/shard_map/ppermute | solution.py:842
  188.2 27.0 %collective-permute-start.24 = (bf16[1728,128]{1,0:T(8,128)(2,1)}, bf16[1728,128]{1,0:T(8,128)(2,1)}, u32[]{:S(2)}, u32[]{:S(2)}) collective-permute-start(bf16[1728,128]{1,0:T(8,128)(2,1)} %get-tuple-element.208), channel_id=1, source_target_pairs={{0,8},{8,0},{1,9},{9,1},{2,10},{10,2},{3,11},{11,3},{4,12},{12,4},... | collective-permute-start | bytes 1327112 | tf_op jit(solution)/shard_map/ppermute | solution.py:842
  190.7 24.5 %collective-permute-start.25 = (bf16[1728,128]{1,0:T(8,128)(2,1)}, bf16[1728,128]{1,0:T(8,128)(2,1)}, u32[]{:S(2)}, u32[]{:S(2)}) collective-permute-start(bf16[1728,128]{1,0:T(8,128)(2,1)} %get-tuple-element.209), channel_id=1, source_target_pairs={{0,16},{16,0},{1,17},{17,1},{2,18},{18,2},{3,19},{19,3},{4,20},{20... | collective-permute-start | bytes 1327112 | tf_op jit(solution)/shard_map/ppermute | solution.py:842
  221.5 52.6 %all-to-all-start.5 = ((bf16[4,192,512]{2,1,0:T(8,128)(2,1)}), bf16[4,192,512]{2,1,0:T(8,128)(2,1)}, u32[]{:S(2)}, u32[]{:S(2)}) async-start(bf16[4,192,512]{2,1,0:T(8,128)(2,1)} %bitcast.34), calls=%async_computation.5 | async-start | bytes 1572864 | tf_op jit(solution)/shard_map/all_to_all | solution.py:1014
  226.3 49.8 %collective-permute-start.28 = (bf16[3456,128]{1,0:T(8,128)(2,1)}, bf16[3456,128]{1,0:T(8,128)(2,1)}, u32[]{:S(2)}, u32[]{:S(2)}) collective-permute-start(bf16[3456,128]{1,0:T(8,128)(2,1)} %get-tuple-element.222), channel_id=1, source_target_pairs={{0,8},{8,0},{1,9},{9,1},{2,10},{10,2},{3,11},{11,3},{4,12},{12,4},... | collective-permute-start | bytes 2654216 | tf_op jit(solution)/shard_map/ppermute | solution.py:842
  226.9 49.2 %collective-permute-start.29 = (bf16[3456,128]{1,0:T(8,128)(2,1)}, bf16[3456,128]{1,0:T(8,128)(2,1)}, u32[]{:S(2)}, u32[]{:S(2)}) collective-permute-start(bf16[3456,128]{1,0:T(8,128)(2,1)} %get-tuple-element.223), channel_id=1, source_target_pairs={{0,16},{16,0},{1,17},{17,1},{2,18},{18,2},{3,19},{19,3},{4,20},{20... | collective-permute-start | bytes 2654216 | tf_op jit(solution)/shard_map/ppermute | solution.py:842
  226.9 30.2 %collective-permute-start.22 = (bf16[1728,128]{1,0:T(8,128)(2,1)}, bf16[1728,128]{1,0:T(8,128)(2,1)}, u32[]{:S(2)}, u32[]{:S(2)}) collective-permute-start(bf16[1728,128]{1,0:T(8,128)(2,1)} %get-tuple-element.203), channel_id=1, source_target_pairs={{0,8},{8,0},{1,9},{9,1},{2,10},{10,2},{3,11},{11,3},{4,12},{12,4},... | collective-permute-start | bytes 1327112 | tf_op jit(solution)/shard_map/ppermute | solution.py:842
  228.9 28.6 %collective-permute-start.23 = (bf16[1728,128]{1,0:T(8,128)(2,1)}, bf16[1728,128]{1,0:T(8,128)(2,1)}, u32[]{:S(2)}, u32[]{:S(2)}) collective-permute-start(bf16[1728,128]{1,0:T(8,128)(2,1)} %get-tuple-element.204), channel_id=1, source_target_pairs={{0,16},{16,0},{1,17},{17,1},{2,18},{18,2},{3,19},{19,3},{4,20},{20... | collective-permute-start | bytes 1327112 | tf_op jit(solution)/shard_map/ppermute | solution.py:842
  279.9 25.4 %all-to-all-start.6 = ((bf16[4,864,128]{2,1,0:T(8,128)(2,1)}), bf16[4,864,128]{2,1,0:T(8,128)(2,1)}, u32[]{:S(2)}, u32[]{:S(2)}) async-start(bf16[4,864,128]{2,1,0:T(8,128)(2,1)} %bitcast.33), calls=%async_computation.6 | async-start | bytes 1769472 | tf_op jit(solution)/shard_map/all_to_all | solution.py:1014
  284.7 22.7 %collective-permute-start.30 = (bf16[3456,128]{1,0:T(8,128)(2,1)}, bf16[3456,128]{1,0:T(8,128)(2,1)}, u32[]{:S(2)}, u32[]{:S(2)}) collective-permute-start(bf16[3456,128]{1,0:T(8,128)(2,1)} %get-tuple-element.228), channel_id=1, source_target_pairs={{0,8},{8,0},{1,9},{9,1},{2,10},{10,2},{3,11},{11,3},{4,12},{12,4},... | collective-permute-start | bytes 2654216 | tf_op jit(solution)/shard_map/ppermute | solution.py:842
  286.2 21.2 %collective-permute-start.31 = (bf16[3456,128]{1,0:T(8,128)(2,1)}, bf16[3456,128]{1,0:T(8,128)(2,1)}, u32[]{:S(2)}, u32[]{:S(2)}) collective-permute-start(bf16[3456,128]{1,0:T(8,128)(2,1)} %get-tuple-element.229), channel_id=1, source_target_pairs={{0,16},{16,0},{1,17},{17,1},{2,18},{18,2},{3,19},{19,3},{4,20},{20... | collective-permute-start | bytes 2654216 | tf_op jit(solution)/shard_map/ppermute | solution.py:842
  311.3 23.6 %collective-permute-start.32 = (bf16[864,128]{1,0:T(8,128)(2,1)}, bf16[864,128]{1,0:T(8,128)(2,1)}, u32[]{:S(2)}, u32[]{:S(2)}) collective-permute-start(bf16[864,128]{1,0:T(8,128)(2,1)} %get-tuple-element.236), channel_id=1, source_target_pairs={{0,2},{2,0},{4,6},{6,4},{1,3},{3,1},{5,7},{7,5},{8,10},{10,8},{12,... | collective-permute-start | bytes 663560 | tf_op jit(solution)/shard_map/ppermute | solution.py:842
  311.3 23.6 %collective-permute-start.33 = (bf16[864,128]{1,0:T(8,128)(2,1)}, bf16[864,128]{1,0:T(8,128)(2,1)}, u32[]{:S(2)}, u32[]{:S(2)}) collective-permute-start(bf16[864,128]{1,0:T(8,128)(2,1)} %get-tuple-element.237), channel_id=1, source_target_pairs={{0,4},{2,6},{4,0},{6,2},{1,5},{3,7},{5,1},{7,3},{8,12},{10,14},{12... | collective-permute-start | bytes 663560 | tf_op jit(solution)/shard_map/ppermute | solution.py:842
  313.5 21.4 %collective-permute-start.34 = (bf16[864,128]{1,0:T(8,128)(2,1)}, bf16[864,128]{1,0:T(8,128)(2,1)}, u32[]{:S(2)}, u32[]{:S(2)}) collective-permute-start(bf16[864,128]{1,0:T(8,128)(2,1)} %get-tuple-element.238), channel_id=1, source_target_pairs={{0,6},{2,4},{4,2},{6,0},{1,7},{3,5},{5,3},{7,1},{8,14},{10,12},{12... | collective-permute-start | bytes 663560 | tf_op jit(solution)/shard_map/ppermute | solution.py:842
  316.5 18.3 %collective-permute-start.35 = (f32[432,128]{1,0:T(8,128)}, f32[432,128]{1,0:T(8,128)}, u32[]{:S(2)}, u32[]{:S(2)}) collective-permute-start(f32[432,128]{1,0:T(8,128)} %get-tuple-element.243), channel_id=1, source_target_pairs={{0,1},{1,0},{2,3},{3,2},{4,5},{5,4},{6,7},{7,6},{8,9},{9,8},{10,11... | collective-permute-start | bytes 663560 | tf_op jit(solution)/shard_map/ppermute | solution.py:842
  337.2 10.2 %collective-permute-start.36 = (f32[432,128]{1,0:T(8,128)}, f32[432,128]{1,0:T(8,128)}, u32[]{:S(2)}, u32[]{:S(2)}) collective-permute-start(f32[432,128]{1,0:T(8,128)} %get-tuple-element.248), channel_id=1, source_target_pairs={{0,1},{1,0},{2,3},{3,2},{4,5},{5,4},{6,7},{7,6},{8,9},{9,8},{10,11... | collective-permute-start | bytes 663560 | tf_op jit(solution)/shard_map/ppermute | solution.py:842
  (15 other events, 48.5 us)

commit v4 on v3

--- a/solution.py
+++ b/solution.py
@@ -67,8 +67,8 @@
         )(*args, *last)
         return outs[0] if single else outs
 
-    def pause(self, *waits):
-        self.call(lambda: None, "pause", (), [], [], [], waits=waits)
+    def pause(self, waits=(), through=()):
+        return self.call(lambda: None, "pause", (), [], [], [], waits=waits, through=through)
 
 
 def smem():
@@ -228,7 +228,7 @@
 
         @pl.when(step == g)
         def _():
-            out[...] = result if first else result + before[g][...]
+            out[...] = (result if first else result + before[g][...]).astype(out.dtype)
 
 
 def mix_call(chain, spot, u, side, pieces, plan, notes, gains, size, width, before=()):
@@ -245,7 +245,8 @@
         [smem(), pl.BlockSpec((1, step, depth), lambda i: (side, i, 0))] + [anywhere() for _ in pieces]
         + [out for _ in before] + [note for _ in given],
         [out, out] + [note for _ in range(1 - len(given))],
-        [shaped((step, width), f32)] * 2 + [shaped((NOTE, width), f32) for _ in range(1 - len(given))],
+        [shaped((step, width), f32), shaped((step, width), bf if before else f32)]
+        + [shaped((NOTE, width), f32) for _ in range(1 - len(given))],
         grid=(2,),
         scratch_shapes=[
             pltpu.VMEM((total, w), bf), pltpu.VMEM((width, depth), bf), pltpu.SemaphoreType.DMA((len(plan) + len(notes),)),
@@ -253,19 +254,23 @@
     )
 
 
-def hidden_kernel(source_ref, own_ref, came_ref, gain_ref, hidden_ref, normed_ref):
-    hidden = source_ref[...].astype(f32) + (own_ref[...] + came_ref[...])
+def hidden_kernel(source_ref, own_ref, came_ref, gain_ref, hidden_ref, *normed_refs):
+    hidden = source_ref[...].astype(f32) + (own_ref[...] + came_ref[...].astype(f32))
     scale = lax.rsqrt(jnp.mean(hidden * hidden, axis=-1, keepdims=True) + NORM_EPS)
     hidden_ref[...] = hidden
-    normed_ref[...] = (hidden * scale * gain_ref[1:2]).astype(bf)
+    normed = (hidden * scale * gain_ref[1:2]).astype(bf)
+    width = normed_refs[0].shape[1]
+    for i, ref in enumerate(normed_refs):
+        ref[...] = normed[:, i * width : (i + 1) * width]
 
 
 def hidden_call(chain, source, own, came, gain, parts=4):
     rows, width = source.shape
     block = pl.BlockSpec((rows // parts, width), lambda i: (i, 0))
+    thin = pl.BlockSpec((rows // parts, width // 2), lambda i: (i, 0))
     return chain.call(
         hidden_kernel, "hidden", (source, own, came, gain), [block, block, block, fixed(NOTE, width)],
-        [block, block], [shaped((rows, width), f32), shaped((rows, width), bf)],
+        [block, thin, thin], [shaped((rows, width), f32)] + [shaped((rows, width // 2), bf)] * 2,
         grid=(parts,),
     )
 
@@ -476,9 +481,9 @@
     return v.reshape(-1, v.shape[-1])
 
 
-def ffn_kernel(count, outs, steps, slots, size, crossed, spot_ref, lengths_ref, came_ref, *refs):
+def ffn_kernel(count, outs, steps, slots, out_slots, size, crossed, spot_ref, lengths_ref, came_ref, *refs):
     turned = spot_ref[3] if crossed else 0
-    tokens, pieces, refs = refs[:4], refs[4 : 4 + count], refs[4 + count :]
+    tokens, pieces, refs = refs[:6], refs[6 : 6 + count], refs[6 + count :]
     results, grads, (held, dealt, normed, back, sem) = refs[:4], refs[4 : 4 + outs], refs[4 + outs :]
     n = tokens[0].shape[0]
     chips, units, width = held.shape[0], held.shape[1] * 2 // 3, held.shape[2]
@@ -502,9 +507,12 @@
                 at += 1
         for c in copies:
             c.start()
-        normed[:n], normed[n:] = tokens[0][...], tokens[1][...]
-        back[:n] = live_rows(tokens[2][...].astype(f32), lengths_ref).astype(bf)
-        back[n:] = live_rows(tokens[3][...].astype(f32), came_ref).astype(bf)
+        half_width = tokens[0].shape[1]
+        for i in range(2):
+            cols = slice(i * half_width, (i + 1) * half_width)
+            normed[:n, cols], normed[n:, cols] = tokens[i][...], tokens[2 + i][...]
+        back[:n] = live_rows(tokens[4][...].astype(f32), lengths_ref).astype(bf)
+        back[n:] = live_rows(tokens[5][...].astype(f32), came_ref).astype(bf)
         for c in copies:
             c.wait()
 
@@ -545,21 +553,21 @@
         for ref in grads:
             for b in range(ref.shape[0]):
                 copies.append(
-                    pltpu.make_async_copy(dealt.at[chip_of(spot_ref, slots[at], size)], ref.at[b], sem.at[0, at])
+                    pltpu.make_async_copy(dealt.at[chip_of(spot_ref, out_slots[at], size)], ref.at[b], sem.at[0, at])
                 )
                 at += 1
         run_copies(copies)
 
 
-def ffn_call(chain, spot, lengths, tokens, pieces, blocks, slots, size, crossed, chunk=256):
-    n, d = tokens[0].shape
+def ffn_call(chain, spot, lengths, tokens, pieces, blocks, slots, out_slots, size, crossed, chunk=256):
+    n, d = tokens[-1].shape
     chips, rows = len(slots), pieces[0].shape[1]
     units = rows * 2 // 3
     steps = chips // 2 * units // chunk
     return chain.call(
-        functools.partial(ffn_kernel, len(pieces), len(blocks), steps, slots, size, crossed), "ffn",
+        functools.partial(ffn_kernel, len(pieces), len(blocks), steps, slots, out_slots, size, crossed), "ffn",
         (spot, *lengths, *tokens, *pieces),
-        [smem()] * 3 + [fixed(n, d)] * 4 + [anywhere() for _ in pieces],
+        [smem()] * 3 + [fixed(*v.shape) for v in tokens] + [anywhere() for _ in pieces],
         [fixed(n, d)] * 4 + [anywhere() for _ in blocks],
         [shaped((n, d), f32)] * 4 + [shaped((b, rows, d), bf) for b in blocks],
         grid=(steps,),
@@ -752,9 +760,8 @@
         whole = jnp.sum(squares, axis=1, keepdims=True)
         for ref in more[:-1]:
             whole = whole + jnp.sum(ref[...], axis=1, keepdims=True)
-        gains = more[-1][...]
-        whole = whole + jnp.sum(jnp.sum(gains * gains, axis=1, keepdims=True), axis=0, keepdims=True)
-        squares = jnp.broadcast_to(whole, squares_ref.shape)
+        gains = jnp.sum(more[-1][...], axis=0, keepdims=True)
+        squares = jnp.broadcast_to(whole + jnp.sum(gains * gains, axis=1, keepdims=True), squares_ref.shape)
     squares_ref[...] = squares
     for ref, start in zip(outs, cuts):
         rows = ref.shape[0]
@@ -763,14 +770,14 @@
         ref[...] = total[pl.ds(start, rows), :]
 
 
-def finish_call(chain, spot, first, came, blocks, cuts, note=0, more=()):
+def finish_call(chain, spot, first, came, blocks, cuts, note=0, more=(), waits=()):
     rows, width = first.shape[0] // blocks, first.shape[1]
     shapes = [(r, width) for _, r in cuts] + [(note, 128) if note else (1, width)]
     return chain.call(
         functools.partial(finish_kernel, [c for c, _ in cuts], len(came), note), "finish", (spot, first, *came, *more),
         [smem(), fixed(*first.shape)] + [fixed(rows, width)] * len(came) + [fixed(*v.shape) for v in more],
         [fixed(*s) for s in shapes], [shaped(s, f32) for s in shapes],
-        grid=(1,), scratch_shapes=[pltpu.VMEM((rows, width), f32)],
+        grid=(1,), scratch_shapes=[pltpu.VMEM((rows, width), f32)], waits=waits,
     )
 
 
@@ -807,10 +814,13 @@
         half = parts[4].shape[0]
         tall[pl.ds(pl.multiple_of(core * half, half), half), :] = parts[4][...]
         tall[pl.ds(pl.multiple_of((1 - core) * half, half), half), :] = parts[5][...]
+        own = gains[0].shape[1]
+        sums = jnp.sum(parts[7][...], axis=0, keepdims=True)
+        gain_grad = jnp.concatenate([sums[:, :own], sums[:, own : 2 * own]])
         for olds, news, grad, rate, decay in (
             (gate_up, gate_up_out, tall[...], RATE_MATRIX, DECAY_MATRIX),
             (down, down_out, parts[6][...], RATE_MATRIX, DECAY_MATRIX),
-            (gains, gains_out, parts[7][...], RATE_GAIN, 0.0),
+            (gains, gains_out, gain_grad, RATE_GAIN, 0.0),
         ):
             old, first, second = (r[...] for r in olds)
             scale = factor if rate == RATE_MATRIX else factor[:, :1]
@@ -876,7 +886,8 @@
         self.spot, self.core = spot, spot[3]
         self.size = lax.axis_size("z")
         self.chips = lax.axis_size("d0") * lax.axis_size("d1") * self.size
-        self.ffn_slots, self.ffn_blocks = tuple(range(groups)), (groups,)
+        self.ffn_in = self.ffn_out = tuple(range(groups))
+        self.ffn_blocks = (groups,)
 
     def gather(self, chain, mixer, gate_up, down, gains, waits):
         def trade(v, axis):
@@ -884,7 +895,7 @@
 
         everything = lambda v: lax.all_gather(v, CHIPS, axis=0, tiled=True)
         mixer_block = trade(low(mixer), 1)
-        w, groups = mixer_block.shape[1] // 2, len(self.ffn_slots)
+        w, groups = mixer_block.shape[1] // 2, len(self.ffn_in)
         sides = []
         for s in range(2):
             whole = everything(mixer_block[:, s * w : (s + 1) * w])
@@ -914,7 +925,7 @@
         yield
         yield outs + [squares]
 
-    def scatter_gains(self, grad):
+    def spread_gains(self, grad):
         return lax.psum_scatter(grad, EVERY, scatter_dimension=1, tiled=True)
 
     def total(self, v):
@@ -928,7 +939,9 @@
     def __init__(self, spot, groups):
         super().__init__(spot, groups)
         slots = lambda fixed_z: tuple((y, x, s, fixed_z) for y, x in self.near for s in range(self.size))
-        self.mixer_slots = slots(True), slots(False)
+        self.mixer_slots = slots(False), slots(False)
+        self.ffn_in = slots(True)
+        self.ffn_out = tuple(yx * self.size + z for z in range(self.size) for yx in range(4))
         self.mixer_blocks = (self.size,) * 3 + (self.size // 2,) * 2
 
     def lines(self, block):
@@ -970,7 +983,7 @@
 
         corner = turn_corner(own_x, own_y)
         yield
-        chain.pause(*corner)
+        chain.pause(corner)
         others, line_rows = range(1, size), (size - 1) * rows
         moves = [(0, (rows + NOTE, s, 0), rows, 0, (s - 1) * rows) for s in others]
         moves += [(0, (rows + NOTE, s, rows), NOTE, 0, line_rows + (s - 1) * NOTE) for s in others]
@@ -982,7 +995,6 @@
         line = self.along_z(block)
         yield
         first_corner = turn_corner(*first[1:], (size - 1) * NOTE)
-        chain.pause(*first_corner)
         notes = [(p, rows, near + (0, False)) for p, near in enumerate(self.near)]
         for s in others:
             notes += [(4 + p, line_rows + (s - 1) * NOTE, near + (s, False)) for p, near in enumerate(self.near[:3])]
@@ -997,25 +1009,22 @@
         line, block = stack_call(
             chain, spot, (line, gate_mine, gate_came, down_low), (line_rows, size * ffn_rows), tuple(moves)
         )
-        second = spread_out(line)
-        line = self.along_z(block)
+        across, line = line, self.along_z(block)
+        second = spread_out(*chain.pause(first_corner, (across,)))
         yield sides, None
         second_corner = turn_corner(*second[1:])
-        chain.pause(*second_corner)
         sides.append(([own, own_x, own_y, corner[1], *second, *second_corner], plan(1), ()))
-        count = size * ffn_rows
-        (block,) = stack_call(
-            chain, spot, (line,), (4 * count,), tuple((0, 0, count, 0, c * count) for c in range(4))
-        )
-        ffn = lax.all_to_all(block, ("d0", "d1"), 0, 0, tiled=True)
-        yield sides, [ffn.reshape(-1, ffn_rows, ffn.shape[-1])]
+        ffn = spread_out(*chain.pause(second_corner, (line,)))
+        yield sides, None
+        ffn = (*ffn, *turn_corner(*ffn[1:]))
+        yield sides, [v.reshape(-1, ffn_rows, v.shape[-1]) for v in ffn]
 
     def along_z(self, v):
         return lax.all_to_all(v, "z", 0, 0, tiled=True)
 
     def scatter(self, chain, parts, cuts, groups=1, apart=False):
         if groups > 1:
-            came = (lax.all_to_all(flat(parts[0]), ("d0", "d1"), 0, 0, tiled=True),)
+            came = (self.along_z(flat(parts[0])),)
         else:
             own, to_x, to_y, far_low, far_high = (flat(v) for v in parts)
             by_x, by_y = flip(far_low, "d1"), flip(far_high, "d0")
@@ -1023,27 +1032,27 @@
             to_x, to_y = yield near_call(chain, to_x, to_y, by_x, by_y)
             came = own, flip(to_x, "d1"), flip(to_y, "d0")
         through = yield
-        outs = line_call(chain, came, self.size, apart, through=through)
+        outs = line_call(chain, came, self.size, apart, through=through or ())
         count = self.size if apart else 1
         first, *rest = yield outs[:count], outs[count:]
         if apart:
             came = [flip(v, "z", s + 1) for s, v in enumerate(rest)]
+        elif groups > 1:
+            first, came = lax.all_to_all(first, ("d0", "d1"), 0, 0, tiled=True), ()
         else:
             first, came = self.along_z(first), ()
-        more = yield
+        more, waits = yield
         yield finish_call(
-            chain, self.spot, first, came, 1 if apart else self.size, cuts, 2 * self.chips if more else 0, more or ()
+            chain, self.spot, first, came, 1 if apart else self.size, cuts, 2 * self.chips if more else 0, more, waits
         )
 
-    def everyone(self, rows):
-        count, length = rows.shape
-        rows = jnp.pad(rows, ((0, 0), (0, -length % 128)))
-        return lax.all_to_all(rows, EVERY, 0, 0, tiled=True)[:, :length]
-
-    def scatter_gains(self, grad):
+    def spread_gains(self, grad):
         devices = 2 * self.chips
         rows = grad.reshape(2, devices, -1).transpose(1, 0, 2).reshape(devices, -1)
-        return jnp.sum(self.everyone(rows), axis=0).reshape(2, -1)
+        return self.everyone(jnp.pad(rows, ((0, 0), (0, -rows.shape[1] % 128))))
+
+    def everyone(self, rows):
+        return lax.all_to_all(rows, EVERY, 0, 0, tiled=True)
 
 
 def body(
@@ -1073,20 +1082,21 @@
     gains = next(weights)
     tokens = normed_call(chain, spot, inputs, source_other)
     blocks = taps.shape[0]
-    cuts, spread = (0, blocks * 5 // 9, blocks * 7 // 9, blocks), None
+    cuts, spread = (0, blocks // 3, blocks * 2 // 3, blocks), None
     for at in range(3):
         spread = spread_call(chain, sums, taps_turned, *tokens, cuts[at], cuts[at + 1] - cuts[at], spread)
         sides = next(weights)
     sides, _ = sides
     quarter = sides[0][0][0].shape[1]
     *mixed, gains = (*mix_call(chain, spot, spread, 0, *sides[0], gains, size, width), gains)[:3]
-    sides, ffn = next(weights)
+    sides, _ = next(weights)
     mixed_own, mixed_other = mix_call(chain, spot, spread, 1, *sides[1], gains, size, width, mixed)
-
-    hidden, normed_two = hidden_call(chain, inputs, mixed_own, swap(mixed_other), gains)
-    tokens = (normed_two, swap(normed_two), cotangent, cotangent_other)
+    _, ffn = next(weights)
+
+    hidden, *normed_two = hidden_call(chain, inputs, mixed_own, swap(mixed_other), gains)
+    tokens = (*normed_two, *(swap(v) for v in normed_two), cotangent, cotangent_other)
     branch_own, branch_other, two_own, two_other, *grad_ffn = ffn_call(
-        chain, spot, sums, tokens, ffn, links.ffn_blocks, links.ffn_slots, size, links.crossed
+        chain, spot, sums, tokens, ffn, links.ffn_blocks, links.ffn_in, links.ffn_out, size, links.crossed
     )
     ffn_sum = links.scatter(chain, grad_ffn, ((0, units // 2), (units // 2, units // 2), (units, units // 2)), groups)
     next(ffn_sum)
@@ -1094,41 +1104,47 @@
         chain, lengths, hidden, cotangent, two_own, swap(two_other), gains
     )
     grad_other = swap(grad_low)
-    output = output_call(chain, hidden, branch_own, swap(branch_other))
     rows = mixer_weight.shape[0]
     cuts = (((0,), rows), ((1,), rows))
     grads_of = lambda s: grad_call(
         chain, spot, gains, grad_low, grad_other, spread, s, quarter, links.mixer_blocks, links.mixer_slots[s], size
     )
-    first_sum = links.scatter(chain, grads_of(0), cuts)
+    first_sum = links.scatter(chain, grads_of(0), cuts, apart=True)
     next(first_sum)
     second_sum = links.scatter(chain, grads_of(1), cuts, apart=True)
     next(second_sum)
-    early = blocks // 2
-    backward = lambda *how: back_call(
-        chain, spot, sums, taps, grad_low, grad_other, [s[0] for s in sides], [s[1] for s in sides], size, *how
-    )
-    one = backward(0, early)
-    outs, held = ffn_sum.send(next(first_sum))
-    first_sum.send(held)
+    one = ()
+    backward = lambda at, one: back_call(
+        chain, spot, sums, taps, grad_low, grad_other, [s[0] for s in sides], [s[1] for s in sides], size,
+        at * (blocks // 3), blocks // 3, one,
+    )
+    one = backward(0, one)
+    held = next(first_sum), next(second_sum)
+    count = len(held[0])
+    held = chain.pause(through=(*held[0], *held[1])) if cube else ()
+    first_sum.send(held[:count])
+    second_sum.send(held[count:])
+    one = backward(1, one)
+    one_own, one_other = backward(2, one)
+    outs, _ = first_sum.send(())
+    first_sum.send(outs)
+    outs, _ = ffn_sum.send(())
     ffn_sum.send(outs)
-    second_sum.send(next(second_sum))
-    one_own, one_other = backward(early, blocks - early, one)
-    gate_up_mine, gate_up_theirs, shard_down, *squares = ffn_sum.send(())
-    gate_up_came = swap(gate_up_theirs)
-    outs, held = first_sum.send(())
-    first_sum.send(outs)
+    outs, _ = second_sum.send(())
+    first_mine, first_theirs, square = first_sum.send(((), ()))
+    one_other, first_theirs, branch_other, *outs = chain.pause(
+        through=(one_other, first_theirs, branch_other, *outs)
+    )
+    second_sum.send(outs)
+    gate_up_mine, gate_up_theirs, shard_down, *squares = ffn_sum.send(((), ()))
     input_grad, gains_one = last_call(
-        chain, spot, grad_hidden, inputs, one_own, swap(one_other), gains, (gate_up_came,)
-    )
-    first_mine, first_theirs, square = first_sum.send(())
-    first_came = swap(first_theirs)
+        chain, spot, grad_hidden, inputs, one_own, swap(one_other), gains, ()
+    )
     squares.append(square)
-    outs, held = second_sum.send((gains_one, gains_two))
-    second_sum.send(outs)
-    shard_gains = links.scatter_gains(jnp.concatenate(held))
-    chain.pause(first_came)
-    second_mine, second_theirs, note = second_sum.send((*squares, shard_gains))
+    shard_gains = links.spread_gains(jnp.concatenate([gains_one, gains_two]))
+    output = output_call(chain, hidden, branch_own, swap(branch_other))
+    gate_up_came, first_came = swap(gate_up_theirs), swap(first_theirs)
+    second_mine, second_theirs, note = second_sum.send(((*squares, shard_gains), ()))
     second_came = swap(second_theirs)
     mixer = mixer_weight, mixer_first, mixer_second, mixer_average
     gate_up, down = (gate_up_weight, gate_up_first, gate_up_second), (down_weight, down_first, down_second)

time: 358 us -> 315 us (0.88)
  waiting for transfers between devices: 83.1 us -> 55.1 us
  blocking collectives: 27.8 us -> 0 us
  starting transfers between devices: 64.1 us -> 73.1 us
  Pallas kernels: 174 us -> 179 us
    all_to_all x2 -> x0, blocking collectives: 27.8 us -> none  [everyone(): return lax.all_to_all(rows, EVERY, 0, 0, tiled=True)[:, :length]]
    ppermute x37 -> x45, waiting for transfers between devices: 62.3 us -> 39.3 us  [flip(): return lax.ppermute(v, axis, [(i, i ^ bits) for i in range(size)])]
    all_to_all x5 -> x4, waiting for transfers between devices: 12 us -> 0.01 us  [along_z(): return lax.all_to_all(v, 'z', 0, 0, tiled=True)]
    ppermute x37 -> x45, starting transfers between devices: 28.9 us -> 39.5 us  [flip(): return lax.ppermute(v, axis, [(i, i ^ bits) for i in range(size)])]
    all_to_all x2 -> x3, waiting for transfers between devices: 8.8 us -> 15.8 us  [the longest x2 9.84 us: everyone(): return lax.all_to_all(rows, EVERY, 0, 0, tiled=True)]
    pallas_call x36 -> x38, Pallas kernels: 174 us -> 179 us  [call(): pl.pallas_call(whole, name=name, in_specs=list(in_specs) + [anywhere() fo...]
    all_to_all x5 -> x4, starting transfers between devices: 25.4 us -> 20.6 us  [along_z(): return lax.all_to_all(v, 'z', 0, 0, tiled=True)]
    all_to_all x2 -> x3, starting transfers between devices: 9.82 us -> 13 us  [the longest x2 8.49 us: everyone(): return lax.all_to_all(rows, EVERY, 0, 0, tiled=True)]
  transfers between devices with their start and end apart: 44 -> 52, of which waited for: 17 -> 23; matrix products, arithmetic and copies ran while one was open for 2% -> 2% of each run, Pallas kernels for 34% -> 46%
where the time goes in v4:
time: 315 us; the launch traced here: 314 us
  Pallas kernels  179 us (57%)
  starting transfers between devices  73.1 us (23%)
  waiting for transfers between devices  55.1 us (17%)
    pallas_call x38, Pallas kernels, call(): pl.pallas_call(whole, name=name, in_specs=list(in_specs) + [anywhere() fo...  179 us
    ppermute x45, starting transfers between devices, flip(): return lax.ppermute(v, axis, [(i, i ^ bits) for i in range(size)])  39.5 us
    ppermute x45, waiting for transfers between devices, flip(): return lax.ppermute(v, axis, [(i, i ^ bits) for i in range(size)])  39.3 us
    all_to_all x4, starting transfers between devices, along_z(): return lax.all_to_all(v, 'z', 0, 0, tiled=True)  20.6 us
    all_to_all x2, waiting for transfers between devices, everyone(): return lax.all_to_all(rows, EVERY, 0, 0, tiled=True)  9.84 us
    all_to_all x2, starting transfers between devices, everyone(): return lax.all_to_all(rows, EVERY, 0, 0, tiled=True)  8.49 us
  transfers between devices with their start and end apart: 52, of which 23 were waited for; matrix products, arithmetic and copies ran while one was open for 2% of the time, Pallas kernels for 46%

profile of v4, /device:TPU:0, one launch (start us, length us, event | category | flops | bytes accessed | tf_op | source)
XLA Modules:
  0.0 313.6 jit_solution(12840148289717532046)
XLA Ops:
  8.4 6.2 %all-to-all-start = ((bf16[4,880,128]{2,1,0:T(8,128)(2,1)}), bf16[4,880,128]{2,1,0:T(8,128)(2,1)}, u32[]{:S(2)}, u32[]{:S(2)}) async-start(bf16[4,880,128]{2,1,0:T(8,128)(2,1)} %bitcast.31), calls=%async_computation | async-start | bytes 1802240 | tf_op jit(solution)/shard_map/all_to_all | solution.py:1023
  21.8 5.8 %spread.3 = (bf16[2,1024,3456]{2,1,0:T(8,128)(2,1)}, f32[8,128]{1,0:T(8,128)}) custom-call(s32[1,3]{1,0:T(1,128)} %refs_1_.11, s32[1,3]{1,0:T(1,128)} %collective-permute-done.refs_5_.refs_1_.refs_2_, f32[9,3,512]{2,1,0:T(4,128)} %reshape.75.refs_2_, bf16[512,256]{1,0:T(8,128)(2,1)} %get-tuple-element.168.refs_3_, ...), custom_call_target="tpu_custom_call" | custom-call | flops 1 | bytes 1 | tf_op jit(solution)/shard_map/spread/pallas_call | solution.py:57
  33.1 5.8 %spread.4 = (bf16[2,1024,3456]{2,1,0:T(8,128)(2,1)}, f32[8,128]{1,0:T(8,128)}) custom-call(s32[1,3]{1,0:T(1,128)} %refs_1_.11, s32[1,3]{1,0:T(1,128)} %collective-permute-done.refs_5_.refs_1_.refs_2_, f32[9,3,512]{2,1,0:T(4,128)} %reshape.75.refs_2_, bf16[512,256]{1,0:T(8,128)(2,1)} %get-tuple-element.168.refs_3_, ...), custom_call_target="tpu_custom_call", output_to_operand_aliasing={{0}: (5, {})} | custom-call | flops 1 | bytes 1 | tf_op jit(solution)/shard_map/spread/pallas_call | solution.py:57
  41.4 4.8 %all-to-all-start.1 = ((bf16[4,864,128]{2,1,0:T(8,128)(2,1)}), bf16[4,864,128]{2,1,0:T(8,128)(2,1)}, u32[]{:S(2)}, u32[]{:S(2)}) async-start(bf16[4,864,128]{2,1,0:T(8,128)(2,1)} %bitcast.32), calls=%async_computation.1 | async-start | bytes 1769472 | tf_op jit(solution)/shard_map/all_to_all | solution.py:1023
  48.3 5.9 %spread.5 = (bf16[2,1024,3456]{2,1,0:T(8,128)(2,1)}, f32[8,128]{1,0:T(8,128)}) custom-call(s32[1,3]{1,0:T(1,128)} %refs_1_.11, s32[1,3]{1,0:T(1,128)} %collective-permute-done.refs_5_.refs_1_.refs_2_, f32[9,3,512]{2,1,0:T(4,128)} %reshape.75.refs_2_, bf16[512,256]{1,0:T(8,128)(2,1)} %get-tuple-element.168.refs_3_, ...), custom_call_target="tpu_custom_call", output_to_operand_aliasing={{0}: (5, {})} | custom-call | flops 1 | bytes 1 | tf_op jit(solution)/shard_map/spread/pallas_call | solution.py:57
  54.1 7.3 %collective-permute-done.10.refs_1_.refs_8_.refs_12_ = bf16[2640,128]{1,0:T(8,128)(2,1)} collective-permute-done((bf16[2640,128]{1,0:T(8,128)(2,1)}, bf16[2640,128]{1,0:T(8,128)(2,1)}, u32[]{:S(2)}, u32[]{:S(2)}) %collective-permute-start.10) | collective-permute-done | bytes 675872 | tf_op jit(solution)/shard_map/ppermute | solution.py:852
  69.1 4.7 %all-to-all-start.2 = ((bf16[4,192,512]{2,1,0:T(8,128)(2,1)}), bf16[4,192,512]{2,1,0:T(8,128)(2,1)}, u32[]{:S(2)}, u32[]{:S(2)}) async-start(bf16[4,192,512]{2,1,0:T(8,128)(2,1)} %bitcast.34), calls=%async_computation.2 | async-start | bytes 1572864 | tf_op jit(solution)/shard_map/all_to_all | solution.py:1023
  76.1 11.4 %mix.2 = (f32[512,512]{1,0:T(8,128)}, f32[512,512]{1,0:T(8,128)}, f32[16,512]{1,0:T(8,128)}, f32[8,128]{1,0:T(8,128)}) custom-call(s32[4]{0:T(128)} %pad_add_fusion.refs_0_, bf16[2,1024,3456]{2,1,0:T(8,128)(2,1)} %get-tuple-element.181.refs_1_.refs_4_, bf16[1760,128]{1,0:T(8,128)(2,1)} %get-tuple-element.172.refs_2_.refs_6_.refs_15_, ...), custom_call_target="tpu_custom_call" | custom-call | flops 1 | bytes 1 | tf_op jit(solution)/shard_map/mix/pallas_call | solution.py:57
  94.7 6.2 %collective-permute-done.15.refs_1_.refs_9_.refs_22_ = bf16[1296,128]{1,0:T(8,128)(2,1)} collective-permute-done((bf16[1296,128]{1,0:T(8,128)(2,1)}, bf16[1296,128]{1,0:T(8,128)(2,1)}, u32[]{:S(2)}, u32[]{:S(2)}) %collective-permute-start.15) | collective-permute-done | bytes 331808 | tf_op jit(solution)/shard_map/ppermute | solution.py:852
  103.8 11.3 %mix.3 = (f32[512,512]{1,0:T(8,128)}, bf16[512,512]{1,0:T(8,128)(2,1)}, f32[8,128]{1,0:T(8,128)}) custom-call(s32[4]{0:T(128)} %pad_add_fusion.refs_0_, bf16[2,1024,3456]{2,1,0:T(8,128)(2,1)} %get-tuple-element.181.refs_1_.refs_4_, bf16[1760,128]{1,0:T(8,128)(2,1)} %get-tuple-element.172.refs_2_.refs_6_.refs_15_, ...), custom_call_target="tpu_custom_call" | custom-call | flops 1 | bytes 1 | tf_op jit(solution)/shard_map/mix/pallas_call | solution.py:57
  122.9 3.7 %hidden.1 = (f32[512,512]{1,0:T(8,128)}, bf16[512,256]{1,0:T(8,128)(2,1)}, bf16[512,256]{1,0:T(8,128)(2,1)}, f32[8,128]{1,0:T(8,128)}) custom-call(bf16[512,512]{1,0:T(8,128)(2,1)} %refs_2_.6, f32[512,512]{1,0:T(8,128)} %get-tuple-element.203.refs_1_, bf16[512,512]{1,0:T(8,128)(2,1)} %collective-permute-done.17.refs_2_, ...), custom_call_target="tpu_custom_call" | custom-call | flops 1 | bytes 1 | tf_op jit(solution)/shard_map/hidden/pallas_call | solution.py:57
  129.9 20.5 %ffn.1 = (f32[512,512]{1,0:T(8,128)}, f32[512,512]{1,0:T(8,128)}, f32[512,512]{1,0:T(8,128)}, f32[512,512]{1,0:T(8,128)}, bf16[16,192,512]{2,1,0:T(8,128)(2,1)}, /*index=5*/f32[8,128]{1,0:T(8,128)}) custom-call(s32[4]{0:T(128)} %pad_add_fusion.refs_0_, s32[1,3]{1,0:T(1,128)} %refs_1_.11, s32[1,3]{1,0:T(1,128)} %collective-permute-done.refs_5_.refs_1_.refs_2_, ...), custom_call_target="tpu_custom_call" | custom-call | flops 1 | bytes 1 | tf_op jit(solution)/shard_map/ffn/pallas_call | solution.py:57
  150.4 4.9 %all-to-all-start.3 = ((bf16[4,768,512]{2,1,0:T(8,128)(2,1)}), bf16[4,768,512]{2,1,0:T(8,128)(2,1)}, u32[]{:S(2)}, u32[]{:S(2)}) async-start(bf16[4,768,512]{2,1,0:T(8,128)(2,1)} %bitcast.30), calls=%async_computation.3 | async-start | bytes 6291456 | tf_op jit(solution)/shard_map/all_to_all | solution.py:1023
  155.4 3.0 collective-permute-done.24.refs_4_
  158.4 4.4 %turn.1 = (f32[512,512]{1,0:T(8,128)}, bf16[512,512]{1,0:T(8,128)(2,1)}, f32[1,512]{1,0:T(1,128)}, f32[8,128]{1,0:T(8,128)}) custom-call(s32[1,3]{1,0:T(1,128)} %refs_1_.11, f32[512,512]{1,0:T(8,128)} %get-tuple-element.208.refs_1_.refs_0_, bf16[512,512]{1,0:T(8,128)(2,1)} %refs_2_.5, f32[512,512]{1,0:T(8,128)} %get-tuple-element.215.refs_3_, ...), custom_call_target="tpu_custom_call" | custom-call | flops 1 | bytes 1 | tf_op jit(solution)/shard_map/turn/pallas_call | solution.py:57
  165.0 9.1 %mixer_grad.2 = (bf16[3456,128]{1,0:T(8,128)(2,1)}, bf16[3456,128]{1,0:T(8,128)(2,1)}, bf16[3456,128]{1,0:T(8,128)(2,1)}, bf16[1728,128]{1,0:T(8,128)(2,1)}, bf1...) custom-call(s32[4]{0:T(128)} %pad_add_fusion.refs_0_, f32[16,512]{1,0:T(8,128)} %get-tuple-element.199.refs_13_.refs_3_.refs_5_.refs_1_, ...), custom_call_target="tpu_custom_call" | custom-call | flops 1 | bytes 1 | tf_op jit(solution)/shard_map/mixer_grad/pallas_call | solution.py:57
  176.6 9.1 %mixer_grad.3 = (bf16[3456,128]{1,0:T(8,128)(2,1)}, bf16[3456,128]{1,0:T(8,128)(2,1)}, bf16[3456,128]{1,0:T(8,128)(2,1)}, bf16[1728,128]{1,0:T(8,128)(2,1)}, bf1...) custom-call(s32[4]{0:T(128)} %pad_add_fusion.refs_0_, f32[16,512]{1,0:T(8,128)} %get-tuple-element.199.refs_13_.refs_3_.refs_5_.refs_1_, ...), custom_call_target="tpu_custom_call" | custom-call | flops 1 | bytes 1 | tf_op jit(solution)/shard_map/mixer_grad/pallas_call | solution.py:57
  188.8 10.6 %spread_back.3 = (f32[512,256]{1,0:T(8,128)}, f32[512,256]{1,0:T(8,128)}, f32[8,128]{1,0:T(8,128)}) custom-call(s32[4]{0:T(128)} %pad_add_fusion.refs_0_, s32[1,3]{1,0:T(1,128)} %refs_1_.11, s32[1,3]{1,0:T(1,128)} %collective-permute-done.refs_5_.refs_1_.refs_2_, f32[9,3,512]{2,1,0:T(4,128)} %reshape.81.refs_3_, ...), custom_call_target="tpu_custom_call" | custom-call | flops 1 | bytes 1 | tf_op jit(solution)/shard_map/spread_back/pallas_call | solution.py:57
  208.3 11.0 %spread_back.4 = (f32[512,256]{1,0:T(8,128)}, f32[512,256]{1,0:T(8,128)}, f32[8,128]{1,0:T(8,128)}) custom-call(s32[4]{0:T(128)} %pad_add_fusion.refs_0_, s32[1,3]{1,0:T(1,128)} %refs_1_.11, s32[1,3]{1,0:T(1,128)} %collective-permute-done.refs_5_.refs_1_.refs_2_, f32[9,3,512]{2,1,0:T(4,128)} %reshape.81.refs_3_, ...), custom_call_target="tpu_custom_call" | custom-call | flops 1 | bytes 1 | tf_op jit(solution)/shard_map/spread_back/pallas_call | solution.py:57
  219.3 11.0 %spread_back.5 = (f32[512,256]{1,0:T(8,128)}, f32[512,256]{1,0:T(8,128)}, f32[8,128]{1,0:T(8,128)}) custom-call(s32[4]{0:T(128)} %pad_add_fusion.refs_0_, s32[1,3]{1,0:T(1,128)} %refs_1_.11, s32[1,3]{1,0:T(1,128)} %collective-permute-done.refs_5_.refs_1_.refs_2_, f32[9,3,512]{2,1,0:T(4,128)} %reshape.81.refs_3_, ...), custom_call_target="tpu_custom_call" | custom-call | flops 1 | bytes 1 | tf_op jit(solution)/shard_map/spread_back/pallas_call | solution.py:57
  230.3 3.8 %line.3 = (f32[864,128]{1,0:T(8,128)}, bf16[864,128]{1,0:T(8,128)(2,1)}, bf16[864,128]{1,0:T(8,128)(2,1)}, bf16[864,128]{1,0:T(8,128)(2,1)}, f32[8,128]{1,0:T(8,128)}) custom-call(bf16[3456,128]{1,0:T(8,128)(2,1)} %get-tuple-element.244.refs_0_, bf16[3456,128]{1,0:T(8,128)(2,1)} %collective-permute-done.30.refs_1_, ...), custom_call_target="tpu_custom_call" | custom-call | flops 1 | bytes 1 | tf_op jit(solution)/shard_map/line/pallas_call | solution.py:57
  238.6 3.9 %line.4 = (bf16[768,512]{1,0:T(8,128)(2,1)}, f32[8,128]{1,0:T(8,128)}) custom-call(bf16[3072,512]{1,0:T(8,128)(2,1)} %bitcast.16.refs_0_.refs_1_.refs_2_.refs_3_, bf16[3072,512]{1,0:T(8,128)(2,1)} %bitcast.16.refs_0_.refs_1_.refs_2_.refs_3_, bf16[3072,512]{1,0:T(8,128)(2,1)} %bitcast.16.refs_0_.refs_1_.refs_2_.refs_3_, ...), custom_call_target="tpu_custom_call" | custom-call | flops 1 | bytes 1 | tf_op jit(solution)/shard_map/line/pallas_call | solution.py:57
  245.1 3.8 %line.5 = (f32[864,128]{1,0:T(8,128)}, bf16[864,128]{1,0:T(8,128)(2,1)}, bf16[864,128]{1,0:T(8,128)(2,1)}, bf16[864,128]{1,0:T(8,128)(2,1)}, f32[8,128]{1,0:T(8,128)}) custom-call(bf16[3456,128]{1,0:T(8,128)(2,1)} %get-tuple-element.252.refs_0_, bf16[3456,128]{1,0:T(8,128)(2,1)} %collective-permute-done.35.refs_1_, ...), custom_call_target="tpu_custom_call" | custom-call | flops 1 | bytes 1 | tf_op jit(solution)/shard_map/line/pallas_call | solution.py:57
  249.0 5.0 %collective-permute-done.33.refs_3_ = bf16[864,128]{1,0:T(8,128)(2,1)} collective-permute-done((bf16[864,128]{1,0:T(8,128)(2,1)}, bf16[864,128]{1,0:T(8,128)(2,1)}, u32[]{:S(2)}, u32[]{:S(2)}) %collective-permute-start.33) | collective-permute-done | bytes 221216 | tf_op jit(solution)/shard_map/ppermute | solution.py:852
  256.1 4.5 %all-to-all-start.4 = ((bf16[4,192,512]{2,1,0:T(8,128)(2,1)}), bf16[4,192,512]{2,1,0:T(8,128)(2,1)}, u32[]{:S(2)}, u32[]{:S(2)}) async-start(bf16[4,192,512]{2,1,0:T(8,128)(2,1)} %bitcast.33), calls=%async_computation.4 | async-start | bytes 1572864 | tf_op jit(solution)/shard_map/all_to_all | solution.py:1041
  266.5 5.9 %all-to-all-done.4 = bf16[4,192,512]{2,1,0:T(8,128)(2,1)} async-done(((bf16[4,192,512]{2,1,0:T(8,128)(2,1)}), bf16[4,192,512]{2,1,0:T(8,128)(2,1)}, u32[]{:S(2)}, u32[]{:S(2)}) %all-to-all-start.4) | async-done | bytes 786464 | tf_op jit(solution)/shard_map/all_to_all | solution.py:1041
  274.4 4.1 %last.1 = (f32[512,512]{1,0:T(8,128)}, f32[1,512]{1,0:T(1,128)}, f32[8,128]{1,0:T(8,128)}) custom-call(s32[4]{0:T(128)} %pad_add_fusion.refs_0_, f32[512,512]{1,0:T(8,128)} %get-tuple-element.267.refs_1_, bf16[512,512]{1,0:T(8,128)(2,1)} %refs_2_.6, f32[512,256]{1,0:T(8,128)} %get-tuple-element.268.refs_3_, f32[512,256]{1,0:T(8,128)} %collective-permute-done.38.refs_4_, ...), custom_call_target="tpu_custom_call" | custom-call | flops 1 | bytes 1 | tf_op jit(solution)/shard_map/last/pallas_call | solution.py:57
  280.0 5.3 %all-to-all-start.5 = ((f32[32,1,128]{2,1,0:T(1,128)}), f32[32,1,128]{2,1,0:T(1,128)}, u32[]{:S(2)}, u32[]{:S(2)}) async-start(f32[32,1,128]{2,1,0:T(1,128)} %copy.56), calls=%async_computation.5 | async-start | bytes 32768 | tf_op jit(solution)/shard_map/all_to_all | solution.py:1055
  285.5 3.7 %output.1 = (bf16[512,512]{1,0:T(8,128)(2,1)}, f32[8,128]{1,0:T(8,128)}) custom-call(f32[512,512]{1,0:T(8,128)} %get-tuple-element.208.refs_1_.refs_0_, f32[512,512]{1,0:T(8,128)} %get-tuple-element.214.refs_1_, f32[512,512]{1,0:T(8,128)} %collective-permute-done.37.refs_2_, f32[8,128]{1,0:T(8,128)} %get-tuple-element.273.refs_3_), custom_call_target="tpu_custom_call" | custom-call | flops 1 | bytes 1 | tf_op jit(solution)/shard_map/output/pallas_call | solution.py:57
  295.0 3.2 %all-to-all-start.6 = ((f32[32,1,128]{2,1,0:T(1,128)}), f32[32,1,128]{2,1,0:T(1,128)}, u32[]{:S(2)}, u32[]{:S(2)}) async-start(f32[32,1,128]{2,1,0:T(1,128)} %bitcast.38), calls=%async_computation.6 | async-start | bytes 32768 | tf_op jit(solution)/shard_map/all_to_all | solution.py:1055
  298.3 6.9 %all-to-all-done.6 = f32[32,1,128]{2,1,0:T(1,128)} async-done(((f32[32,1,128]{2,1,0:T(1,128)}), f32[32,1,128]{2,1,0:T(1,128)}, u32[]{:S(2)}, u32[]{:S(2)}) %all-to-all-start.6) | async-done | bytes 16416 | tf_op jit(solution)/shard_map/all_to_all | solution.py:1055
  305.2 8.2 %adam.1 = (f32[432,512]{1,0:T(8,128)}, f32[432,512]{1,0:T(8,128)}, f32[432,512]{1,0:T(8,128)}, f32[432,512]{1,0:T(8,128)}, f32[128,512]{1,0:T(8,128)}, /*index=5...) custom-call(s32[4]{0:T(128)} %pad_add_fusion.refs_0_, ...), custom_call_target="tpu_custom_call" | custom-call | flops 1 | bytes 1 | tf_op jit(solution)/shard_map/adam/pallas_call | solution.py:57
  (131 shorter events, 97.3 us)
Async XLA Ops:
  8.4 30.5 %all-to-all-start = ((bf16[4,880,128]{2,1,0:T(8,128)(2,1)}), bf16[4,880,128]{2,1,0:T(8,128)(2,1)}, u32[]{:S(2)}, u32[]{:S(2)}) async-start(bf16[4,880,128]{2,1,0:T(8,128)(2,1)} %bitcast.31), calls=%async_computation | async-start | bytes 1802240 | tf_op jit(solution)/shard_map/all_to_all | solution.py:1023
  15.4 12.5 %collective-permute-start.5 = (bf16[1760,128]{1,0:T(8,128)(2,1)}, bf16[1760,128]{1,0:T(8,128)(2,1)}, u32[]{:S(2)}, u32[]{:S(2)}) collective-permute-start(bf16[1760,128]{1,0:T(8,128)(2,1)} %get-tuple-element.172.refs_2_.refs_6_.refs_15_), channel_id=1, source_target_pairs={{0,8},{8,0},{1,9},{9,1},{2,10},{10,2},{3,11},{11,3},{4,12},{12,4},... | collective-permute-start | bytes 1351688 | tf_op jit(solution)/shard_map/ppermute | solution.py:852
  16.9 12.2 %collective-permute-start.6 = (bf16[1760,128]{1,0:T(8,128)(2,1)}, bf16[1760,128]{1,0:T(8,128)(2,1)}, u32[]{:S(2)}, u32[]{:S(2)}) collective-permute-start(bf16[1760,128]{1,0:T(8,128)(2,1)} %get-tuple-element.172.refs_2_.refs_6_.refs_15_), channel_id=1, source_target_pairs={{0,16},{16,0},{1,17},{17,1},{2,18},{18,2},{3,19},{19,3},{4,20},{20... | collective-permute-start | bytes 1351688 | tf_op jit(solution)/shard_map/ppermute | solution.py:852
  41.4 25.3 %all-to-all-start.1 = ((bf16[4,864,128]{2,1,0:T(8,128)(2,1)}), bf16[4,864,128]{2,1,0:T(8,128)(2,1)}, u32[]{:S(2)}, u32[]{:S(2)}) async-start(bf16[4,864,128]{2,1,0:T(8,128)(2,1)} %bitcast.32), calls=%async_computation.1 | async-start | bytes 1769472 | tf_op jit(solution)/shard_map/all_to_all | solution.py:1023
  46.3 15.1 %collective-permute-start.10 = (bf16[2640,128]{1,0:T(8,128)(2,1)}, bf16[2640,128]{1,0:T(8,128)(2,1)}, u32[]{:S(2)}, u32[]{:S(2)}) collective-permute-start(bf16[2640,128]{1,0:T(8,128)(2,1)} %get-tuple-element.185.refs_6_.refs_10_), channel_id=1, source_target_pairs={{0,16},{16,0},{1,17},{17,1},{2,18},{18,2},{3,19},{19,3},{4,20},{20... | collective-permute-start | bytes 2027528 | tf_op jit(solution)/shard_map/ppermute | solution.py:852
  46.8 15.5 %collective-permute-start.9 = (bf16[2640,128]{1,0:T(8,128)(2,1)}, bf16[2640,128]{1,0:T(8,128)(2,1)}, u32[]{:S(2)}, u32[]{:S(2)}) collective-permute-start(bf16[2640,128]{1,0:T(8,128)(2,1)} %get-tuple-element.185.refs_6_.refs_10_), channel_id=1, source_target_pairs={{0,8},{8,0},{1,9},{9,1},{2,10},{10,2},{3,11},{11,3},{4,12},{12,4},... | collective-permute-start | bytes 2027528 | tf_op jit(solution)/shard_map/ppermute | solution.py:852
  69.1 32.1 %all-to-all-start.2 = ((bf16[4,192,512]{2,1,0:T(8,128)(2,1)}), bf16[4,192,512]{2,1,0:T(8,128)(2,1)}, u32[]{:S(2)}, u32[]{:S(2)}) async-start(bf16[4,192,512]{2,1,0:T(8,128)(2,1)} %bitcast.34), calls=%async_computation.2 | async-start | bytes 1572864 | tf_op jit(solution)/shard_map/all_to_all | solution.py:1023
  73.9 15.9 %collective-permute-start.13 = (bf16[2592,128]{1,0:T(8,128)(2,1)}, bf16[2592,128]{1,0:T(8,128)(2,1)}, u32[]{:S(2)}, u32[]{:S(2)}) collective-permute-start(bf16[2592,128]{1,0:T(8,128)(2,1)} %get-tuple-element.192.refs_6_.refs_19_), channel_id=1, source_target_pairs={{0,8},{8,0},{1,9},{9,1},{2,10},{10,2},{3,11},{11,3},{4,12},{12,4},... | collective-permute-start | bytes 1990664 | tf_op jit(solution)/shard_map/ppermute | solution.py:852
  75.0 15.9 %collective-permute-start.14 = (bf16[2592,128]{1,0:T(8,128)(2,1)}, bf16[2592,128]{1,0:T(8,128)(2,1)}, u32[]{:S(2)}, u32[]{:S(2)}) collective-permute-start(bf16[2592,128]{1,0:T(8,128)(2,1)} %get-tuple-element.192.refs_6_.refs_19_), channel_id=1, source_target_pairs={{0,16},{16,0},{1,17},{17,1},{2,18},{18,2},{3,19},{19,3},{4,20},{20... | collective-permute-start | bytes 1990664 | tf_op jit(solution)/shard_map/ppermute | solution.py:852
  101.2 16.6 %collective-permute-start.18 = (bf16[768,512]{1,0:T(8,128)(2,1)}, bf16[768,512]{1,0:T(8,128)(2,1)}, u32[]{:S(2)}, u32[]{:S(2)}) collective-permute-start(bf16[768,512]{1,0:T(8,128)(2,1)} %get-tuple-element.205), channel_id=1, source_target_pairs={{0,8},{8,0},{1,9},{9,1},{2,10},{10,2},{3,11},{11,3},{4,12},{12,4},... | collective-permute-start | bytes 2359304 | tf_op jit(solution)/shard_map/ppermute | solution.py:852
  102.7 16.1 %collective-permute-start.19 = (bf16[768,512]{1,0:T(8,128)(2,1)}, bf16[768,512]{1,0:T(8,128)(2,1)}, u32[]{:S(2)}, u32[]{:S(2)}) collective-permute-start(bf16[768,512]{1,0:T(8,128)(2,1)} %get-tuple-element.205), channel_id=1, source_target_pairs={{0,16},{16,0},{1,17},{17,1},{2,18},{18,2},{3,19},{19,3},{4,20},{20... | collective-permute-start | bytes 2359304 | tf_op jit(solution)/shard_map/ppermute | solution.py:852
  150.4 88.2 %all-to-all-start.3 = ((bf16[4,768,512]{2,1,0:T(8,128)(2,1)}), bf16[4,768,512]{2,1,0:T(8,128)(2,1)}, u32[]{:S(2)}, u32[]{:S(2)}) async-start(bf16[4,768,512]{2,1,0:T(8,128)(2,1)} %bitcast.30), calls=%async_computation.3 | async-start | bytes 6291456 | tf_op jit(solution)/shard_map/all_to_all | solution.py:1023
  174.1 25.4 %collective-permute-start.26 = (bf16[1728,128]{1,0:T(8,128)(2,1)}, bf16[1728,128]{1,0:T(8,128)(2,1)}, u32[]{:S(2)}, u32[]{:S(2)}) collective-permute-start(bf16[1728,128]{1,0:T(8,128)(2,1)} %get-tuple-element.226), channel_id=1, source_target_pairs={{0,8},{8,0},{1,9},{9,1},{2,10},{10,2},{3,11},{11,3},{4,12},{12,4},... | collective-permute-start | bytes 1327112 | tf_op jit(solution)/shard_map/ppermute | solution.py:852
  175.5 24.0 %collective-permute-start.27 = (bf16[1728,128]{1,0:T(8,128)(2,1)}, bf16[1728,128]{1,0:T(8,128)(2,1)}, u32[]{:S(2)}, u32[]{:S(2)}) collective-permute-start(bf16[1728,128]{1,0:T(8,128)(2,1)} %get-tuple-element.227), channel_id=1, source_target_pairs={{0,16},{16,0},{1,17},{17,1},{2,18},{18,2},{3,19},{19,3},{4,20},{20... | collective-permute-start | bytes 1327112 | tf_op jit(solution)/shard_map/ppermute | solution.py:852
  185.7 16.2 %collective-permute-start.28 = (bf16[1728,128]{1,0:T(8,128)(2,1)}, bf16[1728,128]{1,0:T(8,128)(2,1)}, u32[]{:S(2)}, u32[]{:S(2)}) collective-permute-start(bf16[1728,128]{1,0:T(8,128)(2,1)} %get-tuple-element.233), channel_id=1, source_target_pairs={{0,8},{8,0},{1,9},{9,1},{2,10},{10,2},{3,11},{11,3},{4,12},{12,4},... | collective-permute-start | bytes 1327112 | tf_op jit(solution)/shard_map/ppermute | solution.py:852
  186.5 15.4 %collective-permute-start.29 = (bf16[1728,128]{1,0:T(8,128)(2,1)}, bf16[1728,128]{1,0:T(8,128)(2,1)}, u32[]{:S(2)}, u32[]{:S(2)}) collective-permute-start(bf16[1728,128]{1,0:T(8,128)(2,1)} %get-tuple-element.234), channel_id=1, source_target_pairs={{0,16},{16,0},{1,17},{17,1},{2,18},{18,2},{3,19},{19,3},{4,20},{20... | collective-permute-start | bytes 1327112 | tf_op jit(solution)/shard_map/ppermute | solution.py:852
  204.3 26.1 %collective-permute-start.30 = (bf16[3456,128]{1,0:T(8,128)(2,1)}, bf16[3456,128]{1,0:T(8,128)(2,1)}, u32[]{:S(2)}, u32[]{:S(2)}) collective-permute-start(bf16[3456,128]{1,0:T(8,128)(2,1)} %get-tuple-element.245), channel_id=1, source_target_pairs={{0,8},{8,0},{1,9},{9,1},{2,10},{10,2},{3,11},{11,3},{4,12},{12,4},... | collective-permute-start | bytes 2654216 | tf_op jit(solution)/shard_map/ppermute | solution.py:852
  205.6 24.7 %collective-permute-start.31 = (bf16[3456,128]{1,0:T(8,128)(2,1)}, bf16[3456,128]{1,0:T(8,128)(2,1)}, u32[]{:S(2)}, u32[]{:S(2)}) collective-permute-start(bf16[3456,128]{1,0:T(8,128)(2,1)} %get-tuple-element.246), channel_id=1, source_target_pairs={{0,16},{16,0},{1,17},{17,1},{2,18},{18,2},{3,19},{19,3},{4,20},{20... | collective-permute-start | bytes 2654216 | tf_op jit(solution)/shard_map/ppermute | solution.py:852
  206.7 37.4 %collective-permute-start.35 = (bf16[3456,128]{1,0:T(8,128)(2,1)}, bf16[3456,128]{1,0:T(8,128)(2,1)}, u32[]{:S(2)}, u32[]{:S(2)}) collective-permute-start(bf16[3456,128]{1,0:T(8,128)(2,1)} %get-tuple-element.253), channel_id=1, source_target_pairs={{0,8},{8,0},{1,9},{9,1},{2,10},{10,2},{3,11},{11,3},{4,12},{12,4},... | collective-permute-start | bytes 2654216 | tf_op jit(solution)/shard_map/ppermute | solution.py:852
  207.5 37.7 %collective-permute-start.36 = (bf16[3456,128]{1,0:T(8,128)(2,1)}, bf16[3456,128]{1,0:T(8,128)(2,1)}, u32[]{:S(2)}, u32[]{:S(2)}) collective-permute-start(bf16[3456,128]{1,0:T(8,128)(2,1)} %get-tuple-element.254), channel_id=1, source_target_pairs={{0,16},{16,0},{1,17},{17,1},{2,18},{18,2},{3,19},{19,3},{4,20},{20... | collective-permute-start | bytes 2654216 | tf_op jit(solution)/shard_map/ppermute | solution.py:852
  234.2 14.8 %collective-permute-start.32 = (bf16[864,128]{1,0:T(8,128)(2,1)}, bf16[864,128]{1,0:T(8,128)(2,1)}, u32[]{:S(2)}, u32[]{:S(2)}) collective-permute-start(bf16[864,128]{1,0:T(8,128)(2,1)} %get-tuple-element.249), channel_id=1, source_target_pairs={{0,2},{2,0},{4,6},{6,4},{1,3},{3,1},{5,7},{7,5},{8,10},{10,8},{12,... | collective-permute-start | bytes 663560 | tf_op jit(solution)/shard_map/ppermute | solution.py:852
  235.9 18.1 %collective-permute-start.33 = (bf16[864,128]{1,0:T(8,128)(2,1)}, bf16[864,128]{1,0:T(8,128)(2,1)}, u32[]{:S(2)}, u32[]{:S(2)}) collective-permute-start(bf16[864,128]{1,0:T(8,128)(2,1)} %get-tuple-element.250), channel_id=1, source_target_pairs={{0,4},{2,6},{4,0},{6,2},{1,5},{3,7},{5,1},{7,3},{8,12},{10,14},{12... | collective-permute-start | bytes 663560 | tf_op jit(solution)/shard_map/ppermute | solution.py:852
  238.2 15.7 %collective-permute-start.34 = (bf16[864,128]{1,0:T(8,128)(2,1)}, bf16[864,128]{1,0:T(8,128)(2,1)}, u32[]{:S(2)}, u32[]{:S(2)}) collective-permute-start(bf16[864,128]{1,0:T(8,128)(2,1)} %get-tuple-element.251), channel_id=1, source_target_pairs={{0,6},{2,4},{4,2},{6,0},{1,7},{3,5},{5,3},{7,1},{8,14},{10,12},{12... | collective-permute-start | bytes 663560 | tf_op jit(solution)/shard_map/ppermute | solution.py:852
  256.1 29.4 %collective-permute-start.37 = (f32[512,512]{1,0:T(8,128)}, f32[512,512]{1,0:T(8,128)}, u32[]{:S(2)}, u32[]{:S(2)}) collective-permute-start(f32[512,512]{1,0:T(8,128)} %get-tuple-element.266), channel_id=1, source_target_pairs={{0,1},{1,0},{2,3},{3,2},{4,5},{5,4},{6,7},{7,6},{8,9},{9,8},{10,11... | collective-permute-start | bytes 3145736 | tf_op jit(solution)/shard_map/ppermute | solution.py:852
  256.1 16.3 %all-to-all-start.4 = ((bf16[4,192,512]{2,1,0:T(8,128)(2,1)}), bf16[4,192,512]{2,1,0:T(8,128)(2,1)}, u32[]{:S(2)}, u32[]{:S(2)}) async-start(bf16[4,192,512]{2,1,0:T(8,128)(2,1)} %bitcast.33), calls=%async_computation.4 | async-start | bytes 1572864 | tf_op jit(solution)/shard_map/all_to_all | solution.py:1041
  260.6 13.8 %collective-permute-start.38 = (f32[512,256]{1,0:T(8,128)}, f32[512,256]{1,0:T(8,128)}, u32[]{:S(2)}, u32[]{:S(2)}) collective-permute-start(f32[512,256]{1,0:T(8,128)} %get-tuple-element.269), channel_id=1, source_target_pairs={{0,1},{1,0},{2,3},{3,2},{4,5},{5,4},{6,7},{7,6},{8,9},{9,8},{10,11... | collective-permute-start | bytes 1572872 | tf_op jit(solution)/shard_map/ppermute | solution.py:852
  261.1 28.0 %collective-permute-start.39 = (bf16[864,128]{1,0:T(8,128)(2,1)}, bf16[864,128]{1,0:T(8,128)(2,1)}, u32[]{:S(2)}, u32[]{:S(2)}) collective-permute-start(bf16[864,128]{1,0:T(8,128)(2,1)} %get-tuple-element.277), channel_id=1, source_target_pairs={{0,2},{2,0},{4,6},{6,4},{1,3},{3,1},{5,7},{7,5},{8,10},{10,8},{12,... | collective-permute-start | bytes 663560 | tf_op jit(solution)/shard_map/ppermute | solution.py:852
  264.1 25.1 %collective-permute-start.40 = (bf16[864,128]{1,0:T(8,128)(2,1)}, bf16[864,128]{1,0:T(8,128)(2,1)}, u32[]{:S(2)}, u32[]{:S(2)}) collective-permute-start(bf16[864,128]{1,0:T(8,128)(2,1)} %get-tuple-element.278), channel_id=1, source_target_pairs={{0,4},{2,6},{4,0},{6,2},{1,5},{3,7},{5,1},{7,3},{8,12},{10,14},{12... | collective-permute-start | bytes 663560 | tf_op jit(solution)/shard_map/ppermute | solution.py:852
  265.0 24.2 %collective-permute-start.41 = (bf16[864,128]{1,0:T(8,128)(2,1)}, bf16[864,128]{1,0:T(8,128)(2,1)}, u32[]{:S(2)}, u32[]{:S(2)}) collective-permute-start(bf16[864,128]{1,0:T(8,128)(2,1)} %get-tuple-element.279), channel_id=1, source_target_pairs={{0,6},{2,4},{4,2},{6,0},{1,7},{3,5},{5,3},{7,1},{8,14},{10,12},{12... | collective-permute-start | bytes 663560 | tf_op jit(solution)/shard_map/ppermute | solution.py:852
  280.0 12.2 %all-to-all-start.5 = ((f32[32,1,128]{2,1,0:T(1,128)}), f32[32,1,128]{2,1,0:T(1,128)}, u32[]{:S(2)}, u32[]{:S(2)}) async-start(f32[32,1,128]{2,1,0:T(1,128)} %copy.56), calls=%async_computation.5 | async-start | bytes 32768 | tf_op jit(solution)/shard_map/all_to_all | solution.py:1055
  285.3 13.0 %collective-permute-start.42 = (f32[432,128]{1,0:T(8,128)}, f32[432,128]{1,0:T(8,128)}, u32[]{:S(2)}, u32[]{:S(2)}) collective-permute-start(f32[432,128]{1,0:T(8,128)} %get-tuple-element.288), channel_id=1, source_target_pairs={{0,1},{1,0},{2,3},{3,2},{4,5},{5,4},{6,7},{7,6},{8,9},{9,8},{10,11... | collective-permute-start | bytes 663560 | tf_op jit(solution)/shard_map/ppermute | solution.py:852
  294.5 10.7 %collective-permute-start.43 = (f32[432,128]{1,0:T(8,128)}, f32[432,128]{1,0:T(8,128)}, u32[]{:S(2)}, u32[]{:S(2)}) collective-permute-start(f32[432,128]{1,0:T(8,128)} %get-tuple-element.289), channel_id=1, source_target_pairs={{0,1},{1,0},{2,3},{3,2},{4,5},{5,4},{6,7},{7,6},{8,9},{9,8},{10,11... | collective-permute-start | bytes 663560 | tf_op jit(solution)/shard_map/ppermute | solution.py:852
  (22 other events, 115.9 us)
